TPU v7x, 128 devices: a whole 4x4x4 slice. The times are simulated.
128 devices in a mesh: slab: 16 (over y_hi, z, core), split: 8 (over y_lo, x).
Axes of the slice: x: 4, y: 4 (y_hi: 2, y_lo: 2; y = y_hi * 2 + y_lo), z: 4, core: 2. Of those that a mesh axis runs over, the one named last changes fastest.
Arguments:
- displacement: float32 [3, 128, 256, 256], P(None, 'slab', 'split'), may hold values from -0.3 to 0.3
- velocity: float32 [3, 128, 256, 256], P(None, 'slab', 'split'), may hold values from -0.6 to 0.6
- acceleration: float32 [3, 128, 256, 256], P(None, 'slab', 'split'), may hold values from -1.8 to 1.8
- bond_masks: int32 [4, 128, 256, 256], P(None, 'slab', 'split'), may hold values from 0 to 255, as said below
- proj_pos: float32 [128, 3, 128], replicated, may hold values from -0.5 to 257, as said below
- proj_vel: float32 [128, 3, 128], replicated, may hold values from -1.8 to 1.8
- proj_acc: float32 [128, 3, 128], replicated, may hold values from -1.8 to 1.8
- contact_pairs: int32 [3, 2, 2048], P(None, None, ('slab', 'split')), may hold values from -1 to 127, as said below
Outputs:
- final_displacement: float32 [3, 128, 256, 256], P(None, 'slab', 'split')
- final_velocity: float32 [3, 128, 256, 256], P(None, 'slab', 'split')
- final_proj_pos: float32 [128, 3, 128], replicated
- final_proj_vel: float32 [128, 3, 128], replicated
Inputs may be any that keep to these rules, and one draw needn't show every extreme that they name: `bond_masks`: bit b of word w (the value divided by 2 to the b, modulo 2) is 1 where the bond from the cell to the offset numbered 8 w + b is intact. `contact_pairs`: slots d * 16 to (d + 1) * 16 - 1 belong to device d. Row 0 names one of that device's 8 surface blocks; row 1 names a projectile block, or -1 for an empty slot. Live slots come first on every device and no pair repeats on a device within a substep. In every substep each projectile block is paired on exactly one device, one of the four devices of the 2 x 2 group of device blocks under it, and on another device than in the substep before; in every substep some device has all 16 slots live. `proj_pos`: the device blocks fall into 2 x 2 groups (slab indices 2a and 2a + 1, split indices 2b and 2b + 1). Every projectile block lies above one such group, between 0.5 and 2 cells over the top layer, and every group lies under exactly 4 projectile blocks.
All inputs are finite; a program needn't handle non-finite values.
Results may differ from a plain program's by a relative error of at most 0.0003.
Values sent between devices are 32-bit elements; how exact they have to be, the bound alone decides.
No kernel may reach another device: no remote copies, remote signals or barrier semaphores. Data moves between devices by JAX's collectives and lax.ppermute only.
A program may use at most 128 MiB of HBM per device.

v0:
```python
import math

import jax
import jax.numpy as jnp
from jax import lax
from jax.sharding import PartitionSpec as P

SUB = 3
SL = 4
PTS = 128
SB_DEV = 8


time_step = 0.25
bond_stiffness = 0.5
contact_stiffness = 0.05
contact_width = 8.0
inverse_mass = 0.5


def with_halo(cells, sides, width):
    for axis, dim in sides:
        count = lax.axis_size(axis)
        ends = count - 1
        head = lax.slice_in_dim(cells, 0, width, axis=dim)
        tail = lax.slice_in_dim(cells, cells.shape[dim] - width, cells.shape[dim], axis=dim)
        cells = jnp.concatenate(
            [
                lax.ppermute(tail, axis, [(i, (i + 1) % count) for i in range(ends)]),
                cells,
                lax.ppermute(head, axis, [((i + 1) % count, i) for i in range(ends)]),
            ],
            axis=dim,
        )
    return cells


def bond_offsets():
    listed = []
    for shift_x in (-2, -1, 0, 1, 2):
        for shift_y in (-2, -1, 0, 1, 2):
            for shift_z in (-2, -1, 0, 1, 2):
                squared = shift_x * shift_x + shift_y * shift_y + shift_z * shift_z
                if 0 < squared <= 4:
                    listed.append((shift_x, shift_y, shift_z))
    return listed


def bond_term(neighbour, displace, intact, valid_bond, offset):
    shift_x, shift_y, shift_z = offset
    length = math.sqrt(shift_x * shift_x + shift_y * shift_y + shift_z * shift_z)
    along_x = shift_x + (neighbour[0] - displace[0])
    along_y = shift_y + (neighbour[1] - displace[1])
    along_z = shift_z + (neighbour[2] - displace[2])
    squared = along_x * along_x + along_y * along_y + along_z * along_z
    stretch = (squared - length * length) / (length * (jnp.sqrt(squared) + length))
    return bond_stiffness / length * stretch * intact * valid_bond


def add_bond(bond_total, coefficient, offset):
    direction = jnp.array(offset, bond_total.dtype)
    return bond_total + direction[:, None, None, None] * coefficient[None]


def shift_depth(values_in, shift_size):
    if shift_size == 0:
        return values_in
    filler = jnp.zeros(values_in.shape[:-1] + (abs(shift_size),), values_in.dtype)
    if shift_size > 0:
        return jnp.concatenate([values_in[..., shift_size:], filler], axis=-1)
    return jnp.concatenate([filler, values_in[..., :shift_size]], axis=-1)


def bond_forces(padded, displace, mask_words, inside_x, inside_y):
    cells_x, cells_y, cells_z = (displace.shape[1], displace.shape[2], displace.shape[3])
    depth_index = jnp.arange(cells_z)
    bond_total = jnp.zeros_like(displace)
    for number, offset in enumerate(bond_offsets()):
        shift_x, shift_y, shift_z = offset
        window = padded[
            :, 2 + shift_x : 2 + shift_x + cells_x, 2 + shift_y : 2 + shift_y + cells_y, :
        ]
        neighbour = shift_depth(window, shift_z)
        moved_depth = depth_index + shift_z
        inside_z = ((moved_depth >= 0) & (moved_depth < cells_z)).astype(jnp.float32)
        valid_bond = (
            inside_x[2 + shift_x : 2 + shift_x + cells_x][:, None, None]
            * inside_y[2 + shift_y : 2 + shift_y + cells_y][None, :, None]
            * inside_z[None, None, :]
        )
        intact = (mask_words[number // 8] // 2 ** (number % 8) % 2).astype(jnp.float32)
        bond_total = add_bond(
            bond_total, bond_term(neighbour, displace, intact, valid_bond, offset), offset
        )
    return bond_total


def contact_tile(points, particles):
    separation = points[:, :, None] - particles[:, None, :]
    squared = jnp.sum(separation * separation, axis=0)
    weight = contact_stiffness * jnp.exp(-squared / contact_width)
    pulled = weight[None] * separation
    return (jnp.sum(pulled, axis=2), -jnp.sum(pulled, axis=1))


def slot_tiles(slot_points, chosen, positions):
    picked = positions[jnp.maximum(chosen, 0)]
    on_points, on_particles = jax.vmap(contact_tile)(slot_points, picked)
    live = (chosen >= 0).astype(jnp.float32)[:, None, None]
    return (on_points * live, on_particles * live)


def per_device(
    displacement, velocity, acceleration, bond_masks, proj_pos, proj_vel, proj_acc, contact_pairs
):
    cells_x, cells_y, cells_z = (
        displacement.shape[1],
        displacement.shape[2],
        displacement.shape[3],
    )
    slab_count = lax.axis_size("slab")
    split_count = lax.axis_size("split")
    corner_x = lax.axis_index("slab") * cells_x
    corner_y = lax.axis_index("split") * cells_y
    span_x = jnp.arange(-2, cells_x + 2) + corner_x
    span_y = jnp.arange(-2, cells_y + 2) + corner_y
    inside_x = ((span_x >= 0) & (span_x < slab_count * cells_x)).astype(jnp.float32)
    inside_y = ((span_y >= 0) & (span_y < split_count * cells_y)).astype(jnp.float32)
    place_x = (corner_x + jnp.arange(cells_x)).astype(jnp.float32)
    place_y = (corner_y + jnp.arange(cells_y)).astype(jnp.float32)
    place_z = (cells_z - SL + jnp.arange(SL)).astype(jnp.float32)
    lattice = jnp.stack(
        [
            jnp.broadcast_to(place_x[:, None, None], (cells_x, cells_y, SL)),
            jnp.broadcast_to(place_y[None, :, None], (cells_x, cells_y, SL)),
            jnp.broadcast_to(place_z[None, None, :], (cells_x, cells_y, SL)),
        ]
    )
    blocks_total = proj_pos.shape[0]
    particle_slots = jnp.arange(blocks_total)
    block_slots = jnp.arange(SB_DEV)
    for substep in range(SUB):
        half_velocity = velocity + 0.5 * time_step * acceleration
        displacement = displacement + time_step * half_velocity
        proj_half = proj_vel + 0.5 * time_step * proj_acc
        proj_pos = proj_pos + time_step * proj_half
        padded = with_halo(displacement, (("slab", 1), ("split", 2)), 2)
        forces = bond_forces(padded, displacement, bond_masks, inside_x, inside_y)
        top_layers = displacement[:, :, :, cells_z - SL :]
        places = (top_layers + lattice).reshape(3, SB_DEV, PTS)
        slot_pairs = contact_pairs[substep]
        targets = slot_pairs[0]
        chosen = slot_pairs[1]
        slot_points = jnp.moveaxis(jnp.take(places, targets, axis=1), 1, 0)
        on_points, on_particles = slot_tiles(slot_points, chosen, proj_pos)
        target_hits = (targets[:, None] == block_slots[None, :]).astype(jnp.float32)
        surface = jnp.einsum("ks,kcp->csp", target_hits, on_points, precision=lax.Precision.HIGHEST)
        forces = forces + jnp.pad(
            surface.reshape(3, cells_x, cells_y, SL), ((0, 0), (0, 0), (0, 0), (cells_z - SL, 0))
        )
        particle_hits = (chosen[:, None] == particle_slots[None, :]).astype(jnp.float32)
        particle_local = jnp.einsum(
            "kb,kcp->bcp", particle_hits, on_particles, precision=lax.Precision.HIGHEST
        )
        acceleration = forces
        velocity = half_velocity + 0.5 * time_step * acceleration
        particle_force = lax.psum(particle_local, ("slab", "split"))
        proj_acc = inverse_mass * particle_force
        proj_vel = proj_half + 0.5 * time_step * proj_acc
    return (displacement, velocity, proj_pos, proj_vel)


def solution(mesh):
    placed = (
        P(None, "slab", "split", None),
        P(None, "slab", "split", None),
        P(None, "slab", "split", None),
        P(None, "slab", "split", None),
        P(),
        P(),
        P(),
        P(None, None, ("slab", "split")),
    )
    return jax.shard_map(
        per_device,
        mesh=mesh,
        in_specs=placed,
        out_specs=(P(None, "slab", "split", None), P(None, "slab", "split", None), P(), P()),
        check_vma=False,
    )
```

profile of v0, /device:TPU:0, one launch (start us, length us, event | category | flops | bytes accessed | tf_op | source)
XLA Modules:
  0.0 584.7 jit_solution(5576427639228934593)
XLA Ops:
  7.3 1.9 multiply_add_fusion.3
  11.2 3.0 collective-permute-start
  19.6 2.0 fusion
  29.7 141.1 %all-reduce.67.cloned.1.call-done = f32[128,3,128]{2,0,1:T(8,128)} async-done(((f32[128,3,128]{2,0,1:T(8,128)}), f32[128,3,128]{2,0,1:T(8,128)}) %all-reduce.67.cloned.1.call-update) | async-done | bytes 196624 | tf_op jit(solution)/shard_map/psum | solution.py:167
  170.9 1.7 multiply_add_fusion.7
  175.2 4.7 collective-permute-start.2
  180.0 2.5 fusion.16
  183.9 2.9 fusion.1166
  186.8 1.9 fusion.102
  193.8 1.8 fusion.111
  207.4 3.3 multiply_add_fusion.2
  215.9 2.1 fusion.2
  222.2 3.0 collective-permute-start.4
  225.2 136.4 %all-reduce.69.cloned.1.call-done = f32[128,3,128]{2,0,1:T(8,128)} async-done(((f32[128,3,128]{2,0,1:T(8,128)}), f32[128,3,128]{2,0,1:T(8,128)}) %all-reduce.69.cloned.1.call-update) | async-done | bytes 196624 | tf_op jit(solution)/shard_map/psum | solution.py:167
  364.8 2.8 collective-permute-start.6
  389.4 3.3 multiply_add_fusion.1
  399.5 1.8 fusion.8
  401.5 2.0 fusion.4
  407.7 3.0 collective-permute-start.8
  410.7 137.7 %all-reduce.71.cloned.1.call-done = f32[128,3,128]{2,0,1:T(8,128)} async-done(((f32[128,3,128]{2,0,1:T(8,128)}), f32[128,3,128]{2,0,1:T(8,128)}) %all-reduce.71.cloned.1.call-update) | async-done | bytes 196624 | tf_op jit(solution)/shard_map/psum | solution.py:167
  548.4 1.8 multiply_add_fusion.5
  550.3 2.8 collective-permute-start.10
  553.1 1.7 collective-permute-start.11
  574.6 3.3 multiply_add_fusion
  (505 shorter events, 99.1 us)
Async XLA Ops:
  7.2 163.7 %all-reduce.67.cloned.1.call-start = ((), (), s32[]{:S(2)}) async-start(), calls=%async_computation | async-start | bytes 393216 | tf_op jit(solution)/shard_map/psum | solution.py:167
  9.9 163.9 %collective-permute-start.1 = (f32[3,2,32,256]{3,2,1,0:T(8,128)}, f32[3,2,32,256]{3,2,1,0:T(8,128)S(1)}, u32[]{:S(2)}, u32[]{:S(2)}) collective-permute-start(f32[3,2,32,256]{3,2,1,0:T(8,128)} %get-tuple-element.218), channel_id=1, source_target_pairs={{8,0},{16,8},{24,16},{32,24},{40,32},{48,40},{56,48},{64,56},{72,6... | collective-permute-start | bytes 589832 | tf_op jit(solution)/shard_map/ppermute | solution.py:31
  11.2 162.6 %collective-permute-start = (f32[3,2,32,256]{3,2,1,0:T(8,128)}, f32[3,2,32,256]{3,2,1,0:T(8,128)S(1)}, u32[]{:S(2)}, u32[]{:S(2)}) collective-permute-start(f32[3,2,32,256]{3,2,1,0:T(8,128)} %get-tuple-element.217), channel_id=1, source_target_pairs={{0,8},{8,16},{16,24},{24,32},{32,40},{40,48},{48,56},{56,64},{64,7... | collective-permute-start | bytes 589832 | tf_op jit(solution)/shard_map/ppermute | solution.py:29
  15.6 155.3 %copy-start.12 = (f32[128,3,128]{2,0,1:T(8,128)}, f32[128,3,128]{2,0,1:T(8,128)S(1)}, u32[]{:S(2)}) copy-start(f32[128,3,128]{2,0,1:T(8,128)S(1)} %multiply_add_fusion.8) | copy-start | bytes 589828
  22.7 338.9 %all-reduce.69.cloned.1.call-start = ((), (), s32[]{:S(2)}) async-start(), calls=%async_computation.1 | async-start | bytes 393216 | tf_op jit(solution)/shard_map/psum | solution.py:167
  29.7 157.1 %copy-start.48 = (f32[8,32]{1,0:T(8,128)}, f32[8,32]{1,0:T(8,128)S(1)}, u32[]{:S(2)}) copy-start(f32[8,32]{1,0:T(8,128)S(1)} %get-tuple-element.240) | copy-start | bytes 3076
  29.7 157.1 %copy-start.65 = (f32[8,32]{1,0:T(8,128)}, f32[8,32]{1,0:T(8,128)S(1)}, u32[]{:S(2)}) copy-start(f32[8,32]{1,0:T(8,128)S(1)} %get-tuple-element.247) | copy-start | bytes 3076
  29.7 161.6 %copy-start.55 = (f32[8,32]{1,0:T(8,128)}, f32[8,32]{1,0:T(8,128)S(1)}, u32[]{:S(2)}) copy-start(f32[8,32]{1,0:T(8,128)S(1)} %get-tuple-element.242) | copy-start | bytes 3076
  29.7 162.6 %copy-start.31 = (f32[8,32]{1,0:T(8,128)}, f32[8,32]{1,0:T(8,128)S(1)}, u32[]{:S(2)}) copy-start(f32[8,32]{1,0:T(8,128)S(1)} %get-tuple-element.236) | copy-start | bytes 3076
  29.7 162.6 %copy-start.35 = (f32[8,32]{1,0:T(8,128)}, f32[8,32]{1,0:T(8,128)S(1)}, u32[]{:S(2)}) copy-start(f32[8,32]{1,0:T(8,128)S(1)} %get-tuple-element.244) | copy-start | bytes 3076
  173.9 9.7 %collective-permute-start.3 = (f32[3,12,2,256]{3,2,1,0:T(2,128)S(1)}, f32[3,12,2,256]{3,2,1,0:T(2,128)S(1)}, u32[]{:S(2)}, u32[]{:S(2)}) collective-permute-start(f32[3,12,2,256]{3,2,1,0:T(2,128)S(1)} %get-tuple-element.190), channel_id=1, source_target_pairs={{1,0},{2,1},{3,2},{4,3},{5,4},{6,5},{7,6},{9,8},{10,9},{11,10},{12... | collective-permute-start | bytes 221192 | tf_op jit(solution)/shard_map/ppermute | solution.py:31
  175.2 8.4 %collective-permute-start.2 = (f32[3,12,2,256]{3,2,1,0:T(2,128)S(1)}, f32[3,12,2,256]{3,2,1,0:T(2,128)S(1)}, u32[]{:S(2)}, u32[]{:S(2)}) collective-permute-start(f32[3,12,2,256]{3,2,1,0:T(2,128)S(1)} %get-tuple-element.191), channel_id=1, source_target_pairs={{0,1},{1,2},{2,3},{3,4},{4,5},{5,6},{6,7},{8,9},{9,10},{10,11},{11... | collective-permute-start | bytes 221192 | tf_op jit(solution)/shard_map/ppermute | solution.py:29
  215.9 145.8 %copy-start.13 = (f32[128,3,128]{2,0,1:T(8,128)S(1)}, f32[128,3,128]{2,0,1:T(8,128)}, u32[]{:S(2)}) copy-start(f32[128,3,128]{2,0,1:T(8,128)} %copy-done.12) | copy-start | bytes 589828
  215.9 145.8 %copy-start.20 = (f32[128,3,128]{2,0,1:T(8,128)S(1)}, f32[128,3,128]{2,0,1:T(8,128)}, u32[]{:S(2)}) copy-start(f32[128,3,128]{2,0,1:T(8,128)} %get-tuple-element.30) | copy-start | bytes 589828
  219.1 329.3 %all-reduce.71.cloned.1.call-start = ((), (), s32[]{:S(2)}) async-start(), calls=%async_computation.2 | async-start | bytes 393216 | tf_op jit(solution)/shard_map/psum | solution.py:167
  220.9 143.9 %collective-permute-start.5 = (f32[3,2,32,256]{3,2,1,0:T(8,128)}, f32[3,2,32,256]{3,2,1,0:T(8,128)S(1)}, u32[]{:S(2)}, u32[]{:S(2)}) collective-permute-start(f32[3,2,32,256]{3,2,1,0:T(8,128)} %get-tuple-element.211), channel_id=1, source_target_pairs={{8,0},{16,8},{24,16},{32,24},{40,32},{48,40},{56,48},{64,56},{72,6... | collective-permute-start | bytes 589832 | tf_op jit(solution)/shard_map/ppermute | solution.py:31
  222.2 142.6 %collective-permute-start.4 = (f32[3,2,32,256]{3,2,1,0:T(8,128)}, f32[3,2,32,256]{3,2,1,0:T(8,128)S(1)}, u32[]{:S(2)}, u32[]{:S(2)}) collective-permute-start(f32[3,2,32,256]{3,2,1,0:T(8,128)} %get-tuple-element.210), channel_id=1, source_target_pairs={{0,8},{8,16},{16,24},{24,32},{32,40},{40,48},{48,56},{56,64},{64,7... | collective-permute-start | bytes 589832 | tf_op jit(solution)/shard_map/ppermute | solution.py:29
  364.8 11.6 %collective-permute-start.6 = (f32[3,12,2,256]{3,2,1,0:T(2,128)S(1)}, f32[3,12,2,256]{3,2,1,0:T(2,128)S(1)}, u32[]{:S(2)}, u32[]{:S(2)}) collective-permute-start(f32[3,12,2,256]{3,2,1,0:T(2,128)S(1)} %get-tuple-element.186), channel_id=1, source_target_pairs={{0,1},{1,2},{2,3},{3,4},{4,5},{5,6},{6,7},{8,9},{9,10},{10,11},{11... | collective-permute-start | bytes 221192 | tf_op jit(solution)/shard_map/ppermute | solution.py:29
  367.7 8.8 %collective-permute-start.7 = (f32[3,12,2,256]{3,2,1,0:T(2,128)S(1)}, f32[3,12,2,256]{3,2,1,0:T(2,128)S(1)}, u32[]{:S(2)}, u32[]{:S(2)}) collective-permute-start(f32[3,12,2,256]{3,2,1,0:T(2,128)S(1)} %get-tuple-element.187), channel_id=1, source_target_pairs={{1,0},{2,1},{3,2},{4,3},{5,4},{6,5},{7,6},{9,8},{10,9},{11,10},{12... | collective-permute-start | bytes 221192 | tf_op jit(solution)/shard_map/ppermute | solution.py:31
  392.7 180.2 %copy-start = (f32[3,8,32,256]{3,2,1,0:T(8,128)}, f32[3,8,32,256]{3,2,1,0:T(8,128)S(1)}, u32[]{:S(2)}) copy-start(f32[3,8,32,256]{3,2,1,0:T(8,128)S(1)} %get-tuple-element.25) | copy-start | bytes 2359300
  406.4 143.8 %collective-permute-start.9 = (f32[3,2,32,256]{3,2,1,0:T(8,128)}, f32[3,2,32,256]{3,2,1,0:T(8,128)S(1)}, u32[]{:S(2)}, u32[]{:S(2)}) collective-permute-start(f32[3,2,32,256]{3,2,1,0:T(8,128)} %get-tuple-element.204), channel_id=1, source_target_pairs={{8,0},{16,8},{24,16},{32,24},{40,32},{48,40},{56,48},{64,56},{72,6... | collective-permute-start | bytes 589832 | tf_op jit(solution)/shard_map/ppermute | solution.py:31
  407.7 142.5 %collective-permute-start.8 = (f32[3,2,32,256]{3,2,1,0:T(8,128)}, f32[3,2,32,256]{3,2,1,0:T(8,128)S(1)}, u32[]{:S(2)}, u32[]{:S(2)}) collective-permute-start(f32[3,2,32,256]{3,2,1,0:T(8,128)} %get-tuple-element.203), channel_id=1, source_target_pairs={{0,8},{8,16},{16,24},{24,32},{32,40},{40,48},{48,56},{56,64},{64,7... | collective-permute-start | bytes 589832 | tf_op jit(solution)/shard_map/ppermute | solution.py:29
  550.3 11.5 %collective-permute-start.10 = (f32[3,12,2,256]{3,2,1,0:T(2,128)S(1)}, f32[3,12,2,256]{3,2,1,0:T(2,128)S(1)}, u32[]{:S(2)}, u32[]{:S(2)}) collective-permute-start(f32[3,12,2,256]{3,2,1,0:T(2,128)S(1)} %get-tuple-element.182), channel_id=1, source_target_pairs={{0,1},{1,2},{2,3},{3,4},{4,5},{5,6},{6,7},{8,9},{9,10},{10,11},{11... | collective-permute-start | bytes 221192 | tf_op jit(solution)/shard_map/ppermute | solution.py:29
  553.1 8.7 %collective-permute-start.11 = (f32[3,12,2,256]{3,2,1,0:T(2,128)S(1)}, f32[3,12,2,256]{3,2,1,0:T(2,128)S(1)}, u32[]{:S(2)}, u32[]{:S(2)}) collective-permute-start(f32[3,12,2,256]{3,2,1,0:T(2,128)S(1)} %get-tuple-element.183), channel_id=1, source_target_pairs={{1,0},{2,1},{3,2},{4,3},{5,4},{6,5},{7,6},{9,8},{10,9},{11,10},{12... | collective-permute-start | bytes 221192 | tf_op jit(solution)/shard_map/ppermute | solution.py:31
  (166 other events, 251.3 us)
Sparse Core Ops, SparseCore 0:
  22.8 147.9 all-reduce.66
  219.2 142.3 all-reduce.68
  404.8 143.5 all-reduce.70
where the time goes:
time: 593 us; the launch traced here: 585 us
  waiting for transfers between devices  415 us (70%)
  other arithmetic  88.5 us (15%)
  local copies, waits for them, and re-layouts  32.2 us (5%)
  starting transfers between devices  27.9 us (5%)
  between operations  16.9 us (3%)
    psum x3, waiting for transfers between devices, per_device(): particle_force = lax.psum(particle_local, ('slab', 'split'))  415 us
    mul x49, other arithmetic, add_bond(): return bond_total + direction[:, None, None, None] * coefficient[None]  48 us
    ppermute x6, starting transfers between devices, with_halo(): lax.ppermute(tail, axis, [(i, (i + 1) % count) for i in range(ends)])  19.5 us
  transfers between devices with their start and end apart: 15, of which 3 were waited for; matrix products, arithmetic and copies ran while one was open for 7% of the time, Pallas kernels for 0%

commit v1 on v0

v1 whole, which is shorter than its diff:
```python
import functools
import math

import jax
import jax.numpy as jnp
from jax import lax
from jax.experimental import pallas as pl
from jax.experimental.pallas import tpu as pltpu
from jax.sharding import PartitionSpec as P

SUB = 3
SL = 4
SLOTS = 16
GROUP = 4

DT = 0.25
STIFF = 0.5
CONTACT = 0.05
WIDTH = 8.0
INV_MASS = 0.5

CX, CY, CZ = 8, 32, 256
LO = 8
F32 = jnp.float32
PARAMS = pltpu.CompilerParams(vmem_limit_bytes=48 * 1024 * 1024)


def bond_offsets():
    listed = []
    for sx in (-2, -1, 0, 1, 2):
        for sy in (-2, -1, 0, 1, 2):
            for sz in (-2, -1, 0, 1, 2):
                if 0 < sx * sx + sy * sy + sz * sz <= 4:
                    listed.append((sx, sy, sz))
    return listed


OFFSETS = bond_offsets()


def as_int32(bits):
    return bits - (1 << 32) if bits >= 1 << 31 else bits


def keep_bits(dim, allowed):
    return as_int32(sum(1 << n for n, e in enumerate(OFFSETS) if allowed(e[dim])))


def keep_word(index, last, dim):
    word = jnp.where(index == 0, keep_bits(dim, lambda e: e >= 0), -1)
    word = jnp.where(index == 1, keep_bits(dim, lambda e: e >= -1), word)
    word = jnp.where(index == last - 1, keep_bits(dim, lambda e: e <= 1), word)
    return jnp.where(index == last, keep_bits(dim, lambda e: e <= 0), word)


def position():
    return lax.axis_index("slab"), lax.axis_index("split")


def contact(substep, pairs, u_ref, half_ref, share, pos, ids, corner):
    row = lax.broadcasted_iota(jnp.int32, (CY, 128), 0)
    lane = lax.broadcasted_iota(jnp.int32, (CY, 128), 1)
    place_y = (row + corner[1]).astype(F32)
    live = jnp.int32(0)
    for k in range(SLOTS):
        live += (pairs[substep, 1, k] >= 0).astype(jnp.int32)

    def slot(k, totals):
        target = pairs[substep, 0, k]
        hit = ids == pairs[substep, 1, k]
        q = [jnp.sum(jnp.where(hit, pos[c], 0.0), axis=0, keepdims=True) for c in range(3)]
        tops = [u_ref[c, target, :, CZ - 128 :] for c in range(3)]
        place_x = (corner[0] + target).astype(F32)
        on_particles = [jnp.zeros((CY, 128), F32) for _ in range(3)]
        surface = [jnp.zeros((CY, 128), F32) for _ in range(3)]
        for z in range(SL):
            at = 128 - SL + z
            lattice = (place_x, place_y, float(CZ - SL + z))
            r = [(tops[c][:, at : at + 1] + lattice[c]) - q[c] for c in range(3)]
            squared = r[0] * r[0] + r[1] * r[1] + r[2] * r[2]
            weight = CONTACT * jnp.exp(squared * (-1.0 / WIDTH))
            for c in range(3):
                pulled = weight * r[c]
                on_particles[c] = on_particles[c] + pulled
                on_points = jnp.sum(pulled, axis=1, keepdims=True)
                surface[c] = jnp.where(lane == at, on_points, surface[c])
        for c in range(3):
            half_ref[c, target, :, CZ - 128 :] += share * surface[c]
        return tuple(
            totals[c] - jnp.where(hit, jnp.sum(on_particles[c], axis=0, keepdims=True), 0.0)
            for c in range(3)
        )

    return lax.fori_loop(0, live, slot, tuple(jnp.zeros((8, 128), F32) for _ in range(3)))


def send_edges(u_ref, force, xa, xb, ya, yb, even_x, even_y):
    at_a = jnp.where(even_x, CX - 2, 0)
    at_b = jnp.where(even_x, 0, CX - 2)
    for c in range(3):
        for layer in range(2):
            rows = slice((2 * c + layer) * CY, (2 * c + layer + 1) * CY)
            xa[rows, :] = u_ref[c, at_a + layer]
            xb[rows, :] = u_ref[c, at_b + layer]
        xa[6 * CY + 8 * c : 6 * CY + 8 * c + 8, 0:128] = force[c]
        xa[6 * CY + 8 * c : 6 * CY + 8 * c + 8, 128:256] = force[c]
    for want_even, low, high in ((True, yb, ya), (False, ya, yb)):

        @pl.when(even_y == want_even)
        def _(low=low, high=high):
            for c in range(3):
                for x in range(CX):
                    low[c, x] = u_ref[c, x, 0:2, :]
                    high[c, x] = u_ref[c, x, CY - 2 : CY, :]


def begin_kernel(pairs, u, v, a, masks, pp, pv, pa, u_out, half_out, w_out, pst, perm, xa, xb, ya, yb):
    slab, split = position()
    slabs, splits = lax.axis_size("slab"), lax.axis_size("split")
    even_x, even_y = lax.rem(slab, 2) == 0, lax.rem(split, 2) == 0

    def layer(x, carry):
        kx = keep_word(slab * CX + x, slabs * CX - 1, 0)
        ky = keep_word(split * CY + lax.broadcasted_iota(jnp.int32, (CY, CZ), 0), splits * CY - 1, 1)
        kz = keep_word(lax.broadcasted_iota(jnp.int32, (CY, CZ), 1), CZ - 1, 2)
        word = masks[0, x] | (masks[1, x] << 8) | (masks[2, x] << 16) | (masks[3, x] << 24)
        w_out[x] = word & ky & kz & kx
        for c in range(3):
            half = v[c, x] + 0.5 * DT * a[c, x]
            half_out[c, x] = half
            u_out[c, x] = u[c, x] + DT * half
        return carry

    lax.fori_loop(0, CX, layer, 0)

    blocks = pp.shape[1]
    mean_x = jnp.sum(pp[0], axis=1, keepdims=True) * (1.0 / pp.shape[2])
    mean_y = jnp.sum(pp[1], axis=1, keepdims=True) * (1.0 / pp.shape[2])
    group_x = jnp.floor((mean_x + 0.5) * (1.0 / (2 * CX)))
    group_y = jnp.floor((mean_y + 0.5) * (1.0 / (2 * CY)))
    group = jnp.broadcast_to(group_x * (splits // 2) + group_y, (blocks, blocks))
    row = lax.broadcasted_iota(jnp.int32, (blocks, blocks), 0)
    lane = lax.broadcasted_iota(jnp.int32, (blocks, blocks), 1)
    earlier = jnp.where((group == group.T) & (lane < row), 1.0, 0.0)
    rank = jnp.sum(earlier, axis=1, keepdims=True).astype(jnp.int32)
    group = group.astype(jnp.int32)
    mine = (slab // 2) * (splits // 2) + split // 2
    slot = (group ^ mine) * GROUP + rank
    perm[...] = jnp.where(slot == lane, 1.0, 0.0)

    pst[...] = jnp.zeros_like(pst)
    pst[6] = jnp.full((8, 128), -5.0, F32)
    for k in range(GROUP):
        chosen = slot == k
        pst[6, k : k + 1, :] = jnp.sum(jnp.where(chosen, row.astype(F32), 0.0), axis=0, keepdims=True)
        for c in range(3):
            pos, vel, acc = [
                jnp.sum(jnp.where(chosen, p[c], 0.0), axis=0, keepdims=True) for p in (pp, pv, pa)
            ]
            half = vel + 0.5 * DT * acc
            pst[3 + c, k : k + 1, :] = half
            pst[c, k : k + 1, :] = pos + DT * half
    ids = pst[6].astype(jnp.int32)
    force = contact(
        0, pairs, u_out, half_out, DT, [pst[c] for c in range(3)], ids, (slab * CX, split * CY)
    )
    for c in range(3):
        pst[7 + c] = force[c]
    send_edges(u_out, force, xa, xb, ya, yb, even_x, even_y)


def corner_kernel(ya_own, yb_own, xa, xb, pst, ya, yb):
    slab, split = position()
    even_x, even_y = lax.rem(slab, 2) == 0, lax.rem(split, 2) == 0
    for c in range(3):
        ya[c, 1 : CX + 1] = ya_own[c]
        yb[c, 1 : CX + 1] = yb_own[c]
        force = pst[7 + c] + xa[6 * CY + 8 * c : 6 * CY + 8 * c + 8, 0:128]
        for k in range(2):
            ya[c, CX + 2 + k, :, 0:128] = force[2 * k : 2 * k + 2]
            ya[c, CX + 2 + k, :, 128:256] = force[2 * k : 2 * k + 2]
    for is_x in (True, False):
        for is_y in (True, False):

            @pl.when((even_x == is_x) & (even_y == is_y))
            def _(is_x=is_x, is_y=is_y):
                for c in range(3):
                    for message, high in ((ya, is_y), (yb, not is_y)):
                        y = CY - 2 if high else 0
                        for got, top in ((xa, is_x), (xb, not is_x)):
                            entry, layer = (CX + 1, 0) if top else (0, 1)
                            at = (2 * c + layer) * CY + y
                            message[c, entry] = got[at : at + 2, :]


def bonds_kernel(substep, *refs):
    last = substep == SUB - 1
    pairs, u, half, w, xa, xb, ya, yb, pst = refs[:9]
    if last:
        u_out, half_out, pst_out = u, refs[9], refs[10]
        pad, left, right = refs[11:]
    else:
        u_out, half_out, pst_out, xa_out, xb_out, ya_out, yb_out = refs[9:16]
        pad, left, right = refs[16:]
    slab, split = position()
    even_x, even_y = lax.rem(slab, 2) == 0, lax.rem(split, 2) == 0
    rows = slice(LO, LO + CY)

    def fill(c, _):
        def own(x, carry):
            pad[c, x + 2, rows, :] = u[c, x]
            return carry

        lax.fori_loop(0, CX, own, 0)
        return _

    for c in range(3):
        fill(c, 0)
        to_a = jnp.where(even_x, CX + 2, 0)
        to_b = jnp.where(even_x, 0, CX + 2)
        for layer in range(2):
            part = slice((2 * c + layer) * CY, (2 * c + layer + 1) * CY)
            pad[c, to_a + layer, rows, :] = xa[part, :]
            pad[c, to_b + layer, rows, :] = xb[part, :]
    for is_y in (True, False):

        @pl.when(even_y == is_y)
        def _(is_y=is_y):
            for got, high in ((ya, is_y), (yb, not is_y)):
                at = LO + CY if high else LO - 2
                for c in range(3):
                    for entry in range(CX + 2):
                        pad[c, entry + 1, at : at + 2, :] = got[c, entry]

    def shifted(x, carry):
        for c in range(3):
            for y in range(0, CY + 16, 8):
                value = pad[c, x + 1, y : y + 8, :]
                left[c, x, y : y + 8, :] = pltpu.roll(value, CZ - 1, 1)
                right[c, x, y : y + 8, :] = pltpu.roll(value, 1, 1)
        return carry

    lax.fori_loop(0, CX + 2, shifted, 0)

    def forces(x, y, z):
        lanes = slice(z, z + 128)
        own = [pad[c, x + 2, LO + y : LO + y + 8, lanes] for c in range(3)]
        less = {(c, e): own[c] - float(e) if e else own[c] for c in range(3) for e in (-2, -1, 0, 1, 2)}
        word = w[x, y : y + 8, lanes]
        wide = [pad[c, x + 2, LO + y : LO + y + 8, :] for c in range(3)]
        total = [None] * 3
        for squared_length in (1, 2, 3, 4):
            sums = [None] * 3
            for number, e in enumerate(OFFSETS):
                if sum(k * k for k in e) != squared_length:
                    continue
                at = slice(LO + y + e[1], LO + y + e[1] + 8)
                if e[2] == 0:
                    near = [pad[c, x + 2 + e[0], at, lanes] for c in range(3)]
                elif abs(e[2]) == 2:
                    near = [pltpu.roll(wide[c], (CZ - e[2]) % CZ, 1)[:, lanes] for c in range(3)]
                else:
                    source = left if e[2] > 0 else right
                    near = [source[c, x + 1 + e[0], at, lanes] for c in range(3)]
                d = [near[c] - less[c, e[c]] for c in range(3)]
                q = jnp.maximum(d[0] * d[0] + d[1] * d[1] + d[2] * d[2], 1e-30)
                pull = q * lax.rsqrt(q) - math.sqrt(squared_length)
                pull = jnp.where((word & as_int32(1 << number)) != 0, pull, 0.0)
                for c in range(3):
                    if e[c] > 0:
                        sums[c] = pull if sums[c] is None else sums[c] + pull
                    elif e[c] < 0:
                        sums[c] = -pull if sums[c] is None else sums[c] - pull
            factor = STIFF / squared_length * (2.0 if squared_length == 4 else 1.0)
            for c in range(3):
                term = factor * sums[c]
                total[c] = term if total[c] is None else total[c] + term
        return total

    def layer(x, carry):
        for y in range(0, CY, 8):
            for z in range(0, CZ, 128):
                lanes = slice(z, z + 128)
                total = forces(x, y, z)
                for c in range(3):
                    moved = half[c, x, y : y + 8, lanes] + (0.5 * DT if last else DT) * total[c]
                    half_out[c, x, y : y + 8, lanes] = moved
                    if not last:
                        u_out[c, x, y : y + 8, lanes] = u[c, x, y : y + 8, lanes] + DT * moved
        return carry

    lax.fori_loop(0, CX, layer, 0)

    pst_out[6:] = pst[6:]
    pos = []
    for c in range(3):
        theirs = jnp.concatenate(
            [ya[c, CX + 2, :, 0:128], ya[c, CX + 3, :, 0:128], jnp.zeros((4, 128), F32)], axis=0
        )
        acc = INV_MASS * (pst[7 + c] + xa[6 * CY + 8 * c : 6 * CY + 8 * c + 8, 0:128] + theirs)
        if last:
            pst_out[c] = pst[c]
            pst_out[3 + c] = pst[3 + c] + 0.5 * DT * acc
        else:
            moved = pst[3 + c] + DT * acc
            pst_out[3 + c] = moved
            pos.append(pst[c] + DT * moved)
            pst_out[c] = pos[c]
    if last:
        return
    share = 0.5 * DT if substep == SUB - 2 else DT
    ids = pst[6].astype(jnp.int32)
    force = contact(
        substep + 1, pairs, u_out, half_out, share, pos, ids, (slab * CX, split * CY)
    )
    for c in range(3):
        pst_out[7 + c] = force[c]
    send_edges(u_out, force, xa_out, xb_out, ya_out, yb_out, even_x, even_y)


def final_kernel(perm, gathered, pos_out, vel_out):
    for c in range(3):
        for at, out in ((c, pos_out), (3 + c, vel_out)):
            out[c] = jnp.dot(
                perm[...],
                gathered[at],
                precision=lax.Precision.HIGHEST,
                preferred_element_type=F32,
            )


VMEM = pl.BlockSpec(memory_space=pltpu.VMEM)
SMEM = pl.BlockSpec(memory_space=pltpu.SMEM)
STATE = jax.ShapeDtypeStruct((3, CX, CY, CZ), F32)
WORDS = jax.ShapeDtypeStruct((CX, CY, CZ), jnp.int32)
PST = jax.ShapeDtypeStruct((10, 8, 128), F32)
XA = jax.ShapeDtypeStruct((6 * CY + 24, CZ), F32)
XB = jax.ShapeDtypeStruct((6 * CY, CZ), F32)
YE = jax.ShapeDtypeStruct((3, CX, 2, CZ), F32)
YA = jax.ShapeDtypeStruct((3, CX + 4, 2, CZ), F32)
YB = jax.ShapeDtypeStruct((3, CX + 2, 2, CZ), F32)


def call(kernel, inputs, outputs, scalars=0, scratch=()):
    return pl.pallas_call(
        kernel,
        out_shape=outputs,
        in_specs=[SMEM] * scalars + [VMEM] * (len(inputs) - scalars),
        out_specs=[VMEM] * len(outputs),
        scratch_shapes=list(scratch),
        compiler_params=PARAMS,
    )(*inputs)


def swap(value, axis, offset):
    pairs = []
    for i in range(offset, lax.axis_size(axis) - 1, 2):
        pairs += [(i, i + 1), (i + 1, i)]
    return lax.ppermute(value, axis, pairs)


def exchange(xa, xb, ya, yb, pst):
    xa, xb = swap(xa, "slab", 0), swap(xb, "slab", 1)
    ya, yb = call(corner_kernel, (ya, yb, xa, xb, pst), [YA, YB])
    return xa, xb, swap(ya, "split", 0), swap(yb, "split", 1)


def per_device(u, v, a, masks, proj_pos, proj_vel, proj_acc, pairs):
    pp, pv, pa = [jnp.transpose(p, (1, 0, 2)) for p in (proj_pos, proj_vel, proj_acc)]
    blocks = pp.shape[1]
    u, half, words, pst, perm, *edges = call(
        begin_kernel,
        (pairs, u, v, a, masks, pp, pv, pa),
        [STATE, STATE, WORDS, PST, jax.ShapeDtypeStruct((blocks, blocks), F32), XA, XB, YE, YE],
        scalars=1,
    )
    pad = pltpu.VMEM((3, CX + 4, CY + 16, CZ), F32)
    side = pltpu.VMEM((3, CX + 2, CY + 16, CZ), F32)
    for substep in range(SUB):
        halos = exchange(*edges, pst)
        last = substep == SUB - 1
        outputs = [STATE, PST] if last else [STATE, STATE, PST, XA, XB, YE, YE]
        got = call(
            functools.partial(bonds_kernel, substep),
            (pairs, u, half, words, *halos, pst),
            outputs,
            scalars=1,
            scratch=(pad, side, side),
        )
        if last:
            velocity, pst = got
        else:
            u, half, pst, *edges = got

    gathered = pst[:6, :GROUP]
    for axis, least in (("split", 2), ("slab", 2)):
        bit = least
        while bit < lax.axis_size(axis):
            theirs = lax.ppermute(
                gathered, axis, [(i, i ^ bit) for i in range(lax.axis_size(axis))]
            )
            gathered = jnp.concatenate([gathered, theirs], axis=1)
            bit *= 2
    final_pos, final_vel = call(final_kernel, (perm, gathered), [jax.ShapeDtypeStruct(pp.shape, F32)] * 2)
    return (
        u,
        velocity,
        jnp.transpose(final_pos, (1, 0, 2)),
        jnp.transpose(final_vel, (1, 0, 2)),
    )


def solution(mesh):
    cells = P(None, "slab", "split", None)
    return jax.shard_map(
        per_device,
        mesh=mesh,
        in_specs=(cells, cells, cells, cells, P(), P(), P(), P(None, None, ("slab", "split"))),
        out_specs=(cells, cells, P(), P()),
        check_vma=False,
    )
```

time: 593 us -> 137 us (0.23); the launches traced: 585 us -> 135 us
  waiting for transfers between devices: 415 us -> 20.5 us
  other arithmetic: 88.5 us -> 0.04 us
  Pallas kernels: 0 us -> 40.3 us
  starting transfers between devices: 27.9 us -> 65.3 us
  local copies, waits for them, and re-layouts: 32.2 us -> 8.06 us
  between operations: 16.9 us -> 0.82 us
    psum x3 -> x0, waiting for transfers between devices: 415 us -> none  [per_device(): particle_force = lax.psum(particle_local, ('slab', 'split'))]
    mul x53 -> x0, other arithmetic: 49.2 us -> none  [the longest x49 48 us: add_bond(): return bond_total + direction[:, None, None, None] * coefficient[None]]
    pallas_call x0 -> x8, Pallas kernels: none -> 40.3 us  [call(): pl.pallas_call(kernel, out_shape=outputs, in_specs=[SMEM] * scalars + [VM...]
    ppermute x12 -> x17, starting transfers between devices: 27.8 us -> 65.3 us  [the longest x5 37.6 us: per_device(): lax.ppermute(gathered, axis, [(i, i ^ bit) for i in range(lax.axis_size(a...]
    ppermute x12 -> x17, waiting for transfers between devices: 0.03 us -> 20.5 us  [the longest x5 12 us: per_device(): lax.ppermute(gathered, axis, [(i, i ^ bit) for i in range(lax.axis_size(a...]
    add x11 -> x0, other arithmetic: 17.7 us -> none  [the longest x3 8.56 us: per_device(): displacement = displacement + time_step * half_velocity]
    slice x13 -> x1, local copies, waits for them, and re-layouts: 13 us -> 0.01 us  [per_device(): gathered = pst[:6, :GROUP]]
    reduce_sum x6 -> x0, other arithmetic: 9.94 us -> none  [the longest x3 6.11 us: contact_tile(): return (jnp.sum(pulled, axis=2), -jnp.sum(pulled, axis=1))]
  transfers between devices with their start and end apart: 15 -> 17, of which waited for: 3 -> 11; matrix products, arithmetic and copies ran while one was open for 7% -> 0% of each run, Pallas kernels for 0% -> 0%
where the time goes in v1:
time: 137 us; the launch traced here: 135 us
  starting transfers between devices  65.3 us (48%)
  Pallas kernels  40.3 us (29%)
  waiting for transfers between devices  20.5 us (15%)
  local copies, waits for them, and re-layouts  8.06 us (6%)
    pallas_call x8, Pallas kernels, call(): pl.pallas_call(kernel, out_shape=outputs, in_specs=[SMEM] * scalars + [VM...  40.3 us
    ppermute x5, starting transfers between devices, per_device(): lax.ppermute(gathered, axis, [(i, i ^ bit) for i in range(lax.axis_size(a...  37.6 us
    ppermute x12, starting transfers between devices, swap(): return lax.ppermute(value, axis, pairs)  27.7 us
    ppermute x5, waiting for transfers between devices, per_device(): lax.ppermute(gathered, axis, [(i, i ^ bit) for i in range(lax.axis_size(a...  12 us
    ppermute x12, waiting for transfers between devices, swap(): return lax.ppermute(value, axis, pairs)  8.43 us
    unnamed x16, local copies, waits for them, and re-layouts  7.99 us
  transfers between devices with their start and end apart: 17, of which 11 were waited for; matrix products, arithmetic and copies ran while one was open for 0% of the time, Pallas kernels for 0%

profile of v1, /device:TPU:0, one launch (start us, length us, event | category | flops | bytes accessed | tf_op | source)
XLA Modules:
  0.0 135.0 jit_solution(2264835928237230114)
XLA Ops:
  1.3 1.1 copy-done.1
  7.5 4.8 %shard_map.111 = (f32[3,8,32,256]{3,2,1,0:T(8,128)S(1)}, f32[3,8,32,256]{3,2,1,0:T(8,128)S(1)}, s32[8,32,256]{2,1,0:T(8,128)S(1)}, f32[10,8,128]{2,1,0:T(8,128)S...) custom-call(s32[3,2,16]{2,1,0:T(2,128)S(1)} %copy-done.7, ...), custom_call_target="tpu_custom_call" | custom-call | tf_op jit(solution)/shard_map/pallas_call | solution.py:345
  14.8 3.5 %collective-permute-done.2.refs_6_ = f32[3,12,2,256]{3,2,1,0:T(2,128)S(1)} collective-permute-done((f32[3,12,2,256]{3,2,1,0:T(2,128)S(1)}, f32[3,12,2,256]{3,2,1,0:T(2,128)S(1)}, u32[]{:S(2)}, u32[]{:S(2)}) %collective-permute-start.2) | collective-permute-done | bytes 73760 | tf_op jit(solution)/shard_map/ppermute | solution.py:359
  18.3 10.4 %shard_map.113 = (f32[3,8,32,256]{3,2,1,0:T(8,128)S(1)}, f32[3,8,32,256]{3,2,1,0:T(8,128)S(1)}, f32[10,8,128]{2,1,0:T(8,128)S(1)}, f32[216,256]{1,0:T(8,128)S(1)...) custom-call(s32[3,2,16]{2,1,0:T(2,128)S(1)} %copy-done.7, ...), custom_call_target="tpu_custom_call" | custom-call | tf_op jit(solution)/shard_map/pallas_call | solution.py:345
  28.7 6.3 %collective-permute-start.4 = (f32[216,256]{1,0:T(8,128)S(1)}, f32[216,256]{1,0:T(8,128)S(1)}, u32[]{:S(2)}, u32[]{:S(2)}) collective-permute-start(f32[216,256]{1,0:T(8,128)S(1)} %get-tuple-element.49), channel_id=1, source_target_pairs={{0,8},{8,0},{16,24},{24,16},{32,40},{40,32},{48,56},{56,48},{64,72... | collective-permute-start | bytes 663560 | tf_op jit(solution)/shard_map/ppermute | solution.py:359
  36.2 3.6 %collective-permute-start.6 = (f32[3,12,2,256]{3,2,1,0:T(2,128)S(1)}, f32[3,12,2,256]{3,2,1,0:T(2,128)S(1)}, u32[]{:S(2)}, u32[]{:S(2)}) collective-permute-start(f32[3,12,2,256]{3,2,1,0:T(2,128)S(1)} %get-tuple-element.54), channel_id=1, source_target_pairs={{0,1},{1,0},{2,3},{3,2},{4,5},{5,4},{6,7},{7,6},{8,9},{9,8},{10,11... | collective-permute-start | bytes 221192 | tf_op jit(solution)/shard_map/ppermute | solution.py:359
  40.4 1.7 %collective-permute-done.6.refs_6_ = f32[3,12,2,256]{3,2,1,0:T(2,128)S(1)} collective-permute-done((f32[3,12,2,256]{3,2,1,0:T(2,128)S(1)}, f32[3,12,2,256]{3,2,1,0:T(2,128)S(1)}, u32[]{:S(2)}, u32[]{:S(2)}) %collective-permute-start.6) | collective-permute-done | bytes 73760 | tf_op jit(solution)/shard_map/ppermute | solution.py:359
  42.1 12.6 %shard_map.115 = (f32[3,8,32,256]{3,2,1,0:T(8,128)}, f32[3,8,32,256]{3,2,1,0:T(8,128)S(1)}, f32[10,8,128]{2,1,0:T(8,128)S(1)}, f32[216,256]{1,0:T(8,128)S(1)}, f...) custom-call(s32[3,2,16]{2,1,0:T(2,128)S(1)} %copy-done.7, ...), custom_call_target="tpu_custom_call" | custom-call | tf_op jit(solution)/shard_map/pallas_call | solution.py:345
  54.7 10.5 %collective-permute-start.8 = (f32[216,256]{1,0:T(8,128)S(1)}, f32[216,256]{1,0:T(8,128)S(1)}, u32[]{:S(2)}, u32[]{:S(2)}) collective-permute-start(f32[216,256]{1,0:T(8,128)S(1)} %get-tuple-element.58), channel_id=1, source_target_pairs={{0,8},{8,0},{16,24},{24,16},{32,40},{40,32},{48,56},{56,48},{64,72... | collective-permute-start | bytes 663560 | tf_op jit(solution)/shard_map/ppermute | solution.py:359
  66.3 3.1 %collective-permute-start.10 = (f32[3,12,2,256]{3,2,1,0:T(2,128)S(1)}, f32[3,12,2,256]{3,2,1,0:T(2,128)S(1)}, u32[]{:S(2)}, u32[]{:S(2)}) collective-permute-start(f32[3,12,2,256]{3,2,1,0:T(2,128)S(1)} %get-tuple-element.63), channel_id=1, source_target_pairs={{0,1},{1,0},{2,3},{3,2},{4,5},{5,4},{6,7},{7,6},{8,9},{9,8},{10,11... | collective-permute-start | bytes 221192 | tf_op jit(solution)/shard_map/ppermute | solution.py:359
  70.1 1.7 %collective-permute-done.10.refs_6_ = f32[3,12,2,256]{3,2,1,0:T(2,128)S(1)} collective-permute-done((f32[3,12,2,256]{3,2,1,0:T(2,128)S(1)}, f32[3,12,2,256]{3,2,1,0:T(2,128)S(1)}, u32[]{:S(2)}, u32[]{:S(2)}) %collective-permute-start.10) | collective-permute-done | bytes 73760 | tf_op jit(solution)/shard_map/ppermute | solution.py:359
  71.7 1.1 copy-done
  72.9 11.1 %shard_map.117 = (f32[3,8,32,256]{3,2,1,0:T(8,128)}, f32[10,8,128]{2,1,0:T(8,128)S(1)}) custom-call(s32[3,2,16]{2,1,0:T(2,128)S(1)} %copy-done.7, f32[3,8,32,256]{3,2,1,0:T(8,128)S(1)} %copy-done, f32[3,8,32,256]{3,2,1,0:T(8,128)S(1)} %get-tuple-element.57.refs_2_, s32[8,32,256]{2,1,0:T(8,128)S(1)} %get-tuple-element.39.refs_3_, ...), custom_call_target="tpu_custom_call" | custom-call | tf_op jit(solution)/shard_map/pallas_call | solution.py:345
  84.0 9.3 %collective-permute-start.12 = (f32[6,4,128]{2,1,0:T(4,128)S(1)}, f32[6,4,128]{2,1,0:T(4,128)S(1)}, u32[]{:S(2)}, u32[]{:S(2)}) collective-permute-start(f32[6,4,128]{2,1,0:T(4,128)S(1)} %slice.3), channel_id=1, source_target_pairs={{0,2},{1,3},{2,0},{3,1},{4,6},{5,7},{6,4},{7,5},{8,10},{9,11},{10,... | collective-permute-start | bytes 36872 | tf_op jit(solution)/shard_map/ppermute | solution.py:399
  93.3 1.7 %collective-permute-done.12 = f32[6,4,128]{2,1,0:T(4,128)S(1)} collective-permute-done((f32[6,4,128]{2,1,0:T(4,128)S(1)}, f32[6,4,128]{2,1,0:T(4,128)S(1)}, u32[]{:S(2)}, u32[]{:S(2)}) %collective-permute-start.12) | collective-permute-done | bytes 12320 | tf_op jit(solution)/shard_map/ppermute | solution.py:399
  95.0 3.9 %collective-permute-start.13 = (f32[6,8,128]{2,1,0:T(8,128)S(1)}, f32[6,8,128]{2,1,0:T(8,128)S(1)}, u32[]{:S(2)}, u32[]{:S(2)}) collective-permute-start(f32[6,8,128]{2,1,0:T(8,128)S(1)} %pad_maximum_fusion.2), channel_id=1, source_target_pairs={{0,4},{1,5},{2,6},{3,7},{4,0},{5,1},{6,2},{7,3},{8,12},{9,13},{10,... | collective-permute-start | bytes 73736 | tf_op jit(solution)/shard_map/ppermute | solution.py:399
  99.0 1.8 %collective-permute-done.13 = f32[6,8,128]{2,1,0:T(8,128)S(1)} collective-permute-done((f32[6,8,128]{2,1,0:T(8,128)S(1)}, f32[6,8,128]{2,1,0:T(8,128)S(1)}, u32[]{:S(2)}, u32[]{:S(2)}) %collective-permute-start.13) | collective-permute-done | bytes 24608 | tf_op jit(solution)/shard_map/ppermute | solution.py:399
  100.8 9.6 %collective-permute-start.14 = (f32[6,16,128]{2,1,0:T(8,128)S(1)}, f32[6,16,128]{2,1,0:T(8,128)S(1)}, u32[]{:S(2)}, u32[]{:S(2)}) collective-permute-start(f32[6,16,128]{2,1,0:T(8,128)S(1)} %pad_maximum_fusion.1), channel_id=1, source_target_pairs={{0,16},{8,24},{16,0},{24,8},{32,48},{40,56},{48,32},{56,40},{64,80... | collective-permute-start | bytes 147464 | tf_op jit(solution)/shard_map/ppermute | solution.py:399
  110.3 2.1 %collective-permute-done.14 = f32[6,16,128]{2,1,0:T(8,128)S(1)} collective-permute-done((f32[6,16,128]{2,1,0:T(8,128)S(1)}, f32[6,16,128]{2,1,0:T(8,128)S(1)}, u32[]{:S(2)}, u32[]{:S(2)}) %collective-permute-start.14) | collective-permute-done | bytes 49184 | tf_op jit(solution)/shard_map/ppermute | solution.py:399
  112.4 6.9 %collective-permute-start.15 = (f32[6,32,128]{2,1,0:T(8,128)S(1)}, f32[6,32,128]{2,1,0:T(8,128)S(1)}, u32[]{:S(2)}, u32[]{:S(2)}) collective-permute-start(f32[6,32,128]{2,1,0:T(8,128)S(1)} %pad_maximum_fusion), channel_id=1, source_target_pairs={{0,32},{8,40},{16,48},{24,56},{32,0},{40,8},{48,16},{56,24},{64,96... | collective-permute-start | bytes 294920 | tf_op jit(solution)/shard_map/ppermute | solution.py:399
  119.3 2.8 %collective-permute-done.15 = f32[6,32,128]{2,1,0:T(8,128)S(1)} collective-permute-done((f32[6,32,128]{2,1,0:T(8,128)S(1)}, f32[6,32,128]{2,1,0:T(8,128)S(1)}, u32[]{:S(2)}, u32[]{:S(2)}) %collective-permute-start.15) | collective-permute-done | bytes 98336 | tf_op jit(solution)/shard_map/ppermute | solution.py:399
  122.2 7.9 %collective-permute-start.16 = (f32[6,64,128]{2,1,0:T(8,128)S(1)}, f32[6,64,128]{2,1,0:T(8,128)S(1)}, u32[]{:S(2)}, u32[]{:S(2)}) collective-permute-start(f32[6,64,128]{2,1,0:T(8,128)S(1)} %concatenate.22), channel_id=1, source_target_pairs={{0,64},{8,72},{16,80},{24,88},{32,96},{40,104},{48,112},{56,120},{... | collective-permute-start | bytes 589832 | tf_op jit(solution)/shard_map/ppermute | solution.py:399
  130.1 3.6 %collective-permute-done.16 = f32[6,64,128]{2,1,0:T(8,128)S(1)} collective-permute-done((f32[6,64,128]{2,1,0:T(8,128)S(1)}, f32[6,64,128]{2,1,0:T(8,128)S(1)}, u32[]{:S(2)}, u32[]{:S(2)}) %collective-permute-start.16) | collective-permute-done | bytes 196640 | tf_op jit(solution)/shard_map/ppermute | solution.py:399
  133.8 1.2 shard_map.118
  (40 shorter events, 11.9 us)
Async XLA Ops:
  1.3 1.1 copy-start.1
  2.5 1.1 copy-start.2
  3.6 1.1 copy-start.3
  4.7 0.9 copy-start.4
  5.6 0.9 copy-start.5
  6.6 0.9 copy-start.6
  12.3 1.6 %collective-permute-start = (f32[216,256]{1,0:T(8,128)S(1)}, f32[216,256]{1,0:T(8,128)S(1)}, u32[]{:S(2)}, u32[]{:S(2)}) collective-permute-start(f32[216,256]{1,0:T(8,128)S(1)} %get-tuple-element.40), channel_id=1, source_target_pairs={{0,8},{8,0},{16,24},{24,16},{32,40},{40,32},{48,56},{56,48},{64,72... | collective-permute-start | bytes 663560 | tf_op jit(solution)/shard_map/ppermute | solution.py:359
  12.4 0.7 collective-permute-start.1
  13.9 4.4 %collective-permute-start.2 = (f32[3,12,2,256]{3,2,1,0:T(2,128)S(1)}, f32[3,12,2,256]{3,2,1,0:T(2,128)S(1)}, u32[]{:S(2)}, u32[]{:S(2)}) collective-permute-start(f32[3,12,2,256]{3,2,1,0:T(2,128)S(1)} %get-tuple-element.45), channel_id=1, source_target_pairs={{0,1},{1,0},{2,3},{3,2},{4,5},{5,4},{6,7},{7,6},{8,9},{9,8},{10,11... | collective-permute-start | bytes 221192 | tf_op jit(solution)/shard_map/ppermute | solution.py:359
  14.2 0.7 collective-permute-start.3
  28.7 7.4 %collective-permute-start.4 = (f32[216,256]{1,0:T(8,128)S(1)}, f32[216,256]{1,0:T(8,128)S(1)}, u32[]{:S(2)}, u32[]{:S(2)}) collective-permute-start(f32[216,256]{1,0:T(8,128)S(1)} %get-tuple-element.49), channel_id=1, source_target_pairs={{0,8},{8,0},{16,24},{24,16},{32,40},{40,32},{48,56},{56,48},{64,72... | collective-permute-start | bytes 663560 | tf_op jit(solution)/shard_map/ppermute | solution.py:359
  35.0 0.7 collective-permute-start.5
  36.2 5.9 %collective-permute-start.6 = (f32[3,12,2,256]{3,2,1,0:T(2,128)S(1)}, f32[3,12,2,256]{3,2,1,0:T(2,128)S(1)}, u32[]{:S(2)}, u32[]{:S(2)}) collective-permute-start(f32[3,12,2,256]{3,2,1,0:T(2,128)S(1)} %get-tuple-element.54), channel_id=1, source_target_pairs={{0,1},{1,0},{2,3},{3,2},{4,5},{5,4},{6,7},{7,6},{8,9},{9,8},{10,11... | collective-permute-start | bytes 221192 | tf_op jit(solution)/shard_map/ppermute | solution.py:359
  39.7 0.7 collective-permute-start.7
  54.7 11.6 %collective-permute-start.8 = (f32[216,256]{1,0:T(8,128)S(1)}, f32[216,256]{1,0:T(8,128)S(1)}, u32[]{:S(2)}, u32[]{:S(2)}) collective-permute-start(f32[216,256]{1,0:T(8,128)S(1)} %get-tuple-element.58), channel_id=1, source_target_pairs={{0,8},{8,0},{16,24},{24,16},{32,40},{40,32},{48,56},{56,48},{64,72... | collective-permute-start | bytes 663560 | tf_op jit(solution)/shard_map/ppermute | solution.py:359
  65.2 0.7 collective-permute-start.9
  66.3 5.4 %collective-permute-start.10 = (f32[3,12,2,256]{3,2,1,0:T(2,128)S(1)}, f32[3,12,2,256]{3,2,1,0:T(2,128)S(1)}, u32[]{:S(2)}, u32[]{:S(2)}) collective-permute-start(f32[3,12,2,256]{3,2,1,0:T(2,128)S(1)} %get-tuple-element.63), channel_id=1, source_target_pairs={{0,1},{1,0},{2,3},{3,2},{4,5},{5,4},{6,7},{7,6},{8,9},{9,8},{10,11... | collective-permute-start | bytes 221192 | tf_op jit(solution)/shard_map/ppermute | solution.py:359
  69.4 0.7 collective-permute-start.11
  71.7 1.1 copy-start
  84.0 11.0 %collective-permute-start.12 = (f32[6,4,128]{2,1,0:T(4,128)S(1)}, f32[6,4,128]{2,1,0:T(4,128)S(1)}, u32[]{:S(2)}, u32[]{:S(2)}) collective-permute-start(f32[6,4,128]{2,1,0:T(4,128)S(1)} %slice.3), channel_id=1, source_target_pairs={{0,2},{1,3},{2,0},{3,1},{4,6},{5,7},{6,4},{7,5},{8,10},{9,11},{10,... | collective-permute-start | bytes 36872 | tf_op jit(solution)/shard_map/ppermute | solution.py:399
  95.0 5.8 %collective-permute-start.13 = (f32[6,8,128]{2,1,0:T(8,128)S(1)}, f32[6,8,128]{2,1,0:T(8,128)S(1)}, u32[]{:S(2)}, u32[]{:S(2)}) collective-permute-start(f32[6,8,128]{2,1,0:T(8,128)S(1)} %pad_maximum_fusion.2), channel_id=1, source_target_pairs={{0,4},{1,5},{2,6},{3,7},{4,0},{5,1},{6,2},{7,3},{8,12},{9,13},{10,... | collective-permute-start | bytes 73736 | tf_op jit(solution)/shard_map/ppermute | solution.py:399
  100.8 11.6 %collective-permute-start.14 = (f32[6,16,128]{2,1,0:T(8,128)S(1)}, f32[6,16,128]{2,1,0:T(8,128)S(1)}, u32[]{:S(2)}, u32[]{:S(2)}) collective-permute-start(f32[6,16,128]{2,1,0:T(8,128)S(1)} %pad_maximum_fusion.1), channel_id=1, source_target_pairs={{0,16},{8,24},{16,0},{24,8},{32,48},{40,56},{48,32},{56,40},{64,80... | collective-permute-start | bytes 147464 | tf_op jit(solution)/shard_map/ppermute | solution.py:399
  112.4 9.7 %collective-permute-start.15 = (f32[6,32,128]{2,1,0:T(8,128)S(1)}, f32[6,32,128]{2,1,0:T(8,128)S(1)}, u32[]{:S(2)}, u32[]{:S(2)}) collective-permute-start(f32[6,32,128]{2,1,0:T(8,128)S(1)} %pad_maximum_fusion), channel_id=1, source_target_pairs={{0,32},{8,40},{16,48},{24,56},{32,0},{40,8},{48,16},{56,24},{64,96... | collective-permute-start | bytes 294920 | tf_op jit(solution)/shard_map/ppermute | solution.py:399
  122.2 11.5 %collective-permute-start.16 = (f32[6,64,128]{2,1,0:T(8,128)S(1)}, f32[6,64,128]{2,1,0:T(8,128)S(1)}, u32[]{:S(2)}, u32[]{:S(2)}) collective-permute-start(f32[6,64,128]{2,1,0:T(8,128)S(1)} %concatenate.22), channel_id=1, source_target_pairs={{0,64},{8,72},{16,80},{24,88},{32,96},{40,104},{48,112},{56,120},{... | collective-permute-start | bytes 589832 | tf_op jit(solution)/shard_map/ppermute | solution.py:399
  (1 other events, 0.7 us)

commit v2 on v1

v2 whole, which is shorter than its diff:
```python
import functools
import math

import jax
import jax.numpy as jnp
from jax import lax
from jax.experimental import pallas as pl
from jax.experimental.pallas import tpu as pltpu
from jax.sharding import PartitionSpec as P

SUB = 3
SL = 4
SLOTS = 16
CHUNK = 4
STEP = 2
GROUP = 4
ROUNDS = (("slab", 8), ("slab", 4), ("split", 2), ("split", 4), ("slab", 2))

DT = 0.25
STIFF = 0.5
CONTACT = 0.05
WIDTH = 8.0
INV_MASS = 0.5

CX, CY, CZ = 8, 32, 256
LO = 8
F32 = jnp.float32


def bond_offsets():
    listed = []
    for sx in (-2, -1, 0, 1, 2):
        for sy in (-2, -1, 0, 1, 2):
            for sz in (-2, -1, 0, 1, 2):
                if 0 < sx * sx + sy * sy + sz * sz <= 4:
                    listed.append((sx, sy, sz))
    return listed


OFFSETS = bond_offsets()


def as_int32(bits):
    return bits - (1 << 32) if bits >= 1 << 31 else bits


def keep_bits(dim, allowed):
    return as_int32(sum(1 << n for n, e in enumerate(OFFSETS) if allowed(e[dim])))


def keep_word(index, last, dim):
    word = jnp.where(index == 0, keep_bits(dim, lambda e: e >= 0), -1)
    word = jnp.where(index == 1, keep_bits(dim, lambda e: e >= -1), word)
    word = jnp.where(index == last - 1, keep_bits(dim, lambda e: e <= 1), word)
    return jnp.where(index == last, keep_bits(dim, lambda e: e <= 0), word)


def position():
    return lax.axis_index("slab"), lax.axis_index("split")


def lane_sums(parts):
    whole = jnp.concatenate(parts, axis=0)
    high = whole.astype(jnp.bfloat16)
    low = (whole - high.astype(F32)).astype(jnp.bfloat16)
    ones = jnp.ones((256, 128), jnp.bfloat16)
    return jnp.dot(jnp.concatenate([high, low], axis=1), ones, preferred_element_type=F32)


def contact(substep, pairs, u_ref, half_ref, places, share, pos, ids, corner):
    row = lax.broadcasted_iota(jnp.int32, (CY, 128), 0)
    lane = lax.broadcasted_iota(jnp.int32, (CY, 128), 1)
    place_y = (row + corner[1]).astype(F32)
    live = jnp.int32(0)
    for k in range(SLOTS):
        live += (pairs[substep, 1, k] >= 0).astype(jnp.int32)

    @pl.when(live > 0)
    def _():
        def place(x, carry):
            for c in range(3):
                top = u_ref[c, 1, x + 2, LO : LO + CY, :]
                for z in range(SL):
                    lattice = ((corner[0] + x).astype(F32), place_y, float(CZ - SL + z))[c]
                    at = 128 - SL + z
                    column = jnp.broadcast_to(top[:, at : at + 1], (CY, 128))
                    places[c, x, z * CY : (z + 1) * CY, :] = column + lattice
            return carry

        lax.fori_loop(0, CX, place, 0)

    def slot(k, totals):
        target = jnp.clip(pairs[substep, 0, k], 0, CX - 1)
        chosen = pairs[substep, 1, k]
        hit = ids == chosen
        stiff = jnp.where(chosen >= 0, CONTACT, 0.0)
        q = [jnp.sum(jnp.where(hit, pos[c], 0.0), axis=0, keepdims=True) for c in range(3)]
        r = [places[c, target] - q[c] for c in range(3)]
        squared = r[0] * r[0] + r[1] * r[1] + r[2] * r[2]
        weight = stiff * jnp.exp(squared * (-1.0 / WIDTH))
        pulled = [weight * r[c] for c in range(3)]
        sums = lane_sums(pulled)
        for c in range(3):
            surface = jnp.zeros((CY, 128), F32)
            for z in range(SL):
                at = c * SL * CY + z * CY
                surface = jnp.where(lane == 128 - SL + z, sums[at : at + CY], surface)
            half_ref[c, target, :, CZ - 128 :] += share * surface
        return tuple(
            totals[c] - jnp.where(hit, jnp.sum(pulled[c], axis=0, keepdims=True), 0.0)
            for c in range(3)
        )

    def some(k, totals):
        for j in range(CHUNK):
            totals = slot(CHUNK * k + j, totals)
        return totals

    none = tuple(jnp.zeros((8, 128), F32) for _ in range(3))
    return lax.fori_loop(0, (live + CHUNK - 1) // CHUNK, some, none)


def send_edges(u_ref, force, xa, xb, ya, yb, even_x, even_y):
    at_a = jnp.where(even_x, CX, 2)
    at_b = jnp.where(even_x, 2, CX)
    for c in range(3):
        for h in range(2):
            lanes = slice(128 * h, 128 * h + 128)
            for layer in range(2):
                rows = slice((2 * c + layer) * CY, (2 * c + layer + 1) * CY)
                xa[rows, lanes] = u_ref[c, h, at_a + layer, LO : LO + CY, :]
                xb[rows, lanes] = u_ref[c, h, at_b + layer, LO : LO + CY, :]
            xa[6 * CY + 8 * c : 6 * CY + 8 * c + 8, lanes] = force[c]
    for want_even, low, high in ((True, yb, ya), (False, ya, yb)):

        @pl.when(even_y == want_even)
        def _(low=low, high=high):
            for c in range(3):
                for h in range(2):
                    lanes = slice(128 * h, 128 * h + 128)
                    for x in range(CX):
                        for r in range(2):
                            low[c, r, x : x + 1, lanes] = u_ref[c, h, x + 2, LO + r : LO + r + 1, :]
                            high[c, r, x : x + 1, lanes] = u_ref[
                                c, h, x + 2, LO + CY - 2 + r : LO + CY - 1 + r, :
                            ]


def begin_kernel(
    pairs, u, v, a, pp, pv, pa,
    u_out, half_out, pst, perm, xa, xb, ya, yb, places, cells, blocks_in, sems, block_sems,
):
    slab, split = position()
    splits = lax.axis_size("split")
    even_x, even_y = lax.rem(slab, 2) == 0, lax.rem(split, 2) == 0

    copies = []
    for x in range(0, CX, STEP):
        copies.append(
            [
                pltpu.make_async_copy(
                    source.at[:, x : x + STEP], cells.at[k, :, x : x + STEP], sems.at[k, x // STEP]
                )
                for k, source in enumerate((u, v, a))
            ]
        )
    block_copies = [
        pltpu.make_async_copy(source, blocks_in.at[k], block_sems.at[k])
        for k, source in enumerate((pp, pv, pa))
    ]
    for copy in block_copies:
        copy.start()
    for group in copies:
        for copy in group:
            copy.start()

    for copy in block_copies:
        copy.wait()
    pp, pv, pa = blocks_in.at[0], blocks_in.at[1], blocks_in.at[2]
    blocks = pp.shape[1]
    mean_x = jnp.sum(pp[0], axis=1, keepdims=True) * (1.0 / pp.shape[2])
    mean_y = jnp.sum(pp[1], axis=1, keepdims=True) * (1.0 / pp.shape[2])
    group_x = jnp.floor((mean_x + 0.5) * (1.0 / (2 * CX)))
    group_y = jnp.floor((mean_y + 0.5) * (1.0 / (2 * CY)))
    group = jnp.broadcast_to(group_x * (splits // 2) + group_y, (blocks, blocks))
    row = lax.broadcasted_iota(jnp.int32, (blocks, blocks), 0)
    lane = lax.broadcasted_iota(jnp.int32, (blocks, blocks), 1)
    earlier = jnp.where((group == group.T) & (lane < row), 1.0, 0.0)
    rank = jnp.sum(earlier, axis=1, keepdims=True).astype(jnp.int32)
    group = group.astype(jnp.int32)
    mine = (slab // 2) * (splits // 2) + split // 2
    other = group ^ mine
    slot = rank
    for order, (axis, bit) in enumerate(ROUNDS):
        place = bit // 2 * (splits // 2 if axis == "slab" else 1)
        slot = slot + jnp.where((other & place) != 0, GROUP << order, 0)
    perm[...] = jnp.where(slot == lane, 1.0, 0.0)

    pst[...] = jnp.zeros_like(pst)
    pst[6] = jnp.full((8, 128), -5.0, F32)
    for k in range(GROUP):
        chosen = slot == k
        pst[6, k : k + 1, :] = jnp.sum(jnp.where(chosen, row.astype(F32), 0.0), axis=0, keepdims=True)
        for c in range(3):
            pos, vel, acc = [
                jnp.sum(jnp.where(chosen, p[c], 0.0), axis=0, keepdims=True) for p in (pp, pv, pa)
            ]
            half = vel + 0.5 * DT * acc
            pst[3 + c, k : k + 1, :] = half
            pst[c, k : k + 1, :] = pos + DT * half

    for at, waits in zip(range(0, CX, STEP), copies):
        for copy in waits:
            copy.wait()
        for x in range(at, at + STEP):
            for c in range(3):
                half = cells[1, c, x] + 0.5 * DT * cells[2, c, x]
                half_out[c, x] = half
                moved = cells[0, c, x] + DT * half
                for h in range(2):
                    u_out[c, h, x + 2, LO : LO + CY, :] = moved[:, 128 * h : 128 * h + 128]

    ids = pst[6].astype(jnp.int32)
    pos = [pst[c] for c in range(3)]
    force = contact(0, pairs, u_out, half_out, places, DT, pos, ids, (slab * CX, split * CY))
    for c in range(3):
        pst[7 + c] = force[c]
    send_edges(u_out, force, xa, xb, ya, yb, even_x, even_y)


def words_kernel(masks, w_out, rim_out):
    slab, split = position()
    slabs, splits = lax.axis_size("slab"), lax.axis_size("split")

    for x in range(CX):
        kx = keep_word(slab * CX + x, slabs * CX - 1, 0)
        y = lax.broadcasted_iota(jnp.int32, (CY, CZ), 0)
        ky = keep_word(split * CY + y, splits * CY - 1, 1)
        kz = keep_word(lax.broadcasted_iota(jnp.int32, (CY, CZ), 1), CZ - 1, 2)
        word = masks[0, x] | (masks[1, x] << 8) | (masks[2, x] << 16) | (masks[3, x] << 24)
        word = word & ky & kz & kx
        w_out[x] = word & keep_word(y, CY - 1, 1)
        for r in range(4):
            y = r if r < 2 else CY - 4 + r
            rim_out[r, x : x + 1, :] = word[y : y + 1, :]


def corner_kernel(ya_own, yb_own, xa, xb, pst, token, ya, yb):
    slab, split = position()
    even_x, even_y = lax.rem(slab, 2) == 0, lax.rem(split, 2) == 0
    for c in range(3):
        for r in range(2):
            ya[c, r, 0:CX, :] = ya_own[c, r]
            yb[c, r, 0:CX, :] = yb_own[c, r]
        force = pst[7 + c] + xa[6 * CY + 8 * c : 6 * CY + 8 * c + 8, 0:128]
        for h in range(2):
            ya[c, 0, CX + 2 : CX + 2 + GROUP, 128 * h : 128 * h + 128] = force[0:GROUP]
    for is_x in (True, False):
        for is_y in (True, False):

            @pl.when((even_x == is_x) & (even_y == is_y))
            def _(is_x=is_x, is_y=is_y):
                for c in range(3):
                    for message, high in ((ya, is_y), (yb, not is_y)):
                        for got, top in ((xa, is_x), (xb, not is_x)):
                            entry, layer = (CX + 1, 0) if top else (CX, 1)
                            for r in range(2):
                                at = (2 * c + layer) * CY + (CY - 2 if high else 0) + r
                                message[c, r, entry : entry + 1, :] = got[at : at + 1, :]


def rolled(u, c, x, at, by):
    lane = lax.broadcasted_iota(jnp.int32, (8, 128), 1)
    turned = [pltpu.roll(u[c, h, x, at, :], by % 128, 1) for h in range(2)]
    wraps = lane < by if by > 0 else lane >= 128 + by
    return [jnp.where(wraps, turned[1 - h], turned[h]) for h in range(2)]


def turn(u, left, right, x, y):
    at = slice(y, y + 8)
    for c in range(3):
        for side, by in ((left, -1), (right, 1)):
            for h, value in enumerate(rolled(u, c, x, at, by)):
                side[c, h, x - 1, at, :] = value


def forces(u, left, right, w, x, y, h):
    own = [u[c, h, x + 2, LO + y : LO + y + 8, :] for c in range(3)]
    less = {(c, e): own[c] - float(e) if e else own[c] for c in range(3) for e in (-2, -1, 0, 1, 2)}
    word = w[x, y : y + 8, 128 * h : 128 * h + 128]
    total = [None] * 3
    for squared_length in (1, 2, 3, 4):
        sums = [None] * 3
        for number, e in enumerate(OFFSETS):
            if sum(k * k for k in e) != squared_length:
                continue
            at = slice(LO + y + e[1], LO + y + e[1] + 8)
            if e[2] == 0:
                near = [u[c, h, x + 2 + e[0], at, :] for c in range(3)]
            elif abs(e[2]) == 2:
                near = [rolled(u, c, x + 2, at, -e[2])[h] for c in range(3)]
            else:
                source = left if e[2] > 0 else right
                near = [source[c, h, x + 1 + e[0], at, :] for c in range(3)]
            d = [near[c] - less[c, e[c]] for c in range(3)]
            q = jnp.maximum(d[0] * d[0] + d[1] * d[1] + d[2] * d[2], 1e-30)
            pull = q * lax.rsqrt(q) - math.sqrt(squared_length)
            pull = jnp.where((word & as_int32(1 << number)) != 0, pull, 0.0)
            for c in range(3):
                if e[c] > 0:
                    sums[c] = pull if sums[c] is None else sums[c] + pull
                elif e[c] < 0:
                    sums[c] = -pull if sums[c] is None else sums[c] - pull
        factor = STIFF / squared_length * (2.0 if squared_length == 4 else 1.0)
        for c in range(3):
            term = factor * sums[c]
            total[c] = term if total[c] is None else total[c] + term
    return total


def advance(scale, u, left, right, w, half, half_out, first, out_first, count):
    def layer(k, carry):
        x = first + k
        for y in range(0, CY, 8):
            for h in range(2):
                at, lanes = slice(y, y + 8), slice(128 * h, 128 * h + 128)
                total = forces(u, left, right, w, x, y, h)
                for c in range(3):
                    half_out[c, out_first + k, at, lanes] = half[c, x, at, lanes] + scale * total[c]
        return carry

    lax.fori_loop(0, count, layer, 0)


def turned_layers(u, left, right):
    def shifted(x, carry):
        for y in range(LO, LO + CY, 8):
            turn(u, left, right, x, y)
        return carry

    lax.fori_loop(2, CX + 2, shifted, 0)


def inner_kernel(scale, u, half, w, half_out, left, right, token):
    turned_layers(u, left, right)
    advance(scale, u, left, right, w, half, half_out, 2, 0, CX - 4)
    token[...] = half_out[0, 0, 0:8, 0:128]


def edge_kernel(scale, xa, xb, u_own, left_own, right_own, half, w, after, half_out, token, u, left, right):
    slab, split = position()
    even_x = lax.rem(slab, 2) == 0
    to_a = jnp.where(even_x, CX + 2, 0)
    to_b = jnp.where(even_x, 0, CX + 2)
    rows = slice(LO, LO + CY)
    for c in range(3):
        for layer in range(2):
            part = slice((2 * c + layer) * CY, (2 * c + layer + 1) * CY)
            for h in range(2):
                lanes = slice(128 * h, 128 * h + 128)
                u[c, h, to_a + layer, rows, :] = xa[part, lanes]
                u[c, h, to_b + layer, rows, :] = xb[part, lanes]

    def own(x, carry):
        for c in range(3):
            for h in range(2):
                u[c, h, x + 2, rows, :] = u_own[c, h, x + 2, rows, :]
                left[c, h, x + 1, rows, :] = left_own[c, h, x + 1, rows, :]
                right[c, h, x + 1, rows, :] = right_own[c, h, x + 1, rows, :]
        return carry

    lax.fori_loop(0, CX, own, 0)
    for x in (1, CX + 2):
        for y in range(LO, LO + CY, 8):
            turn(u, left, right, x, y)
    advance(scale, u, left, right, w, half, half_out, 0, 0, 2)
    advance(scale, u, left, right, w, half, half_out, CX - 2, 2, 2)
    token[...] = half_out[0, 0, 0:8, 0:128]


def rim_forces(own, halo, rim, side, even_y, crossing):
    sub = lax.broadcasted_iota(jnp.int32, (8, 128), 0)
    lane = lax.broadcasted_iota(jnp.int32, (8, 128), 1)
    sign = -1 if side == 0 else 1
    for h in range(2):
        lanes = slice(128 * h, 128 * h + 128)
        total = [[None] * 3, [None] * 3]
        variants = {}

        def near(c, r, ex, ez):
            key = (c, r, ex, ez)
            if key not in variants:
                if ez:
                    both = [near_at(c, r, ex, k) for k in range(2)]
                    turned = [pltpu.roll(value, -ez % 128, 1) for value in both]
                    wraps = lane < -ez if ez < 0 else lane >= 128 - ez
                    variants[key] = jnp.where(wraps, turned[1 - h], turned[h])
                else:
                    variants[key] = near_at(c, r, ex, h)
            return variants[key]

        def near_at(c, r, ex, k):
            here = halo(c, r, slice(0, 8), k)
            if ex == 0:
                return here
            ends = halo(c, r, slice(8, 16), k)
            if ex > 0:
                return jnp.where(sub == 7, ends[1:2], pltpu.roll(here, 7, 0))
            return jnp.where(sub == 0, ends[0:1], pltpu.roll(here, 1, 0))

        for number, e in enumerate(OFFSETS):
            if e[1] * sign <= 0:
                continue
            squared_length = sum(k * k for k in e)
            for r in range(2):
                if abs(e[1]) <= r:
                    continue
                beyond = abs(e[1]) - r - 1
                mine = 1 - r if side else r
                theirs = beyond if side else 1 - beyond
                d = [near(c, theirs, e[0], e[2]) - (own(c, mine, h) - float(e[c])) for c in range(3)]
                q = jnp.maximum(d[0] * d[0] + d[1] * d[1] + d[2] * d[2], 1e-30)
                pull = (q * lax.rsqrt(q) - math.sqrt(squared_length)) * (STIFF / squared_length)
                word = rim[2 * side + mine, :, lanes]
                pull = jnp.where((word & as_int32(1 << number)) != 0, pull, 0.0)
                for c in range(3):
                    if e[c]:
                        term = float(e[c]) * pull
                        total[mine][c] = term if total[mine][c] is None else total[mine][c] + term
        for mine in range(2):
            for c in range(3):
                value = total[mine][c]
                crossing[2 * side + mine, c, h] = jnp.zeros((8, 128), F32) if value is None else value


def close(scale, inner, edge, ya_own, yb_own, ya, yb, rim, even_y, crossing, store):
    for side in range(2):
        first = even_y == (side == 1)

        def own(c, r, h):
            lanes = slice(128 * h, 128 * h + 128)
            return jnp.where(first, ya_own[c, r, :, lanes], yb_own[c, r, :, lanes])

        def halo(c, r, rows, h):
            lanes = slice(128 * h, 128 * h + 128)
            return jnp.where(first, ya[c, r, rows, lanes], yb[c, r, rows, lanes])

        rim_forces(own, halo, rim, side, even_y, crossing)
    sub = lax.broadcasted_iota(jnp.int32, (8, 128), 0)
    for x in range(CX):
        source, at = (inner, x - 2) if 2 <= x < CX - 2 else (edge, x if x < 2 else x - CX + 4)
        for c in range(3):
            for h in range(2):
                for y in range(0, CY, 8):
                    value = source[c, at, y : y + 8, 128 * h : 128 * h + 128]
                    for r in (0, 1) if y == 0 else (2, 3) if y == CY - 8 else ():
                        more = crossing[r, c, h, x : x + 1, :]
                        value = value + scale * jnp.where(sub == (r if r < 2 else r + 4), more, 0.0)
                    store(c, x, y, h, value)


def particle_force(xa, ya, pst, c):
    theirs = jnp.concatenate([ya[c, 0, CX + 2 : CX + 2 + GROUP, 0:128], jnp.zeros((4, 128), F32)], axis=0)
    return pst[7 + c] + xa[6 * CY + 8 * c : 6 * CY + 8 * c + 8, 0:128] + theirs


def close_kernel(
    substep, pairs, u, inner, edge, ya_own, yb_own, xa, ya, yb, rim, pst,
    u_out, half_out, pst_out, xa_out, xb_out, ya_out, yb_out, places, crossing,
):
    slab, split = position()
    even_x, even_y = lax.rem(slab, 2) == 0, lax.rem(split, 2) == 0

    def store(c, x, y, h, value):
        half_out[c, x, y : y + 8, 128 * h : 128 * h + 128] = value
        pad = slice(LO + y, LO + y + 8)
        u_out[c, h, x + 2, pad, :] = u[c, h, x + 2, pad, :] + DT * value

    close(DT, inner, edge, ya_own, yb_own, ya, yb, rim, even_y, crossing, store)

    pst_out[6:] = pst[6:]
    pos = []
    for c in range(3):
        moved = pst[3 + c] + DT * INV_MASS * particle_force(xa, ya, pst, c)
        pst_out[3 + c] = moved
        pos.append(pst[c] + DT * moved)
        pst_out[c] = pos[c]
    share = 0.5 * DT if substep == SUB - 2 else DT
    ids = pst[6].astype(jnp.int32)
    corner = (slab * CX, split * CY)
    force = contact(substep + 1, pairs, u_out, half_out, places, share, pos, ids, corner)
    for c in range(3):
        pst_out[7 + c] = force[c]
    send_edges(u_out, force, xa_out, xb_out, ya_out, yb_out, even_x, even_y)


def pair_kernel(xa, pst, out):
    for c in range(3):
        out[c] = pst[7 + c] + xa[6 * CY + 8 * c : 6 * CY + 8 * c + 8, 0:128]


def state_kernel(ours, theirs, pst, token, out):
    for c in range(3):
        out[c] = pst[c, 0:GROUP]
        acc = INV_MASS * (ours[c] + theirs[c])
        out[3 + c] = (pst[3 + c] + 0.5 * DT * acc)[0:GROUP]


def merge_kernel(ours, theirs, token, out):
    count = ours.shape[1]
    out[:, 0:count] = ours[...]
    out[:, count : 2 * count] = theirs[...]


def last_kernel(u, inner, edge, ya_own, yb_own, ya, yb, rim, after, u_out, v_out, token, crossing):
    slab, split = position()

    def store(c, x, y, h, value):
        lanes = slice(128 * h, 128 * h + 128)
        v_out[c, x, y : y + 8, lanes] = value
        u_out[c, x, y : y + 8, lanes] = u[c, h, x + 2, LO + y : LO + y + 8, :]

    even_y = lax.rem(split, 2) == 0
    close(0.5 * DT, inner, edge, ya_own, yb_own, ya, yb, rim, even_y, crossing, store)
    token[...] = crossing[0, 0, 0]


def final_kernel(perm, gathered, pos_out, vel_out):
    for c in range(3):
        for at, out in ((c, pos_out), (3 + c, vel_out)):
            out[c] = jnp.dot(
                perm[...],
                gathered[at],
                precision=lax.Precision.HIGHEST,
                preferred_element_type=F32,
            )


VMEM = pl.BlockSpec(memory_space=pltpu.VMEM)
SMEM = pl.BlockSpec(memory_space=pltpu.SMEM)
HBM = pl.BlockSpec(memory_space=pltpu.HBM)
STATE = jax.ShapeDtypeStruct((3, CX, CY, CZ), F32)
PADDED = jax.ShapeDtypeStruct((3, 2, CX + 4, CY + 16, 128), F32)
SIDE = jax.ShapeDtypeStruct((3, 2, CX + 2, CY + 16, 128), F32)
WORDS = jax.ShapeDtypeStruct((CX, CY, CZ), jnp.int32)
PST = jax.ShapeDtypeStruct((10, 8, 128), F32)
XA = jax.ShapeDtypeStruct((6 * CY + 24, CZ), F32)
XB = jax.ShapeDtypeStruct((6 * CY, CZ), F32)
YE = jax.ShapeDtypeStruct((3, 2, CX, CZ), F32)
YA = jax.ShapeDtypeStruct((3, 2, 16, CZ), F32)
PAIR = jax.ShapeDtypeStruct((3, 8, 128), F32)
TOKEN = jax.ShapeDtypeStruct((8, 128), F32)
HALVES = jax.ShapeDtypeStruct((3, 4, CY, CZ), F32)
RIM = jax.ShapeDtypeStruct((4, CX, CZ), jnp.int32)
CROSSING = pltpu.VMEM((4, 3, 2, CX, 128), F32)
PLACES = pltpu.VMEM((3, CX, SL * CY, 128), F32)


def call(kernel, inputs, outputs, scalars=0, scratch=(), ins=None, limit=40, us=1.0):
    return pl.pallas_call(
        kernel,
        out_shape=outputs,
        in_specs=ins or [SMEM] * scalars + [VMEM] * (len(inputs) - scalars),
        out_specs=[VMEM] * len(outputs),
        scratch_shapes=list(scratch),
        compiler_params=pltpu.CompilerParams(vmem_limit_bytes=limit << 20),
        cost_estimate=pl.CostEstimate(flops=0, transcendentals=0, bytes_accessed=int(us * 3.0e6)),
    )(*inputs)


def swap(value, axis, offset):
    pairs = []
    for i in range(offset, lax.axis_size(axis) - 1, 2):
        pairs += [(i, i + 1), (i + 1, i)]
    return lax.ppermute(value, axis, pairs)


def rows_of(count):
    return jax.ShapeDtypeStruct((6, count, 128), F32)


def share_round(gathered, number, token):
    axis, bit = ROUNDS[number]
    theirs = lax.ppermute(gathered, axis, [(i, i ^ bit) for i in range(lax.axis_size(axis))])
    (merged,) = call(merge_kernel, (gathered, theirs, token), [rows_of(2 * gathered.shape[1])], us=0.1)
    return merged


def per_device(u, v, a, masks, proj_pos, proj_vel, proj_acc, pairs):
    pp, pv, pa = [jnp.transpose(p, (1, 0, 2)) for p in (proj_pos, proj_vel, proj_acc)]
    blocks = pp.shape[1]
    u, half, pst, perm, *edges = call(
        begin_kernel,
        (pairs, u, v, a, pp, pv, pa),
        [PADDED, STATE, PST, jax.ShapeDtypeStruct((blocks, blocks), F32), XA, XB, YE, YE],
        ins=[SMEM] + [HBM] * 6,
        limit=60,
        scratch=(
            PLACES,
            pltpu.VMEM((3, *STATE.shape), F32),
            pltpu.VMEM((3, *pp.shape), F32),
            pltpu.SemaphoreType.DMA((3, CX // STEP)),
            pltpu.SemaphoreType.DMA((3,)),
        ),
    )
    words, rim = call(words_kernel, (masks,), [WORDS, RIM])
    for substep in range(SUB):
        last = substep == SUB - 1
        scale = 0.5 * DT if last else DT
        xa, xb, ya_own, yb_own = edges
        xa, xb = swap(xa, "slab", 0), swap(xb, "slab", 1)
        if last:
            (ours,) = call(pair_kernel, (xa, pst), [PAIR], us=0.1)
            theirs = swap(ours, "split", 0)
        inner, left, right, token = call(
            functools.partial(inner_kernel, scale), (u, half, words), [HALVES, SIDE, SIDE, TOKEN], us=3.6
        )
        ya, yb = call(corner_kernel, (ya_own, yb_own, xa, xb, pst, token), [YA, YA], us=0.1)
        ya, yb = swap(ya, "split", 0), swap(yb, "split", 1)
        after = token
        if last:
            (gathered,) = call(state_kernel, (ours, theirs, pst, token), [rows_of(GROUP)], us=0.1)
            gathered = after = share_round(gathered, 0, token)
        edge, token = call(
            functools.partial(edge_kernel, scale),
            (xa, xb, u, left, right, half, words, after),
            [HALVES, TOKEN],
            scratch=[pltpu.VMEM(shape.shape, F32) for shape in (PADDED, SIDE, SIDE)],
            us=3.6,
        )
        if last:
            break
        u, half, pst, *edges = call(
            functools.partial(close_kernel, substep),
            (pairs, u, inner, edge, ya_own, yb_own, xa, ya, yb, rim, pst),
            [PADDED, STATE, PST, XA, XB, YE, YE],
            scalars=1,
            scratch=(PLACES, CROSSING),
            us=3.0,
        )

    gathered = share_round(gathered, 1, token)
    final_u, final_v, token = call(
        last_kernel,
        (u, inner, edge, ya_own, yb_own, ya, yb, rim, gathered),
        [STATE, STATE, TOKEN],
        scratch=(CROSSING,),
        us=1.4,
    )
    for number in range(2, len(ROUNDS)):
        gathered = share_round(gathered, number, token)
    final_pos, final_vel = call(final_kernel, (perm, gathered), [jax.ShapeDtypeStruct(pp.shape, F32)] * 2)
    return (
        final_u,
        final_v,
        jnp.transpose(final_pos, (1, 0, 2)),
        jnp.transpose(final_vel, (1, 0, 2)),
    )


def solution(mesh):
    cells = P(None, "slab", "split", None)
    return jax.shard_map(
        per_device,
        mesh=mesh,
        in_specs=(cells, cells, cells, cells, P(), P(), P(), P(None, None, ("slab", "split"))),
        out_specs=(cells, cells, P(), P()),
        check_vma=False,
    )
```

time: 137 us -> 97.8 us (0.71)
  the two profiles are of different devices: /device:TPU:0 before, /device:TPU:24 now
where the time goes in v2:
time: 97.8 us; the launch traced here: 96.7 us
  Pallas kernels  34.4 us (35%)
  starting transfers between devices  32.8 us (34%)
  waiting for transfers between devices  27 us (28%)
  local copies, waits for them, and re-layouts  1.51 us (2%)
  between operations  1.02 us (1%)
    pallas_call x22, Pallas kernels, call(): pl.pallas_call(kernel, out_shape=outputs, in_specs=ins or [SMEM] * scalar...  34.4 us
    ppermute x13, starting transfers between devices, swap(): return lax.ppermute(value, axis, pairs)  29.6 us
    ppermute x5, waiting for transfers between devices, share_round(): lax.ppermute(gathered, axis, [(i, i ^ bit) for i in range(lax.axis_size(a...  19.1 us
    ppermute x13, waiting for transfers between devices, swap(): return lax.ppermute(value, axis, pairs)  7.84 us
    ppermute x5, starting transfers between devices, share_round(): lax.ppermute(gathered, axis, [(i, i ^ bit) for i in range(lax.axis_size(a...  3.19 us
  transfers between devices with their start and end apart: 18, of which 9 were waited for; matrix products, arithmetic and copies ran while one was open for 0% of the time, Pallas kernels for 23%

profile of v2, /device:TPU:24, one launch (start us, length us, event | category | flops | bytes accessed | tf_op | source)
XLA Modules:
  0.0 96.7 jit_solution(11587070279059166907)
XLA Ops:
  0.6 6.7 %shard_map.111 = (f32[3,2,12,48,128]{4,3,2,1,0:T(8,128)}, f32[3,8,32,256]{3,2,1,0:T(8,128)}, f32[10,8,128]{2,1,0:T(8,128)}, f32[128,128]{1,0:T(8,128)}, f32[216,...) custom-call(s32[3,2,16]{2,1,0:T(2,128)} %pairs.5, f32[3,8,32,256]{3,2,1,0:T(8,128)} %u.1, ...), custom_call_target="tpu_custom_call" | custom-call | bytes 3000000 | tf_op jit(solution)/shard_map/pallas_call | solution.py:560
  7.5 6.7 %collective-permute-start.1 = (f32[192,256]{1,0:T(8,128)}, f32[192,256]{1,0:T(8,128)S(1)}, u32[]{:S(2)}, u32[]{:S(2)}) collective-permute-start(f32[192,256]{1,0:T(8,128)} %get-tuple-element.60), channel_id=1, source_target_pairs={{8,16},{16,8},{24,32},{32,24},{40,48},{48,40},{56,64},{64,56},{72,... | collective-permute-start | bytes 589832 | tf_op jit(solution)/shard_map/ppermute | solution.py:575
  15.8 3.6 %shard_map.113 = (f32[3,4,32,256]{3,2,1,0:T(8,128)S(1)}, f32[3,2,10,48,128]{4,3,2,1,0:T(8,128)S(1)}, f32[3,2,10,48,128]{4,3,2,1,0:T(8,128)S(1)}, f32[8,128]{1,0:T(8,128)S(1)}) custom-call(f32[3,2,12,48,128]{4,3,2,1,0:T(8,128)S(1)} %copy-done, f32[3,8,32,256]{3,2,1,0:T(8,128)S(1)} %copy-done.2, s32[8,32,256]{2,1,0:T(8,128)S(1)} %get-tuple-element.57.w), custom_call_target="tpu_custom_call" | custom-call | bytes 10800000 | tf_op jit(solution)/shard_map/pallas_call | solution.py:560
  19.5 1.6 %collective-permute-start.2 = (f32[3,2,16,256]{3,2,1,0:T(8,128)S(1)}, f32[3,2,16,256]{3,2,1,0:T(8,128)S(1)}, u32[]{:S(2)}, u32[]{:S(2)}) collective-permute-start(f32[3,2,16,256]{3,2,1,0:T(8,128)S(1)} %get-tuple-element.68), channel_id=1, source_target_pairs={{0,1},{1,0},{2,3},{3,2},{4,5},{5,4},{6,7},{7,6},{8,9},{9,8},{10,11... | collective-permute-start | bytes 294920 | tf_op jit(solution)/shard_map/ppermute | solution.py:575
  21.1 3.2 %collective-permute-start.3 = (f32[3,2,16,256]{3,2,1,0:T(8,128)S(1)}, f32[3,2,16,256]{3,2,1,0:T(8,128)S(1)}, u32[]{:S(2)}, u32[]{:S(2)}) collective-permute-start(f32[3,2,16,256]{3,2,1,0:T(8,128)S(1)} %get-tuple-element.69), channel_id=1, source_target_pairs={{1,2},{2,1},{3,4},{4,3},{5,6},{6,5},{9,10},{10,9},{11,12},{12,11},... | collective-permute-start | bytes 294920 | tf_op jit(solution)/shard_map/ppermute | solution.py:575
  24.4 3.6 %shard_map.114 = (f32[3,4,32,256]{3,2,1,0:T(8,128)S(1)}, f32[8,128]{1,0:T(8,128)}) custom-call(f32[216,256]{1,0:T(8,128)S(1)} %collective-permute-done.xa, f32[192,256]{1,0:T(8,128)S(1)} %collective-permute-done.1.xb, f32[3,2,12,48,128]{4,3,2,1,0:T(8,128)S(1)} %copy-done.1, f32[3,2,10,48,128]{4,3,2,1,0:T(8,128)S(1)} %get-tuple-element.61.left_own, ...), custom_call_target="tpu_custom_call" | custom-call | bytes 10800000 | tf_op jit(solution)/shard_map/pallas_call | solution.py:560
  28.0 1.8 %collective-permute-done.3.yb = f32[3,2,16,256]{3,2,1,0:T(8,128)S(1)} collective-permute-done((f32[3,2,16,256]{3,2,1,0:T(8,128)S(1)}, f32[3,2,16,256]{3,2,1,0:T(8,128)S(1)}, u32[]{:S(2)}, u32[]{:S(2)}) %collective-permute-start.3) | collective-permute-done | bytes 98336 | tf_op jit(solution)/shard_map/ppermute | solution.py:575
  30.9 5.6 %collective-permute-start.5 = (f32[192,256]{1,0:T(8,128)S(1)}, f32[192,256]{1,0:T(8,128)S(1)}, u32[]{:S(2)}, u32[]{:S(2)}) collective-permute-start(f32[192,256]{1,0:T(8,128)S(1)} %get-tuple-element.75), channel_id=1, source_target_pairs={{8,16},{16,8},{24,32},{32,24},{40,48},{48,40},{56,64},{64,56},{72,... | collective-permute-start | bytes 589832 | tf_op jit(solution)/shard_map/ppermute | solution.py:575
  36.5 3.6 %shard_map.117 = (f32[3,4,32,256]{3,2,1,0:T(8,128)S(1)}, f32[3,2,10,48,128]{4,3,2,1,0:T(8,128)S(1)}, f32[3,2,10,48,128]{4,3,2,1,0:T(8,128)S(1)}, f32[8,128]{1,0:T(8,128)S(1)}) custom-call(f32[3,2,12,48,128]{4,3,2,1,0:T(8,128)S(1)} %get-tuple-element.71.u.u_own, f32[3,8,32,256]{3,2,1,0:T(8,128)S(1)} %get-tuple-element.72.half, ...), custom_call_target="tpu_custom_call" | custom-call | bytes 10800000 | tf_op jit(solution)/shard_map/pallas_call | solution.py:560
  41.6 1.6 %collective-permute-start.6 = (f32[3,2,16,256]{3,2,1,0:T(8,128)S(1)}, f32[3,2,16,256]{3,2,1,0:T(8,128)S(1)}, u32[]{:S(2)}, u32[]{:S(2)}) collective-permute-start(f32[3,2,16,256]{3,2,1,0:T(8,128)S(1)} %get-tuple-element.83), channel_id=1, source_target_pairs={{0,1},{1,0},{2,3},{3,2},{4,5},{5,4},{6,7},{7,6},{8,9},{9,8},{10,11... | collective-permute-start | bytes 294920 | tf_op jit(solution)/shard_map/ppermute | solution.py:575
  43.2 3.2 %collective-permute-start.7 = (f32[3,2,16,256]{3,2,1,0:T(8,128)S(1)}, f32[3,2,16,256]{3,2,1,0:T(8,128)S(1)}, u32[]{:S(2)}, u32[]{:S(2)}) collective-permute-start(f32[3,2,16,256]{3,2,1,0:T(8,128)S(1)} %get-tuple-element.84), channel_id=1, source_target_pairs={{1,2},{2,1},{3,4},{4,3},{5,6},{6,5},{9,10},{10,9},{11,12},{12,11},... | collective-permute-start | bytes 294920 | tf_op jit(solution)/shard_map/ppermute | solution.py:575
  46.4 3.6 %shard_map.118 = (f32[3,4,32,256]{3,2,1,0:T(8,128)S(1)}, f32[8,128]{1,0:T(8,128)}) custom-call(f32[216,256]{1,0:T(8,128)S(1)} %collective-permute-done.4.xa, f32[192,256]{1,0:T(8,128)S(1)} %collective-permute-done.5.xb, f32[3,2,12,48,128]{4,3,2,1,0:T(8,128)S(1)} %get-tuple-element.71.u.u_own, f32[3,2,10,48,128]{4,3,2,1,0:T(8,128)S(1)} %get-tuple-element.76.left_own, ...), custom_call_target="tpu_custom_call" | custom-call | bytes 10800000 | tf_op jit(solution)/shard_map/pallas_call | solution.py:560
  50.0 1.8 %collective-permute-done.7.yb = f32[3,2,16,256]{3,2,1,0:T(8,128)S(1)} collective-permute-done((f32[3,2,16,256]{3,2,1,0:T(8,128)S(1)}, f32[3,2,16,256]{3,2,1,0:T(8,128)S(1)}, u32[]{:S(2)}, u32[]{:S(2)}) %collective-permute-start.7) | collective-permute-done | bytes 98336 | tf_op jit(solution)/shard_map/ppermute | solution.py:575
  51.8 2.6 %shard_map.120 = (f32[3,2,12,48,128]{4,3,2,1,0:T(8,128)S(1)}, f32[3,8,32,256]{3,2,1,0:T(8,128)S(1)}, f32[10,8,128]{2,1,0:T(8,128)S(1)}, f32[216,256]{1,0:T(8,128...) custom-call(s32[3,2,16]{2,1,0:T(2,128)S(1)} %copy-done.8, ...), custom_call_target="tpu_custom_call" | custom-call | bytes 9000000 | tf_op jit(solution)/shard_map/pallas_call | solution.py:560
  54.6 4.0 %collective-permute-start.9 = (f32[192,256]{1,0:T(8,128)S(1)}, f32[192,256]{1,0:T(8,128)S(1)}, u32[]{:S(2)}, u32[]{:S(2)}) collective-permute-start(f32[192,256]{1,0:T(8,128)S(1)} %get-tuple-element.89), channel_id=1, source_target_pairs={{8,16},{16,8},{24,32},{32,24},{40,48},{48,40},{56,64},{64,56},{72,... | collective-permute-start | bytes 589832 | tf_op jit(solution)/shard_map/ppermute | solution.py:575
  58.5 3.6 %shard_map.121 = (f32[3,4,32,256]{3,2,1,0:T(8,128)S(1)}, f32[3,2,10,48,128]{4,3,2,1,0:T(8,128)S(1)}, f32[3,2,10,48,128]{4,3,2,1,0:T(8,128)S(1)}, f32[8,128]{1,0:T(8,128)S(1)}) custom-call(f32[3,2,12,48,128]{4,3,2,1,0:T(8,128)S(1)} %get-tuple-element.85.u.u_own, f32[3,8,32,256]{3,2,1,0:T(8,128)S(1)} %get-tuple-element.86.half, ...), custom_call_target="tpu_custom_call" | custom-call | bytes 10800000 | tf_op jit(solution)/shard_map/pallas_call | solution.py:560
  62.2 2.9 %collective-permute-done.9.xb = f32[192,256]{1,0:T(8,128)S(1)} collective-permute-done((f32[192,256]{1,0:T(8,128)S(1)}, f32[192,256]{1,0:T(8,128)S(1)}, u32[]{:S(2)}, u32[]{:S(2)}) %collective-permute-start.9) | collective-permute-done | bytes 196640 | tf_op jit(solution)/shard_map/ppermute | solution.py:575
  65.3 3.2 %collective-permute-start.13 = (f32[3,2,16,256]{3,2,1,0:T(8,128)S(1)}, f32[3,2,16,256]{3,2,1,0:T(8,128)S(1)}, u32[]{:S(2)}, u32[]{:S(2)}) collective-permute-start(f32[3,2,16,256]{3,2,1,0:T(8,128)S(1)} %get-tuple-element.98), channel_id=1, source_target_pairs={{1,2},{2,1},{3,4},{4,3},{5,6},{6,5},{9,10},{10,9},{11,12},{12,11},... | collective-permute-start | bytes 294920 | tf_op jit(solution)/shard_map/ppermute | solution.py:575
  68.8 5.2 %collective-permute-done.11.theirs = f32[6,4,128]{2,1,0:T(4,128)S(1)} collective-permute-done((f32[6,4,128]{2,1,0:T(4,128)S(1)}, f32[6,4,128]{2,1,0:T(4,128)S(1)}, u32[]{:S(2)}, u32[]{:S(2)}) %collective-permute-start.11) | collective-permute-done | bytes 12320 | tf_op jit(solution)/shard_map/ppermute | solution.py:584
  74.0 3.0 %shard_map.125 = (f32[3,4,32,256]{3,2,1,0:T(8,128)S(1)}, f32[8,128]{1,0:T(8,128)S(1)}) custom-call(f32[216,256]{1,0:T(8,128)S(1)} %collective-permute-done.8.xa, f32[192,256]{1,0:T(8,128)S(1)} %collective-permute-done.9.xb, f32[3,2,12,48,128]{4,3,2,1,0:T(8,128)S(1)} %get-tuple-element.85.u.u_own, f32[3,2,10,48,128]{4,3,2,1,0:T(8,128)S(1)} %get-tuple-element.90.left_own, ...), custom_call_target="tpu_custom_call" | custom-call | bytes 10800000 | tf_op jit(solution)/shard_map/pallas_call | solution.py:560
  77.1 2.3 %collective-permute-done.14.theirs = f32[6,8,128]{2,1,0:T(8,128)S(1)} collective-permute-done((f32[6,8,128]{2,1,0:T(8,128)S(1)}, f32[6,8,128]{2,1,0:T(8,128)S(1)}, u32[]{:S(2)}, u32[]{:S(2)}) %collective-permute-start.14) | collective-permute-done | bytes 24608 | tf_op jit(solution)/shard_map/ppermute | solution.py:584
  79.4 2.7 %collective-permute-start.15 = (f32[6,16,128]{2,1,0:T(8,128)S(1)}, f32[6,16,128]{2,1,0:T(8,128)S(1)}, u32[]{:S(2)}, u32[]{:S(2)}) collective-permute-start(f32[6,16,128]{2,1,0:T(8,128)S(1)} %shard_map.127.after.ours), channel_id=1, source_target_pairs={{0,2},{1,3},{2,0},{3,1},{4,6},{5,7},{6,4},{7,5},{8,10},{9,11},{10,... | collective-permute-start | bytes 147464 | tf_op jit(solution)/shard_map/ppermute | solution.py:584
  85.1 4.6 %collective-permute-done.16.theirs = f32[6,32,128]{2,1,0:T(8,128)S(1)} collective-permute-done((f32[6,32,128]{2,1,0:T(8,128)S(1)}, f32[6,32,128]{2,1,0:T(8,128)S(1)}, u32[]{:S(2)}, u32[]{:S(2)}) %collective-permute-start.16) | collective-permute-done | bytes 98336 | tf_op jit(solution)/shard_map/ppermute | solution.py:584
  89.8 5.7 %collective-permute-done.17.theirs = f32[6,64,128]{2,1,0:T(8,128)S(1)} collective-permute-done((f32[6,64,128]{2,1,0:T(8,128)S(1)}, f32[6,64,128]{2,1,0:T(8,128)S(1)}, u32[]{:S(2)}, u32[]{:S(2)}) %collective-permute-start.17) | collective-permute-done | bytes 196640 | tf_op jit(solution)/shard_map/ppermute | solution.py:584
  (52 shorter events, 9.2 us)
Async XLA Ops:
  0.6 13.5 %copy-start.3 = (s32[4,8,32,256]{3,2,1,0:T(8,128)S(1)}, s32[4,8,32,256]{3,2,1,0:T(8,128)}, u32[]{:S(2)}) copy-start(s32[4,8,32,256]{3,2,1,0:T(8,128)} %masks.1) | copy-start | bytes 3145732
  7.4 7.0 %copy-start.2 = (f32[3,8,32,256]{3,2,1,0:T(8,128)S(1)}, f32[3,8,32,256]{3,2,1,0:T(8,128)}, u32[]{:S(2)}) copy-start(f32[3,8,32,256]{3,2,1,0:T(8,128)} %get-tuple-element.56.half) | copy-start | bytes 2359300
  7.4 12.1 %collective-permute-start = (f32[216,256]{1,0:T(8,128)}, f32[216,256]{1,0:T(8,128)S(1)}, u32[]{:S(2)}, u32[]{:S(2)}) collective-permute-start(f32[216,256]{1,0:T(8,128)} %get-tuple-element.59), channel_id=1, source_target_pairs={{0,8},{8,0},{16,24},{24,16},{32,40},{40,32},{48,56},{56,48},{64,72... | collective-permute-start | bytes 663560 | tf_op jit(solution)/shard_map/ppermute | solution.py:575
  7.5 12.0 %collective-permute-start.1 = (f32[192,256]{1,0:T(8,128)}, f32[192,256]{1,0:T(8,128)S(1)}, u32[]{:S(2)}, u32[]{:S(2)}) collective-permute-start(f32[192,256]{1,0:T(8,128)} %get-tuple-element.60), channel_id=1, source_target_pairs={{8,16},{16,8},{24,32},{32,24},{40,48},{48,40},{56,64},{64,56},{72,... | collective-permute-start | bytes 589832 | tf_op jit(solution)/shard_map/ppermute | solution.py:575
  14.2 5.3 %copy-start.4 = (f32[3,2,8,256]{3,2,1,0:T(8,128)S(1)}, f32[3,2,8,256]{3,2,1,0:T(8,128)}, u32[]{:S(2)}) copy-start(f32[3,2,8,256]{3,2,1,0:T(8,128)} %get-tuple-element.65.ya_own) | copy-start | bytes 147460
  15.8 8.5 %copy-start.1 = (f32[3,2,12,48,128]{4,3,2,1,0:T(8,128)S(1)}, f32[3,2,12,48,128]{4,3,2,1,0:T(8,128)}, u32[]{:S(2)}) copy-start(f32[3,2,12,48,128]{4,3,2,1,0:T(8,128)} %get-tuple-element.55.u.u_own) | copy-start | bytes 5308420
  19.5 8.4 %collective-permute-start.2 = (f32[3,2,16,256]{3,2,1,0:T(8,128)S(1)}, f32[3,2,16,256]{3,2,1,0:T(8,128)S(1)}, u32[]{:S(2)}, u32[]{:S(2)}) collective-permute-start(f32[3,2,16,256]{3,2,1,0:T(8,128)S(1)} %get-tuple-element.68), channel_id=1, source_target_pairs={{0,1},{1,0},{2,3},{3,2},{4,5},{5,4},{6,7},{7,6},{8,9},{9,8},{10,11... | collective-permute-start | bytes 294920 | tf_op jit(solution)/shard_map/ppermute | solution.py:575
  21.1 8.6 %collective-permute-start.3 = (f32[3,2,16,256]{3,2,1,0:T(8,128)S(1)}, f32[3,2,16,256]{3,2,1,0:T(8,128)S(1)}, u32[]{:S(2)}, u32[]{:S(2)}) collective-permute-start(f32[3,2,16,256]{3,2,1,0:T(8,128)S(1)} %get-tuple-element.69), channel_id=1, source_target_pairs={{1,2},{2,1},{3,4},{4,3},{5,6},{6,5},{9,10},{10,9},{11,12},{12,11},... | collective-permute-start | bytes 294920 | tf_op jit(solution)/shard_map/ppermute | solution.py:575
  24.4 5.4 %copy-start.8 = (s32[3,2,16]{2,1,0:T(2,128)S(1)}, s32[3,2,16]{2,1,0:T(2,128)}, u32[]{:S(2)}) copy-start(s32[3,2,16]{2,1,0:T(2,128)} %pairs.5) | copy-start | bytes 1156
  30.8 10.7 %collective-permute-start.4 = (f32[216,256]{1,0:T(8,128)S(1)}, f32[216,256]{1,0:T(8,128)S(1)}, u32[]{:S(2)}, u32[]{:S(2)}) collective-permute-start(f32[216,256]{1,0:T(8,128)S(1)} %get-tuple-element.74), channel_id=1, source_target_pairs={{0,8},{8,0},{16,24},{24,16},{32,40},{40,32},{48,56},{56,48},{64,72... | collective-permute-start | bytes 663560 | tf_op jit(solution)/shard_map/ppermute | solution.py:575
  30.9 10.6 %collective-permute-start.5 = (f32[192,256]{1,0:T(8,128)S(1)}, f32[192,256]{1,0:T(8,128)S(1)}, u32[]{:S(2)}, u32[]{:S(2)}) collective-permute-start(f32[192,256]{1,0:T(8,128)S(1)} %get-tuple-element.75), channel_id=1, source_target_pairs={{8,16},{16,8},{24,32},{32,24},{40,48},{48,40},{56,64},{64,56},{72,... | collective-permute-start | bytes 589832 | tf_op jit(solution)/shard_map/ppermute | solution.py:575
  41.6 8.5 %collective-permute-start.6 = (f32[3,2,16,256]{3,2,1,0:T(8,128)S(1)}, f32[3,2,16,256]{3,2,1,0:T(8,128)S(1)}, u32[]{:S(2)}, u32[]{:S(2)}) collective-permute-start(f32[3,2,16,256]{3,2,1,0:T(8,128)S(1)} %get-tuple-element.83), channel_id=1, source_target_pairs={{0,1},{1,0},{2,3},{3,2},{4,5},{5,4},{6,7},{7,6},{8,9},{9,8},{10,11... | collective-permute-start | bytes 294920 | tf_op jit(solution)/shard_map/ppermute | solution.py:575
  43.2 8.6 %collective-permute-start.7 = (f32[3,2,16,256]{3,2,1,0:T(8,128)S(1)}, f32[3,2,16,256]{3,2,1,0:T(8,128)S(1)}, u32[]{:S(2)}, u32[]{:S(2)}) collective-permute-start(f32[3,2,16,256]{3,2,1,0:T(8,128)S(1)} %get-tuple-element.84), channel_id=1, source_target_pairs={{1,2},{2,1},{3,4},{4,3},{5,6},{6,5},{9,10},{10,9},{11,12},{12,11},... | collective-permute-start | bytes 294920 | tf_op jit(solution)/shard_map/ppermute | solution.py:575
  54.5 7.7 %collective-permute-start.8 = (f32[216,256]{1,0:T(8,128)S(1)}, f32[216,256]{1,0:T(8,128)S(1)}, u32[]{:S(2)}, u32[]{:S(2)}) collective-permute-start(f32[216,256]{1,0:T(8,128)S(1)} %get-tuple-element.88), channel_id=1, source_target_pairs={{0,8},{8,0},{16,24},{24,16},{32,40},{40,32},{48,56},{56,48},{64,72... | collective-permute-start | bytes 663560 | tf_op jit(solution)/shard_map/ppermute | solution.py:575
  54.6 10.6 %collective-permute-start.9 = (f32[192,256]{1,0:T(8,128)S(1)}, f32[192,256]{1,0:T(8,128)S(1)}, u32[]{:S(2)}, u32[]{:S(2)}) collective-permute-start(f32[192,256]{1,0:T(8,128)S(1)} %get-tuple-element.89), channel_id=1, source_target_pairs={{8,16},{16,8},{24,32},{32,24},{40,48},{48,40},{56,64},{64,56},{72,... | collective-permute-start | bytes 589832 | tf_op jit(solution)/shard_map/ppermute | solution.py:575
  62.1 6.4 %collective-permute-start.10 = (f32[3,8,128]{2,1,0:T(8,128)S(1)}, f32[3,8,128]{2,1,0:T(8,128)S(1)}, u32[]{:S(2)}, u32[]{:S(2)}) collective-permute-start(f32[3,8,128]{2,1,0:T(8,128)S(1)} %shard_map.122.ours), channel_id=1, source_target_pairs={{0,1},{1,0},{2,3},{3,2},{4,5},{5,4},{6,7},{7,6},{8,9},{9,8},{10,11... | collective-permute-start | bytes 36872 | tf_op jit(solution)/shard_map/ppermute | solution.py:575
  65.2 16.9 %collective-permute-start.12 = (f32[3,2,16,256]{3,2,1,0:T(8,128)S(1)}, f32[3,2,16,256]{3,2,1,0:T(8,128)S(1)}, u32[]{:S(2)}, u32[]{:S(2)}) collective-permute-start(f32[3,2,16,256]{3,2,1,0:T(8,128)S(1)} %get-tuple-element.97), channel_id=1, source_target_pairs={{0,1},{1,0},{2,3},{3,2},{4,5},{5,4},{6,7},{7,6},{8,9},{9,8},{10,11... | collective-permute-start | bytes 294920 | tf_op jit(solution)/shard_map/ppermute | solution.py:575
  65.3 16.8 %collective-permute-start.13 = (f32[3,2,16,256]{3,2,1,0:T(8,128)S(1)}, f32[3,2,16,256]{3,2,1,0:T(8,128)S(1)}, u32[]{:S(2)}, u32[]{:S(2)}) collective-permute-start(f32[3,2,16,256]{3,2,1,0:T(8,128)S(1)} %get-tuple-element.98), channel_id=1, source_target_pairs={{1,2},{2,1},{3,4},{4,3},{5,6},{6,5},{9,10},{10,9},{11,12},{12,11},... | collective-permute-start | bytes 294920 | tf_op jit(solution)/shard_map/ppermute | solution.py:575
  68.6 5.5 %collective-permute-start.11 = (f32[6,4,128]{2,1,0:T(4,128)S(1)}, f32[6,4,128]{2,1,0:T(4,128)S(1)}, u32[]{:S(2)}, u32[]{:S(2)}) collective-permute-start(f32[6,4,128]{2,1,0:T(4,128)S(1)} %shard_map.123.ours), channel_id=1, source_target_pairs={{0,64},{8,72},{16,80},{24,88},{32,96},{40,104},{48,112},{56,120},{... | collective-permute-start | bytes 36872 | tf_op jit(solution)/shard_map/ppermute | solution.py:584
  74.0 5.3 %collective-permute-start.14 = (f32[6,8,128]{2,1,0:T(8,128)S(1)}, f32[6,8,128]{2,1,0:T(8,128)S(1)}, u32[]{:S(2)}, u32[]{:S(2)}) collective-permute-start(f32[6,8,128]{2,1,0:T(8,128)S(1)} %shard_map.124.after.ours), channel_id=1, source_target_pairs={{0,32},{8,40},{16,48},{24,56},{32,0},{40,8},{48,16},{56,24},{64,96... | collective-permute-start | bytes 73736 | tf_op jit(solution)/shard_map/ppermute | solution.py:584
  79.4 5.6 %collective-permute-start.15 = (f32[6,16,128]{2,1,0:T(8,128)S(1)}, f32[6,16,128]{2,1,0:T(8,128)S(1)}, u32[]{:S(2)}, u32[]{:S(2)}) collective-permute-start(f32[6,16,128]{2,1,0:T(8,128)S(1)} %shard_map.127.after.ours), channel_id=1, source_target_pairs={{0,2},{1,3},{2,0},{3,1},{4,6},{5,7},{6,4},{7,5},{8,10},{9,11},{10,... | collective-permute-start | bytes 147464 | tf_op jit(solution)/shard_map/ppermute | solution.py:584
  82.1 13.3 %copy-start.7 = (f32[128,128]{1,0:T(8,128)S(1)}, f32[128,128]{1,0:T(8,128)}, u32[]{:S(2)}) copy-start(f32[128,128]{1,0:T(8,128)} %get-tuple-element.102.perm) | copy-start | bytes 196612
  85.0 4.7 %collective-permute-start.16 = (f32[6,32,128]{2,1,0:T(8,128)S(1)}, f32[6,32,128]{2,1,0:T(8,128)S(1)}, u32[]{:S(2)}, u32[]{:S(2)}) collective-permute-start(f32[6,32,128]{2,1,0:T(8,128)S(1)} %shard_map.129.ours), channel_id=1, source_target_pairs={{0,4},{1,5},{2,6},{3,7},{4,0},{5,1},{6,2},{7,3},{8,12},{9,13},{10,... | collective-permute-start | bytes 294920 | tf_op jit(solution)/shard_map/ppermute | solution.py:584
  89.7 5.8 %collective-permute-start.17 = (f32[6,64,128]{2,1,0:T(8,128)S(1)}, f32[6,64,128]{2,1,0:T(8,128)S(1)}, u32[]{:S(2)}, u32[]{:S(2)}) collective-permute-start(f32[6,64,128]{2,1,0:T(8,128)S(1)} %shard_map.130.ours), channel_id=1, source_target_pairs={{0,16},{8,24},{16,0},{24,8},{32,48},{40,56},{48,32},{56,40},{64,80... | collective-permute-start | bytes 589832 | tf_op jit(solution)/shard_map/ppermute | solution.py:584
  (3 other events, 12.0 us)

commit v3 on v2

--- a/solution.py
+++ b/solution.py
@@ -341,6 +341,16 @@
     lax.fori_loop(2, CX + 2, shifted, 0)
 
 
+def turn_kernel(u, left, right, token):
+    turned_layers(u, left, right)
+    token[...] = left[0, 0, 1, LO : LO + 8, :]
+
+
+def late_inner_kernel(scale, u, left, right, half, w, after, half_out, token):
+    advance(scale, u, left, right, w, half, half_out, 2, 0, CX - 4)
+    token[...] = half_out[0, 0, 0:8, 0:128]
+
+
 def inner_kernel(scale, u, half, w, half_out, left, right, token):
     turned_layers(u, left, right)
     advance(scale, u, left, right, w, half, half_out, 2, 0, CX - 4)
@@ -569,9 +579,10 @@
 
 
 def swap(value, axis, offset):
+    count = lax.axis_size(axis)
     pairs = []
-    for i in range(offset, lax.axis_size(axis) - 1, 2):
-        pairs += [(i, i + 1), (i + 1, i)]
+    for i in range(offset, count, 2):
+        pairs += [(i, (i + 1) % count), ((i + 1) % count, i)]
     return lax.ppermute(value, axis, pairs)
 
 
@@ -589,12 +600,13 @@
 def per_device(u, v, a, masks, proj_pos, proj_vel, proj_acc, pairs):
     pp, pv, pa = [jnp.transpose(p, (1, 0, 2)) for p in (proj_pos, proj_vel, proj_acc)]
     blocks = pp.shape[1]
+    u, v, a, pp, pv, pa = [pltpu.with_memory_space_constraint(x, pltpu.HBM) for x in (u, v, a, pp, pv, pa)]
     u, half, pst, perm, *edges = call(
         begin_kernel,
         (pairs, u, v, a, pp, pv, pa),
         [PADDED, STATE, PST, jax.ShapeDtypeStruct((blocks, blocks), F32), XA, XB, YE, YE],
         ins=[SMEM] + [HBM] * 6,
-        limit=60,
+        limit=40,
         scratch=(
             PLACES,
             pltpu.VMEM((3, *STATE.shape), F32),
@@ -612,14 +624,22 @@
         if last:
             (ours,) = call(pair_kernel, (xa, pst), [PAIR], us=0.1)
             theirs = swap(ours, "split", 0)
-        inner, left, right, token = call(
-            functools.partial(inner_kernel, scale), (u, half, words), [HALVES, SIDE, SIDE, TOKEN], us=3.6
-        )
-        ya, yb = call(corner_kernel, (ya_own, yb_own, xa, xb, pst, token), [YA, YA], us=0.1)
+            left, right, token = call(turn_kernel, (u,), [SIDE, SIDE, TOKEN])
+            (gathered,) = call(state_kernel, (ours, theirs, pst, token), [rows_of(GROUP)], us=0.1)
+            inner, token = call(
+                functools.partial(late_inner_kernel, scale),
+                (u, left, right, half, words, gathered),
+                [HALVES, TOKEN],
+                us=2.6,
+            )
+        else:
+            inner, left, right, token = call(
+                functools.partial(inner_kernel, scale), (u, half, words), [HALVES, SIDE, SIDE, TOKEN], us=3.6
+            )
+        after = gathered if last else token
+        ya, yb = call(corner_kernel, (ya_own, yb_own, xa, xb, pst, after), [YA, YA], us=0.1)
         ya, yb = swap(ya, "split", 0), swap(yb, "split", 1)
-        after = token
         if last:
-            (gathered,) = call(state_kernel, (ours, theirs, pst, token), [rows_of(GROUP)], us=0.1)
             gathered = after = share_round(gathered, 0, token)
         edge, token = call(
             functools.partial(edge_kernel, scale),

time: 97.8 us -> 86.6 us (0.89)
  the two profiles are of different devices: /device:TPU:24 before, /device:TPU:0 now
where the time goes in v3:
time: 86.6 us; the launch traced here: 86.2 us
  Pallas kernels  31.3 us (36%)
  starting transfers between devices  29.8 us (34%)
  waiting for transfers between devices  23.5 us (27%)
    pallas_call x23, Pallas kernels, call(): pl.pallas_call(kernel, out_shape=outputs, in_specs=ins or [SMEM] * scalar...  31.3 us
    ppermute x13, starting transfers between devices, swap(): return lax.ppermute(value, axis, pairs)  24.8 us
    ppermute x5, waiting for transfers between devices, share_round(): lax.ppermute(gathered, axis, [(i, i ^ bit) for i in range(lax.axis_size(a...  14.4 us
    ppermute x13, waiting for transfers between devices, swap(): return lax.ppermute(value, axis, pairs)  9.09 us
    ppermute x5, starting transfers between devices, share_round(): lax.ppermute(gathered, axis, [(i, i ^ bit) for i in range(lax.axis_size(a...  5.06 us
  transfers between devices with their start and end apart: 18, of which 9 were waited for; matrix products, arithmetic and copies ran while one was open for 0% of the time, Pallas kernels for 26%

profile of v3, /device:TPU:0, one launch (start us, length us, event | category | flops | bytes accessed | tf_op | source)
XLA Modules:
  0.0 86.2 jit_solution(12089543403348275227)
XLA Ops:
  1.3 3.3 %shard_map.111 = (f32[3,2,12,48,128]{4,3,2,1,0:T(8,128)S(1)}, f32[3,8,32,256]{3,2,1,0:T(8,128)S(1)}, f32[10,8,128]{2,1,0:T(8,128)S(1)}, f32[128,128]{1,0:T(8,128...) custom-call(s32[3,2,16]{2,1,0:T(2,128)S(1)} %copy-done.1, ...), custom_call_target="tpu_custom_call" | custom-call | bytes 3000000 | tf_op jit(solution)/shard_map/pallas_call | solution.py:570
  5.3 7.8 %collective-permute-start.1 = (f32[192,256]{1,0:T(8,128)S(1)}, f32[192,256]{1,0:T(8,128)S(1)}, u32[]{:S(2)}, u32[]{:S(2)}) collective-permute-start(f32[192,256]{1,0:T(8,128)S(1)} %get-tuple-element.61), channel_id=1, source_target_pairs={{8,16},{16,8},{24,32},{32,24},{40,48},{48,40},{56,64},{64,56},{72,... | collective-permute-start | bytes 589832 | tf_op jit(solution)/shard_map/ppermute | solution.py:586
  13.2 3.6 %shard_map.113 = (f32[3,4,32,256]{3,2,1,0:T(8,128)S(1)}, f32[3,2,10,48,128]{4,3,2,1,0:T(8,128)S(1)}, f32[3,2,10,48,128]{4,3,2,1,0:T(8,128)S(1)}, f32[8,128]{1,0:T(8,128)S(1)}) custom-call(f32[3,2,12,48,128]{4,3,2,1,0:T(8,128)S(1)} %get-tuple-element.56.u.u_own, f32[3,8,32,256]{3,2,1,0:T(8,128)S(1)} %get-tuple-element.57.half, ...), custom_call_target="tpu_custom_call" | custom-call | bytes 10800000 | tf_op jit(solution)/shard_map/pallas_call | solution.py:570
  16.8 2.5 %collective-permute-start.2 = (f32[3,2,16,256]{3,2,1,0:T(8,128)S(1)}, f32[3,2,16,256]{3,2,1,0:T(8,128)S(1)}, u32[]{:S(2)}, u32[]{:S(2)}) collective-permute-start(f32[3,2,16,256]{3,2,1,0:T(8,128)S(1)} %get-tuple-element.69), channel_id=1, source_target_pairs={{0,1},{1,0},{2,3},{3,2},{4,5},{5,4},{6,7},{7,6},{8,9},{9,8},{10,11... | collective-permute-start | bytes 294920 | tf_op jit(solution)/shard_map/ppermute | solution.py:586
  20.6 3.6 %shard_map.114 = (f32[3,4,32,256]{3,2,1,0:T(8,128)S(1)}, f32[8,128]{1,0:T(8,128)}) custom-call(f32[216,256]{1,0:T(8,128)S(1)} %collective-permute-done.xa, f32[192,256]{1,0:T(8,128)S(1)} %collective-permute-done.1.xb, f32[3,2,12,48,128]{4,3,2,1,0:T(8,128)S(1)} %get-tuple-element.56.u.u_own, f32[3,2,10,48,128]{4,3,2,1,0:T(8,128)S(1)} %get-tuple-element.62.left_own, ...), custom_call_target="tpu_custom_call" | custom-call | bytes 10800000 | tf_op jit(solution)/shard_map/pallas_call | solution.py:570
  24.2 1.8 %collective-permute-done.3.yb = f32[3,2,16,256]{3,2,1,0:T(8,128)S(1)} collective-permute-done((f32[3,2,16,256]{3,2,1,0:T(8,128)S(1)}, f32[3,2,16,256]{3,2,1,0:T(8,128)S(1)}, u32[]{:S(2)}, u32[]{:S(2)}) %collective-permute-start.3) | collective-permute-done | bytes 98336 | tf_op jit(solution)/shard_map/ppermute | solution.py:586
  27.2 5.6 %collective-permute-start.5 = (f32[192,256]{1,0:T(8,128)S(1)}, f32[192,256]{1,0:T(8,128)S(1)}, u32[]{:S(2)}, u32[]{:S(2)}) collective-permute-start(f32[192,256]{1,0:T(8,128)S(1)} %get-tuple-element.76), channel_id=1, source_target_pairs={{8,16},{16,8},{24,32},{32,24},{40,48},{48,40},{56,64},{64,56},{72,... | collective-permute-start | bytes 589832 | tf_op jit(solution)/shard_map/ppermute | solution.py:586
  32.8 3.6 %shard_map.117 = (f32[3,4,32,256]{3,2,1,0:T(8,128)S(1)}, f32[3,2,10,48,128]{4,3,2,1,0:T(8,128)S(1)}, f32[3,2,10,48,128]{4,3,2,1,0:T(8,128)S(1)}, f32[8,128]{1,0:T(8,128)S(1)}) custom-call(f32[3,2,12,48,128]{4,3,2,1,0:T(8,128)S(1)} %get-tuple-element.72.u.u_own, f32[3,8,32,256]{3,2,1,0:T(8,128)S(1)} %get-tuple-element.73.half, ...), custom_call_target="tpu_custom_call" | custom-call | bytes 10800000 | tf_op jit(solution)/shard_map/pallas_call | solution.py:570
  36.5 2.0 %collective-permute-start.6 = (f32[3,2,16,256]{3,2,1,0:T(8,128)S(1)}, f32[3,2,16,256]{3,2,1,0:T(8,128)S(1)}, u32[]{:S(2)}, u32[]{:S(2)}) collective-permute-start(f32[3,2,16,256]{3,2,1,0:T(8,128)S(1)} %get-tuple-element.84), channel_id=1, source_target_pairs={{0,1},{1,0},{2,3},{3,2},{4,5},{5,4},{6,7},{7,6},{8,9},{9,8},{10,11... | collective-permute-start | bytes 294920 | tf_op jit(solution)/shard_map/ppermute | solution.py:586
  38.5 3.6 %shard_map.118 = (f32[3,4,32,256]{3,2,1,0:T(8,128)S(1)}, f32[8,128]{1,0:T(8,128)}) custom-call(f32[216,256]{1,0:T(8,128)S(1)} %collective-permute-done.4.xa, f32[192,256]{1,0:T(8,128)S(1)} %collective-permute-done.5.xb, f32[3,2,12,48,128]{4,3,2,1,0:T(8,128)S(1)} %get-tuple-element.72.u.u_own, f32[3,2,10,48,128]{4,3,2,1,0:T(8,128)S(1)} %get-tuple-element.77.left_own, ...), custom_call_target="tpu_custom_call" | custom-call | bytes 10800000 | tf_op jit(solution)/shard_map/pallas_call | solution.py:570
  42.1 3.1 %collective-permute-done.7.yb = f32[3,2,16,256]{3,2,1,0:T(8,128)S(1)} collective-permute-done((f32[3,2,16,256]{3,2,1,0:T(8,128)S(1)}, f32[3,2,16,256]{3,2,1,0:T(8,128)S(1)}, u32[]{:S(2)}, u32[]{:S(2)}) %collective-permute-start.7) | collective-permute-done | bytes 98336 | tf_op jit(solution)/shard_map/ppermute | solution.py:586
  45.3 3.1 %shard_map.120 = (f32[3,2,12,48,128]{4,3,2,1,0:T(8,128)S(1)}, f32[3,8,32,256]{3,2,1,0:T(8,128)S(1)}, f32[10,8,128]{2,1,0:T(8,128)S(1)}, f32[216,256]{1,0:T(8,128...) custom-call(s32[3,2,16]{2,1,0:T(2,128)S(1)} %copy-done.1, ...), custom_call_target="tpu_custom_call" | custom-call | bytes 9000000 | tf_op jit(solution)/shard_map/pallas_call | solution.py:570
  48.4 3.7 %collective-permute-start.10 = (f32[192,256]{1,0:T(8,128)S(1)}, f32[192,256]{1,0:T(8,128)S(1)}, u32[]{:S(2)}, u32[]{:S(2)}) collective-permute-start(f32[192,256]{1,0:T(8,128)S(1)} %get-tuple-element.94), channel_id=1, source_target_pairs={{8,16},{16,8},{24,32},{32,24},{40,48},{48,40},{56,64},{64,56},{72,... | collective-permute-start | bytes 589832 | tf_op jit(solution)/shard_map/ppermute | solution.py:586
  53.1 2.7 %collective-permute-done.9.theirs = f32[3,8,128]{2,1,0:T(8,128)S(1)} collective-permute-done((f32[3,8,128]{2,1,0:T(8,128)S(1)}, f32[3,8,128]{2,1,0:T(8,128)S(1)}, u32[]{:S(2)}, u32[]{:S(2)}) %collective-permute-start.9) | collective-permute-done | bytes 12320 | tf_op jit(solution)/shard_map/ppermute | solution.py:586
  55.8 1.4 %collective-permute-done.10.xb = f32[192,256]{1,0:T(8,128)S(1)} collective-permute-done((f32[192,256]{1,0:T(8,128)S(1)}, f32[192,256]{1,0:T(8,128)S(1)}, u32[]{:S(2)}, u32[]{:S(2)}) %collective-permute-start.10) | collective-permute-done | bytes 196640 | tf_op jit(solution)/shard_map/ppermute | solution.py:586
  58.3 2.6 %shard_map.124 = (f32[3,4,32,256]{3,2,1,0:T(8,128)S(1)}, f32[8,128]{1,0:T(8,128)S(1)}) custom-call(f32[3,2,12,48,128]{4,3,2,1,0:T(8,128)S(1)} %get-tuple-element.86.u.u_own, f32[3,2,10,48,128]{4,3,2,1,0:T(8,128)S(1)} %get-tuple-element.87.left.left_own, f32[3,2,10,48,128]{4,3,2,1,0:T(8,128)S(1)} %get-tuple-element.88.right.right_own, ...), custom_call_target="tpu_custom_call" | custom-call | bytes 7800000 | tf_op jit(solution)/shard_map/pallas_call | solution.py:570
  60.9 2.5 %collective-permute-done.11.theirs = f32[6,4,128]{2,1,0:T(4,128)S(1)} collective-permute-done((f32[6,4,128]{2,1,0:T(4,128)S(1)}, f32[6,4,128]{2,1,0:T(4,128)S(1)}, u32[]{:S(2)}, u32[]{:S(2)}) %collective-permute-start.11) | collective-permute-done | bytes 12320 | tf_op jit(solution)/shard_map/ppermute | solution.py:595
  63.5 3.0 %shard_map.126 = (f32[3,4,32,256]{3,2,1,0:T(8,128)S(1)}, f32[8,128]{1,0:T(8,128)S(1)}) custom-call(f32[216,256]{1,0:T(8,128)S(1)} %collective-permute-done.8.xa, f32[192,256]{1,0:T(8,128)S(1)} %collective-permute-done.10.xb, f32[3,2,12,48,128]{4,3,2,1,0:T(8,128)S(1)} %get-tuple-element.86.u.u_own, ...), custom_call_target="tpu_custom_call" | custom-call | bytes 10800000 | tf_op jit(solution)/shard_map/pallas_call | solution.py:570
  66.5 2.3 %collective-permute-done.14.theirs = f32[6,8,128]{2,1,0:T(8,128)S(1)} collective-permute-done((f32[6,8,128]{2,1,0:T(8,128)S(1)}, f32[6,8,128]{2,1,0:T(8,128)S(1)}, u32[]{:S(2)}, u32[]{:S(2)}) %collective-permute-start.14) | collective-permute-done | bytes 24608 | tf_op jit(solution)/shard_map/ppermute | solution.py:595
  68.8 3.3 %collective-permute-start.15 = (f32[6,16,128]{2,1,0:T(8,128)S(1)}, f32[6,16,128]{2,1,0:T(8,128)S(1)}, u32[]{:S(2)}, u32[]{:S(2)}) collective-permute-start(f32[6,16,128]{2,1,0:T(8,128)S(1)} %shard_map.128.after.ours), channel_id=1, source_target_pairs={{0,2},{1,3},{2,0},{3,1},{4,6},{5,7},{6,4},{7,5},{8,10},{9,11},{10,... | collective-permute-start | bytes 147464 | tf_op jit(solution)/shard_map/ppermute | solution.py:595
  72.2 1.4 %shard_map.129 = (f32[3,8,32,256]{3,2,1,0:T(8,128)}, f32[3,8,32,256]{3,2,1,0:T(8,128)}, f32[8,128]{1,0:T(8,128)S(1)}) custom-call(f32[3,2,12,48,128]{4,3,2,1,0:T(8,128)S(1)} %get-tuple-element.86.u.u_own, f32[3,4,32,256]{3,2,1,0:T(8,128)S(1)} %get-tuple-element.93.inner, f32[3,4,32,256]{3,2,1,0:T(8,128)S(1)} %get-tuple-element.96.edge, ...), custom_call_target="tpu_custom_call" | custom-call | bytes 4200000 | tf_op jit(solution)/shard_map/pallas_call | solution.py:570
  74.4 1.6 %collective-permute-start.16 = (f32[6,32,128]{2,1,0:T(8,128)S(1)}, f32[6,32,128]{2,1,0:T(8,128)S(1)}, u32[]{:S(2)}, u32[]{:S(2)}) collective-permute-start(f32[6,32,128]{2,1,0:T(8,128)S(1)} %shard_map.130.ours), channel_id=1, source_target_pairs={{0,4},{1,5},{2,6},{3,7},{4,0},{5,1},{6,2},{7,3},{8,12},{9,13},{10,... | collective-permute-start | bytes 294920 | tf_op jit(solution)/shard_map/ppermute | solution.py:595
  76.1 3.1 %collective-permute-done.16.theirs = f32[6,32,128]{2,1,0:T(8,128)S(1)} collective-permute-done((f32[6,32,128]{2,1,0:T(8,128)S(1)}, f32[6,32,128]{2,1,0:T(8,128)S(1)}, u32[]{:S(2)}, u32[]{:S(2)}) %collective-permute-start.16) | collective-permute-done | bytes 98336 | tf_op jit(solution)/shard_map/ppermute | solution.py:595
  79.2 5.7 %collective-permute-done.17.theirs = f32[6,64,128]{2,1,0:T(8,128)S(1)} collective-permute-done((f32[6,64,128]{2,1,0:T(8,128)S(1)}, f32[6,64,128]{2,1,0:T(8,128)S(1)}, u32[]{:S(2)}, u32[]{:S(2)}) %collective-permute-start.17) | collective-permute-done | bytes 196640 | tf_op jit(solution)/shard_map/ppermute | solution.py:595
  (39 shorter events, 8.4 us)
Async XLA Ops:
  0.6 0.7 copy-start.1
  1.3 11.7 %copy-start = (s32[4,8,32,256]{3,2,1,0:T(8,128)S(1)}, s32[4,8,32,256]{3,2,1,0:T(8,128)}, u32[]{:S(2)}) copy-start(s32[4,8,32,256]{3,2,1,0:T(8,128)} %masks.1) | copy-start | bytes 3145732
  4.6 12.2 %collective-permute-start = (f32[216,256]{1,0:T(8,128)S(1)}, f32[216,256]{1,0:T(8,128)S(1)}, u32[]{:S(2)}, u32[]{:S(2)}) collective-permute-start(f32[216,256]{1,0:T(8,128)S(1)} %get-tuple-element.60), channel_id=1, source_target_pairs={{0,8},{8,0},{16,24},{24,16},{32,40},{40,32},{48,56},{56,48},{64,72... | collective-permute-start | bytes 663560 | tf_op jit(solution)/shard_map/ppermute | solution.py:586
  5.3 11.5 %collective-permute-start.1 = (f32[192,256]{1,0:T(8,128)S(1)}, f32[192,256]{1,0:T(8,128)S(1)}, u32[]{:S(2)}, u32[]{:S(2)}) collective-permute-start(f32[192,256]{1,0:T(8,128)S(1)} %get-tuple-element.61), channel_id=1, source_target_pairs={{8,16},{16,8},{24,32},{32,24},{40,48},{48,40},{56,64},{64,56},{72,... | collective-permute-start | bytes 589832 | tf_op jit(solution)/shard_map/ppermute | solution.py:586
  16.8 7.4 %collective-permute-start.2 = (f32[3,2,16,256]{3,2,1,0:T(8,128)S(1)}, f32[3,2,16,256]{3,2,1,0:T(8,128)S(1)}, u32[]{:S(2)}, u32[]{:S(2)}) collective-permute-start(f32[3,2,16,256]{3,2,1,0:T(8,128)S(1)} %get-tuple-element.69), channel_id=1, source_target_pairs={{0,1},{1,0},{2,3},{3,2},{4,5},{5,4},{6,7},{7,6},{8,9},{9,8},{10,11... | collective-permute-start | bytes 294920 | tf_op jit(solution)/shard_map/ppermute | solution.py:586
  19.3 6.7 %collective-permute-start.3 = (f32[3,2,16,256]{3,2,1,0:T(8,128)S(1)}, f32[3,2,16,256]{3,2,1,0:T(8,128)S(1)}, u32[]{:S(2)}, u32[]{:S(2)}) collective-permute-start(f32[3,2,16,256]{3,2,1,0:T(8,128)S(1)} %get-tuple-element.70), channel_id=1, source_target_pairs={{1,2},{2,1},{3,4},{4,3},{5,6},{6,5},{7,0},{0,7},{9,10},{10,9},{11,... | collective-permute-start | bytes 294920 | tf_op jit(solution)/shard_map/ppermute | solution.py:586
  27.1 9.4 %collective-permute-start.4 = (f32[216,256]{1,0:T(8,128)S(1)}, f32[216,256]{1,0:T(8,128)S(1)}, u32[]{:S(2)}, u32[]{:S(2)}) collective-permute-start(f32[216,256]{1,0:T(8,128)S(1)} %get-tuple-element.75), channel_id=1, source_target_pairs={{0,8},{8,0},{16,24},{24,16},{32,40},{40,32},{48,56},{56,48},{64,72... | collective-permute-start | bytes 663560 | tf_op jit(solution)/shard_map/ppermute | solution.py:586
  27.2 9.3 %collective-permute-start.5 = (f32[192,256]{1,0:T(8,128)S(1)}, f32[192,256]{1,0:T(8,128)S(1)}, u32[]{:S(2)}, u32[]{:S(2)}) collective-permute-start(f32[192,256]{1,0:T(8,128)S(1)} %get-tuple-element.76), channel_id=1, source_target_pairs={{8,16},{16,8},{24,32},{32,24},{40,48},{48,40},{56,64},{64,56},{72,... | collective-permute-start | bytes 589832 | tf_op jit(solution)/shard_map/ppermute | solution.py:586
  36.5 5.6 %collective-permute-start.6 = (f32[3,2,16,256]{3,2,1,0:T(8,128)S(1)}, f32[3,2,16,256]{3,2,1,0:T(8,128)S(1)}, u32[]{:S(2)}, u32[]{:S(2)}) collective-permute-start(f32[3,2,16,256]{3,2,1,0:T(8,128)S(1)} %get-tuple-element.84), channel_id=1, source_target_pairs={{0,1},{1,0},{2,3},{3,2},{4,5},{5,4},{6,7},{7,6},{8,9},{9,8},{10,11... | collective-permute-start | bytes 294920 | tf_op jit(solution)/shard_map/ppermute | solution.py:586
  38.5 6.7 %collective-permute-start.7 = (f32[3,2,16,256]{3,2,1,0:T(8,128)S(1)}, f32[3,2,16,256]{3,2,1,0:T(8,128)S(1)}, u32[]{:S(2)}, u32[]{:S(2)}) collective-permute-start(f32[3,2,16,256]{3,2,1,0:T(8,128)S(1)} %get-tuple-element.85), channel_id=1, source_target_pairs={{1,2},{2,1},{3,4},{4,3},{5,6},{6,5},{7,0},{0,7},{9,10},{10,9},{11,... | collective-permute-start | bytes 294920 | tf_op jit(solution)/shard_map/ppermute | solution.py:586
  48.3 3.8 %collective-permute-start.8 = (f32[216,256]{1,0:T(8,128)S(1)}, f32[216,256]{1,0:T(8,128)S(1)}, u32[]{:S(2)}, u32[]{:S(2)}) collective-permute-start(f32[216,256]{1,0:T(8,128)S(1)} %get-tuple-element.90), channel_id=1, source_target_pairs={{0,8},{8,0},{16,24},{24,16},{32,40},{40,32},{48,56},{56,48},{64,72... | collective-permute-start | bytes 663560 | tf_op jit(solution)/shard_map/ppermute | solution.py:586
  48.4 8.8 %collective-permute-start.10 = (f32[192,256]{1,0:T(8,128)S(1)}, f32[192,256]{1,0:T(8,128)S(1)}, u32[]{:S(2)}, u32[]{:S(2)}) collective-permute-start(f32[192,256]{1,0:T(8,128)S(1)} %get-tuple-element.94), channel_id=1, source_target_pairs={{8,16},{16,8},{24,32},{32,24},{40,48},{48,40},{56,64},{64,56},{72,... | collective-permute-start | bytes 589832 | tf_op jit(solution)/shard_map/ppermute | solution.py:586
  52.1 3.7 %collective-permute-start.9 = (f32[3,8,128]{2,1,0:T(8,128)S(1)}, f32[3,8,128]{2,1,0:T(8,128)S(1)}, u32[]{:S(2)}, u32[]{:S(2)}) collective-permute-start(f32[3,8,128]{2,1,0:T(8,128)S(1)} %shard_map.122.ours), channel_id=1, source_target_pairs={{0,1},{1,0},{2,3},{3,2},{4,5},{5,4},{6,7},{7,6},{8,9},{9,8},{10,11... | collective-permute-start | bytes 36872 | tf_op jit(solution)/shard_map/ppermute | solution.py:586
  57.3 14.9 %collective-permute-start.12 = (f32[3,2,16,256]{3,2,1,0:T(8,128)S(1)}, f32[3,2,16,256]{3,2,1,0:T(8,128)S(1)}, u32[]{:S(2)}, u32[]{:S(2)}) collective-permute-start(f32[3,2,16,256]{3,2,1,0:T(8,128)S(1)} %get-tuple-element.99), channel_id=1, source_target_pairs={{0,1},{1,0},{2,3},{3,2},{4,5},{5,4},{6,7},{7,6},{8,9},{9,8},{10,11... | collective-permute-start | bytes 294920 | tf_op jit(solution)/shard_map/ppermute | solution.py:586
  57.5 14.6 %collective-permute-start.13 = (f32[3,2,16,256]{3,2,1,0:T(8,128)S(1)}, f32[3,2,16,256]{3,2,1,0:T(8,128)S(1)}, u32[]{:S(2)}, u32[]{:S(2)}) collective-permute-start(f32[3,2,16,256]{3,2,1,0:T(8,128)S(1)} %get-tuple-element.100), channel_id=1, source_target_pairs={{1,2},{2,1},{3,4},{4,3},{5,6},{6,5},{7,0},{0,7},{9,10},{10,9},{11,... | collective-permute-start | bytes 294920 | tf_op jit(solution)/shard_map/ppermute | solution.py:586
  58.3 5.2 %collective-permute-start.11 = (f32[6,4,128]{2,1,0:T(4,128)S(1)}, f32[6,4,128]{2,1,0:T(4,128)S(1)}, u32[]{:S(2)}, u32[]{:S(2)}) collective-permute-start(f32[6,4,128]{2,1,0:T(4,128)S(1)} %shard_map.123.after.ours.token), channel_id=1, source_target_pairs={{0,64},{8,72},{16,80},{24,88},{32,96},{40,104},{48,112},{56,120},{... | collective-permute-start | bytes 36872 | tf_op jit(solution)/shard_map/ppermute | solution.py:595
  63.5 5.3 %collective-permute-start.14 = (f32[6,8,128]{2,1,0:T(8,128)S(1)}, f32[6,8,128]{2,1,0:T(8,128)S(1)}, u32[]{:S(2)}, u32[]{:S(2)}) collective-permute-start(f32[6,8,128]{2,1,0:T(8,128)S(1)} %shard_map.125.after.ours), channel_id=1, source_target_pairs={{0,32},{8,40},{16,48},{24,56},{32,0},{40,8},{48,16},{56,24},{64,96... | collective-permute-start | bytes 73736 | tf_op jit(solution)/shard_map/ppermute | solution.py:595
  68.8 5.6 %collective-permute-start.15 = (f32[6,16,128]{2,1,0:T(8,128)S(1)}, f32[6,16,128]{2,1,0:T(8,128)S(1)}, u32[]{:S(2)}, u32[]{:S(2)}) collective-permute-start(f32[6,16,128]{2,1,0:T(8,128)S(1)} %shard_map.128.after.ours), channel_id=1, source_target_pairs={{0,2},{1,3},{2,0},{3,1},{4,6},{5,7},{6,4},{7,5},{8,10},{9,11},{10,... | collective-permute-start | bytes 147464 | tf_op jit(solution)/shard_map/ppermute | solution.py:595
  74.4 4.7 %collective-permute-start.16 = (f32[6,32,128]{2,1,0:T(8,128)S(1)}, f32[6,32,128]{2,1,0:T(8,128)S(1)}, u32[]{:S(2)}, u32[]{:S(2)}) collective-permute-start(f32[6,32,128]{2,1,0:T(8,128)S(1)} %shard_map.130.ours), channel_id=1, source_target_pairs={{0,4},{1,5},{2,6},{3,7},{4,0},{5,1},{6,2},{7,3},{8,12},{9,13},{10,... | collective-permute-start | bytes 294920 | tf_op jit(solution)/shard_map/ppermute | solution.py:595
  79.1 5.8 %collective-permute-start.17 = (f32[6,64,128]{2,1,0:T(8,128)S(1)}, f32[6,64,128]{2,1,0:T(8,128)S(1)}, u32[]{:S(2)}, u32[]{:S(2)}) collective-permute-start(f32[6,64,128]{2,1,0:T(8,128)S(1)} %shard_map.131.ours), channel_id=1, source_target_pairs={{0,16},{8,24},{16,0},{24,8},{32,48},{40,56},{48,32},{56,40},{64,80... | collective-permute-start | bytes 589832 | tf_op jit(solution)/shard_map/ppermute | solution.py:595

commit v4 on v3

--- a/solution.py
+++ b/solution.py
@@ -67,7 +67,13 @@
     return jnp.dot(jnp.concatenate([high, low], axis=1), ones, preferred_element_type=F32)
 
 
-def contact(substep, pairs, u_ref, half_ref, places, share, pos, ids, corner):
+def contact_kernel(substep, pairs, u_ref, pst, surface_out, force_out, xa, places):
+    slab, split = position()
+    corner = (slab * CX, split * CY)
+    share = 0.5 * DT if substep == SUB - 1 else DT
+    at_a = jnp.where(lax.rem(slab, 2) == 0, CX, 2)
+    pos, ids = [pst[c] for c in range(3)], pst[6].astype(jnp.int32)
+    surface_out[...] = jnp.zeros_like(surface_out)
     row = lax.broadcasted_iota(jnp.int32, (CY, 128), 0)
     lane = lax.broadcasted_iota(jnp.int32, (CY, 128), 1)
     place_y = (row + corner[1]).astype(F32)
@@ -105,7 +111,7 @@
             for z in range(SL):
                 at = c * SL * CY + z * CY
                 surface = jnp.where(lane == 128 - SL + z, sums[at : at + CY], surface)
-            half_ref[c, target, :, CZ - 128 :] += share * surface
+            surface_out[c, target] += share * surface
         return tuple(
             totals[c] - jnp.where(hit, jnp.sum(pulled[c], axis=0, keepdims=True), 0.0)
             for c in range(3)
@@ -117,20 +123,36 @@
         return totals
 
     none = tuple(jnp.zeros((8, 128), F32) for _ in range(3))
-    return lax.fori_loop(0, (live + CHUNK - 1) // CHUNK, some, none)
-
-
-def send_edges(u_ref, force, xa, xb, ya, yb, even_x, even_y):
-    at_a = jnp.where(even_x, CX, 2)
-    at_b = jnp.where(even_x, 2, CX)
-    for c in range(3):
+    force = lax.fori_loop(0, (live + CHUNK - 1) // CHUNK, some, none)
+    for c in range(3):
+        force_out[c] = force[c]
         for h in range(2):
             lanes = slice(128 * h, 128 * h + 128)
             for layer in range(2):
                 rows = slice((2 * c + layer) * CY, (2 * c + layer + 1) * CY)
                 xa[rows, lanes] = u_ref[c, h, at_a + layer, LO : LO + CY, :]
+
+
+    xa[6 * CY :, 0:128] = jnp.concatenate([force[0][0:GROUP], force[2][0:GROUP]], axis=0)
+    xa[6 * CY :, 128:256] = force[1]
+
+
+def chip_force(xa, c):
+    at, lane = 6 * CY + GROUP * (c // 2), 128 * (c % 2)
+    return jnp.concatenate(
+        [xa[at : at + GROUP, lane : lane + 128], jnp.zeros((8 - GROUP, 128), F32)], axis=0
+    )
+
+
+def send_edges(u_ref, xb, ya, yb, even_x, even_y):
+    at_b = jnp.where(even_x, 2, CX)
+    xb[6 * CY :, :] = jnp.zeros((XB.shape[0] - 6 * CY, CZ), F32)
+    for c in range(3):
+        for h in range(2):
+            lanes = slice(128 * h, 128 * h + 128)
+            for layer in range(2):
+                rows = slice((2 * c + layer) * CY, (2 * c + layer + 1) * CY)
                 xb[rows, lanes] = u_ref[c, h, at_b + layer, LO : LO + CY, :]
-            xa[6 * CY + 8 * c : 6 * CY + 8 * c + 8, lanes] = force[c]
     for want_even, low, high in ((True, yb, ya), (False, ya, yb)):
 
         @pl.when(even_y == want_even)
@@ -147,8 +169,7 @@
 
 
 def begin_kernel(
-    pairs, u, v, a, pp, pv, pa,
-    u_out, half_out, pst, perm, xa, xb, ya, yb, places, cells, blocks_in, sems, block_sems,
+    u, v, a, pp, pv, pa, u_out, half_out, pst, perm, xb, ya, yb, cells, blocks_in, sems, block_sems
 ):
     slab, split = position()
     splits = lax.axis_size("split")
@@ -219,13 +240,7 @@
                 moved = cells[0, c, x] + DT * half
                 for h in range(2):
                     u_out[c, h, x + 2, LO : LO + CY, :] = moved[:, 128 * h : 128 * h + 128]
-
-    ids = pst[6].astype(jnp.int32)
-    pos = [pst[c] for c in range(3)]
-    force = contact(0, pairs, u_out, half_out, places, DT, pos, ids, (slab * CX, split * CY))
-    for c in range(3):
-        pst[7 + c] = force[c]
-    send_edges(u_out, force, xa, xb, ya, yb, even_x, even_y)
+    send_edges(u_out, xb, ya, yb, even_x, even_y)
 
 
 def words_kernel(masks, w_out, rim_out):
@@ -245,14 +260,14 @@
             rim_out[r, x : x + 1, :] = word[y : y + 1, :]
 
 
-def corner_kernel(ya_own, yb_own, xa, xb, pst, token, ya, yb):
+def corner_kernel(ya_own, yb_own, xa, xb, own_force, token, ya, yb):
     slab, split = position()
     even_x, even_y = lax.rem(slab, 2) == 0, lax.rem(split, 2) == 0
     for c in range(3):
         for r in range(2):
             ya[c, r, 0:CX, :] = ya_own[c, r]
             yb[c, r, 0:CX, :] = yb_own[c, r]
-        force = pst[7 + c] + xa[6 * CY + 8 * c : 6 * CY + 8 * c + 8, 0:128]
+        force = own_force[c] + chip_force(xa, c)
         for h in range(2):
             ya[c, 0, CX + 2 : CX + 2 + GROUP, 128 * h : 128 * h + 128] = force[0:GROUP]
     for is_x in (True, False):
@@ -443,7 +458,7 @@
                 crossing[2 * side + mine, c, h] = jnp.zeros((8, 128), F32) if value is None else value
 
 
-def close(scale, inner, edge, ya_own, yb_own, ya, yb, rim, even_y, crossing, store):
+def close(scale, inner, edge, surface, ya_own, yb_own, ya, yb, rim, even_y, crossing, store):
     for side in range(2):
         first = even_y == (side == 1)
 
@@ -463,20 +478,22 @@
             for h in range(2):
                 for y in range(0, CY, 8):
                     value = source[c, at, y : y + 8, 128 * h : 128 * h + 128]
+                    if h == 1:
+                        value = value + surface[c, x, y : y + 8, :]
                     for r in (0, 1) if y == 0 else (2, 3) if y == CY - 8 else ():
                         more = crossing[r, c, h, x : x + 1, :]
                         value = value + scale * jnp.where(sub == (r if r < 2 else r + 4), more, 0.0)
                     store(c, x, y, h, value)
 
 
-def particle_force(xa, ya, pst, c):
+def particle_force(xa, ya, own_force, c):
     theirs = jnp.concatenate([ya[c, 0, CX + 2 : CX + 2 + GROUP, 0:128], jnp.zeros((4, 128), F32)], axis=0)
-    return pst[7 + c] + xa[6 * CY + 8 * c : 6 * CY + 8 * c + 8, 0:128] + theirs
+    return own_force[c] + chip_force(xa, c) + theirs
 
 
 def close_kernel(
-    substep, pairs, u, inner, edge, ya_own, yb_own, xa, ya, yb, rim, pst,
-    u_out, half_out, pst_out, xa_out, xb_out, ya_out, yb_out, places, crossing,
+    u, inner, edge, surface, ya_own, yb_own, xa, ya, yb, rim, pst, own_force,
+    u_out, half_out, pst_out, xb_out, ya_out, yb_out, crossing,
 ):
     slab, split = position()
     even_x, even_y = lax.rem(slab, 2) == 0, lax.rem(split, 2) == 0
@@ -486,27 +503,19 @@
         pad = slice(LO + y, LO + y + 8)
         u_out[c, h, x + 2, pad, :] = u[c, h, x + 2, pad, :] + DT * value
 
-    close(DT, inner, edge, ya_own, yb_own, ya, yb, rim, even_y, crossing, store)
-
-    pst_out[6:] = pst[6:]
-    pos = []
-    for c in range(3):
-        moved = pst[3 + c] + DT * INV_MASS * particle_force(xa, ya, pst, c)
+    close(DT, inner, edge, surface, ya_own, yb_own, ya, yb, rim, even_y, crossing, store)
+
+    pst_out[6] = pst[6]
+    for c in range(3):
+        moved = pst[3 + c] + DT * INV_MASS * particle_force(xa, ya, own_force, c)
         pst_out[3 + c] = moved
-        pos.append(pst[c] + DT * moved)
-        pst_out[c] = pos[c]
-    share = 0.5 * DT if substep == SUB - 2 else DT
-    ids = pst[6].astype(jnp.int32)
-    corner = (slab * CX, split * CY)
-    force = contact(substep + 1, pairs, u_out, half_out, places, share, pos, ids, corner)
-    for c in range(3):
-        pst_out[7 + c] = force[c]
-    send_edges(u_out, force, xa_out, xb_out, ya_out, yb_out, even_x, even_y)
-
-
-def pair_kernel(xa, pst, out):
-    for c in range(3):
-        out[c] = pst[7 + c] + xa[6 * CY + 8 * c : 6 * CY + 8 * c + 8, 0:128]
+        pst_out[c] = pst[c] + DT * moved
+    send_edges(u_out, xb_out, ya_out, yb_out, even_x, even_y)
+
+
+def pair_kernel(xa, own_force, out):
+    for c in range(3):
+        out[c] = own_force[c] + chip_force(xa, c)
 
 
 def state_kernel(ours, theirs, pst, token, out):
@@ -522,7 +531,7 @@
     out[:, count : 2 * count] = theirs[...]
 
 
-def last_kernel(u, inner, edge, ya_own, yb_own, ya, yb, rim, after, u_out, v_out, token, crossing):
+def last_kernel(u, inner, edge, surface, ya_own, yb_own, ya, yb, rim, after, u_out, v_out, token, crossing):
     slab, split = position()
 
     def store(c, x, y, h, value):
@@ -531,7 +540,7 @@
         u_out[c, x, y : y + 8, lanes] = u[c, h, x + 2, LO + y : LO + y + 8, :]
 
     even_y = lax.rem(split, 2) == 0
-    close(0.5 * DT, inner, edge, ya_own, yb_own, ya, yb, rim, even_y, crossing, store)
+    close(0.5 * DT, inner, edge, surface, ya_own, yb_own, ya, yb, rim, even_y, crossing, store)
     token[...] = crossing[0, 0, 0]
 
 
@@ -553,9 +562,10 @@
 PADDED = jax.ShapeDtypeStruct((3, 2, CX + 4, CY + 16, 128), F32)
 SIDE = jax.ShapeDtypeStruct((3, 2, CX + 2, CY + 16, 128), F32)
 WORDS = jax.ShapeDtypeStruct((CX, CY, CZ), jnp.int32)
-PST = jax.ShapeDtypeStruct((10, 8, 128), F32)
-XA = jax.ShapeDtypeStruct((6 * CY + 24, CZ), F32)
-XB = jax.ShapeDtypeStruct((6 * CY, CZ), F32)
+PST = jax.ShapeDtypeStruct((7, 8, 128), F32)
+SURFACE = jax.ShapeDtypeStruct((3, CX, CY, 128), F32)
+XA = jax.ShapeDtypeStruct((6 * CY + 8, CZ), F32)
+XB = jax.ShapeDtypeStruct((6 * CY + 16, CZ), F32)
 YE = jax.ShapeDtypeStruct((3, 2, CX, CZ), F32)
 YA = jax.ShapeDtypeStruct((3, 2, 16, CZ), F32)
 PAIR = jax.ShapeDtypeStruct((3, 8, 128), F32)
@@ -603,12 +613,10 @@
     u, v, a, pp, pv, pa = [pltpu.with_memory_space_constraint(x, pltpu.HBM) for x in (u, v, a, pp, pv, pa)]
     u, half, pst, perm, *edges = call(
         begin_kernel,
-        (pairs, u, v, a, pp, pv, pa),
-        [PADDED, STATE, PST, jax.ShapeDtypeStruct((blocks, blocks), F32), XA, XB, YE, YE],
-        ins=[SMEM] + [HBM] * 6,
-        limit=40,
+        (u, v, a, pp, pv, pa),
+        [PADDED, STATE, PST, jax.ShapeDtypeStruct((blocks, blocks), F32), XB, YE, YE],
+        ins=[HBM] * 6,
         scratch=(
-            PLACES,
             pltpu.VMEM((3, *STATE.shape), F32),
             pltpu.VMEM((3, *pp.shape), F32),
             pltpu.SemaphoreType.DMA((3, CX // STEP)),
@@ -619,10 +627,19 @@
     for substep in range(SUB):
         last = substep == SUB - 1
         scale = 0.5 * DT if last else DT
-        xa, xb, ya_own, yb_own = edges
-        xa, xb = swap(xa, "slab", 0), swap(xb, "slab", 1)
+        xb, ya_own, yb_own = edges
+        xb = swap(xb, "slab", 1)
+        surface, own_force, xa = call(
+            functools.partial(contact_kernel, substep),
+            (pairs, u, pst),
+            [SURFACE, PAIR, XA],
+            scalars=1,
+            scratch=(PLACES,),
+            us=1.5,
+        )
+        xa = swap(xa, "slab", 0)
         if last:
-            (ours,) = call(pair_kernel, (xa, pst), [PAIR], us=0.1)
+            (ours,) = call(pair_kernel, (xa, own_force), [PAIR], us=0.1)
             theirs = swap(ours, "split", 0)
             left, right, token = call(turn_kernel, (u,), [SIDE, SIDE, TOKEN])
             (gathered,) = call(state_kernel, (ours, theirs, pst, token), [rows_of(GROUP)], us=0.1)
@@ -637,7 +654,7 @@
                 functools.partial(inner_kernel, scale), (u, half, words), [HALVES, SIDE, SIDE, TOKEN], us=3.6
             )
         after = gathered if last else token
-        ya, yb = call(corner_kernel, (ya_own, yb_own, xa, xb, pst, after), [YA, YA], us=0.1)
+        ya, yb = call(corner_kernel, (ya_own, yb_own, xa, xb, own_force, after), [YA, YA], us=0.1)
         ya, yb = swap(ya, "split", 0), swap(yb, "split", 1)
         if last:
             gathered = after = share_round(gathered, 0, token)
@@ -651,18 +668,17 @@
         if last:
             break
         u, half, pst, *edges = call(
-            functools.partial(close_kernel, substep),
-            (pairs, u, inner, edge, ya_own, yb_own, xa, ya, yb, rim, pst),
-            [PADDED, STATE, PST, XA, XB, YE, YE],
-            scalars=1,
-            scratch=(PLACES, CROSSING),
-            us=3.0,
+            close_kernel,
+            (u, inner, edge, surface, ya_own, yb_own, xa, ya, yb, rim, pst, own_force),
+            [PADDED, STATE, PST, XB, YE, YE],
+            scratch=(CROSSING,),
+            us=1.3,
         )
 
     gathered = share_round(gathered, 1, token)
     final_u, final_v, token = call(
         last_kernel,
-        (u, inner, edge, ya_own, yb_own, ya, yb, rim, gathered),
+        (u, inner, edge, surface, ya_own, yb_own, ya, yb, rim, gathered),
         [STATE, STATE, TOKEN],
         scratch=(CROSSING,),
         us=1.4,

time: 86.6 us -> 83.3 us (0.962)
  starting transfers between devices: 29.8 us -> 26 us
  Pallas kernels: 31.3 us -> 33.4 us
    ppermute x13, starting transfers between devices: 24.8 us -> 22.4 us  [swap(): return lax.ppermute(value, axis, pairs)]
    pallas_call x23 -> x26, Pallas kernels: 31.3 us -> 33.4 us  [call(): pl.pallas_call(kernel, out_shape=outputs, in_specs=ins or [SMEM] * scalar...]
    ppermute x13, waiting for transfers between devices: 9.09 us -> 7.12 us  [swap(): return lax.ppermute(value, axis, pairs)]
    ppermute x5, waiting for transfers between devices: 14.4 us -> 16.2 us  [share_round(): lax.ppermute(gathered, axis, [(i, i ^ bit) for i in range(lax.axis_size(a...]
    ppermute x5, starting transfers between devices: 5.06 us -> 3.61 us  [share_round(): lax.ppermute(gathered, axis, [(i, i ^ bit) for i in range(lax.axis_size(a...]
  transfers between devices with their start and end apart: 18 -> 18, of which waited for: 9 -> 9; matrix products, arithmetic and copies ran while one was open for 0% -> 0% of each run, Pallas kernels for 26% -> 31%
where the time goes in v4:
time: 83.3 us; the launch traced here: 83.6 us
  Pallas kernels  33.4 us (40%)
  starting transfers between devices  26 us (31%)
  waiting for transfers between devices  23.3 us (28%)
  between operations  0.88 us (1%)
    pallas_call x26, Pallas kernels, call(): pl.pallas_call(kernel, out_shape=outputs, in_specs=ins or [SMEM] * scalar...  33.4 us
    ppermute x13, starting transfers between devices, swap(): return lax.ppermute(value, axis, pairs)  22.4 us
    ppermute x5, waiting for transfers between devices, share_round(): lax.ppermute(gathered, axis, [(i, i ^ bit) for i in range(lax.axis_size(a...  16.2 us
    ppermute x13, waiting for transfers between devices, swap(): return lax.ppermute(value, axis, pairs)  7.12 us
    ppermute x5, starting transfers between devices, share_round(): lax.ppermute(gathered, axis, [(i, i ^ bit) for i in range(lax.axis_size(a...  3.61 us
  transfers between devices with their start and end apart: 18, of which 9 were waited for; matrix products, arithmetic and copies ran while one was open for 0% of the time, Pallas kernels for 31%

profile of v4, /device:TPU:0, one launch (start us, length us, event | category | flops | bytes accessed | tf_op | source)
XLA Modules:
  0.0 83.6 jit_solution(17100134444719992032)
XLA Ops:
  0.6 2.7 %shard_map.111 = (f32[3,2,12,48,128]{4,3,2,1,0:T(8,128)S(1)}, f32[3,8,32,256]{3,2,1,0:T(8,128)S(1)}, f32[7,8,128]{2,1,0:T(8,128)S(1)}, f32[128,128]{1,0:T(8,128)...) custom-call(f32[3,8,32,256]{3,2,1,0:T(8,128)} %u.1, ...), custom_call_target="tpu_custom_call" | custom-call | bytes 3000000 | tf_op jit(solution)/shard_map/pallas_call | solution.py:580
  3.3 6.3 %collective-permute-start.1 = (f32[208,256]{1,0:T(8,128)S(1)}, f32[208,256]{1,0:T(8,128)S(1)}, u32[]{:S(2)}, u32[]{:S(2)}) collective-permute-start(f32[208,256]{1,0:T(8,128)S(1)} %get-tuple-element.68), channel_id=1, source_target_pairs={{8,16},{16,8},{24,32},{32,24},{40,48},{48,40},{56,64},{64,56},{72,... | collective-permute-start | bytes 638984 | tf_op jit(solution)/shard_map/ppermute | solution.py:596
  9.6 2.6 %shard_map.114 = (f32[3,8,32,128]{3,2,1,0:T(8,128)S(1)}, f32[3,8,128]{2,1,0:T(8,128)S(1)}, f32[200,256]{1,0:T(8,128)S(1)}) custom-call(s32[3,2,16]{2,1,0:T(2,128)S(1)} %copy-done.1, f32[3,2,12,48,128]{4,3,2,1,0:T(8,128)S(1)} %get-tuple-element.62.u.u_ref.u_own, f32[7,8,128]{2,1,0:T(8,128)S(1)} %get-tuple-element.66.pst), custom_call_target="tpu_custom_call" | custom-call | bytes 4500000 | tf_op jit(solution)/shard_map/pallas_call | solution.py:580
  12.4 3.6 %shard_map.113 = (f32[3,4,32,256]{3,2,1,0:T(8,128)S(1)}, f32[3,2,10,48,128]{4,3,2,1,0:T(8,128)S(1)}, f32[3,2,10,48,128]{4,3,2,1,0:T(8,128)S(1)}, f32[8,128]{1,0:T(8,128)S(1)}) custom-call(f32[3,2,12,48,128]{4,3,2,1,0:T(8,128)S(1)} %get-tuple-element.62.u.u_ref.u_own, f32[3,8,32,256]{3,2,1,0:T(8,128)S(1)} %get-tuple-element.63.half, ...), custom_call_target="tpu_custom_call" | custom-call | bytes 10800000 | tf_op jit(solution)/shard_map/pallas_call | solution.py:580
  16.2 3.7 %collective-permute-start.3 = (f32[3,2,16,256]{3,2,1,0:T(8,128)S(1)}, f32[3,2,16,256]{3,2,1,0:T(8,128)S(1)}, u32[]{:S(2)}, u32[]{:S(2)}) collective-permute-start(f32[3,2,16,256]{3,2,1,0:T(8,128)S(1)} %get-tuple-element.78), channel_id=1, source_target_pairs={{1,2},{2,1},{3,4},{4,3},{5,6},{6,5},{7,0},{0,7},{9,10},{10,9},{11,... | collective-permute-start | bytes 294920 | tf_op jit(solution)/shard_map/ppermute | solution.py:596
  19.8 3.6 %shard_map.115 = (f32[3,4,32,256]{3,2,1,0:T(8,128)S(1)}, f32[8,128]{1,0:T(8,128)}) custom-call(f32[200,256]{1,0:T(8,128)S(1)} %collective-permute-done.xa, f32[208,256]{1,0:T(8,128)S(1)} %collective-permute-done.1.xb, f32[3,2,12,48,128]{4,3,2,1,0:T(8,128)S(1)} %get-tuple-element.62.u.u_ref.u_own, f32[3,2,10,48,128]{4,3,2,1,0:T(8,128)S(1)} %get-tuple-element.69.left_own, ...), custom_call_target="tpu_custom_call" | custom-call | bytes 10800000 | tf_op jit(solution)/shard_map/pallas_call | solution.py:580
  24.0 2.5 %collective-permute-start.5 = (f32[208,256]{1,0:T(8,128)S(1)}, f32[208,256]{1,0:T(8,128)S(1)}, u32[]{:S(2)}, u32[]{:S(2)}) collective-permute-start(f32[208,256]{1,0:T(8,128)S(1)} %get-tuple-element.85), channel_id=1, source_target_pairs={{8,16},{16,8},{24,32},{32,24},{40,48},{48,40},{56,64},{64,56},{72,... | collective-permute-start | bytes 638984 | tf_op jit(solution)/shard_map/ppermute | solution.py:596
  27.2 3.6 %shard_map.118 = (f32[3,4,32,256]{3,2,1,0:T(8,128)S(1)}, f32[3,2,10,48,128]{4,3,2,1,0:T(8,128)S(1)}, f32[3,2,10,48,128]{4,3,2,1,0:T(8,128)S(1)}, f32[8,128]{1,0:T(8,128)S(1)}) custom-call(f32[3,2,12,48,128]{4,3,2,1,0:T(8,128)S(1)} %get-tuple-element.80.u.u_ref.u_own, f32[3,8,32,256]{3,2,1,0:T(8,128)S(1)} %get-tuple-element.81.half, ...), custom_call_target="tpu_custom_call" | custom-call | bytes 10800000 | tf_op jit(solution)/shard_map/pallas_call | solution.py:580
  30.9 2.1 %collective-permute-done.5.xb = f32[208,256]{1,0:T(8,128)S(1)} collective-permute-done((f32[208,256]{1,0:T(8,128)S(1)}, f32[208,256]{1,0:T(8,128)S(1)}, u32[]{:S(2)}, u32[]{:S(2)}) %collective-permute-start.5) | collective-permute-done | bytes 213024 | tf_op jit(solution)/shard_map/ppermute | solution.py:596
  33.1 3.4 %collective-permute-start.7 = (f32[3,2,16,256]{3,2,1,0:T(8,128)S(1)}, f32[3,2,16,256]{3,2,1,0:T(8,128)S(1)}, u32[]{:S(2)}, u32[]{:S(2)}) collective-permute-start(f32[3,2,16,256]{3,2,1,0:T(8,128)S(1)} %get-tuple-element.95), channel_id=1, source_target_pairs={{1,2},{2,1},{3,4},{4,3},{5,6},{6,5},{7,0},{0,7},{9,10},{10,9},{11,... | collective-permute-start | bytes 294920 | tf_op jit(solution)/shard_map/ppermute | solution.py:596
  36.5 3.6 %shard_map.120 = (f32[3,4,32,256]{3,2,1,0:T(8,128)S(1)}, f32[8,128]{1,0:T(8,128)}) custom-call(f32[200,256]{1,0:T(8,128)S(1)} %collective-permute-done.4.xa, f32[208,256]{1,0:T(8,128)S(1)} %collective-permute-done.5.xb, f32[3,2,12,48,128]{4,3,2,1,0:T(8,128)S(1)} %get-tuple-element.80.u.u_ref.u_own, f32[3,2,10,48,128]{4,3,2,1,0:T(8,128)S(1)} %get-tuple-element.86.left_own, ...), custom_call_target="tpu_custom_call" | custom-call | bytes 10800000 | tf_op jit(solution)/shard_map/pallas_call | solution.py:580
  40.6 2.6 %shard_map.124 = (f32[3,8,32,128]{3,2,1,0:T(8,128)S(1)}, f32[3,8,128]{2,1,0:T(8,128)S(1)}, f32[200,256]{1,0:T(8,128)S(1)}) custom-call(s32[3,2,16]{2,1,0:T(2,128)S(1)} %copy-done.1, f32[3,2,12,48,128]{4,3,2,1,0:T(8,128)S(1)} %get-tuple-element.96.u.u_ref.u_own, f32[7,8,128]{2,1,0:T(8,128)S(1)} %get-tuple-element.100.pst), custom_call_target="tpu_custom_call" | custom-call | bytes 4500000 | tf_op jit(solution)/shard_map/pallas_call | solution.py:580
  43.3 2.1 %collective-permute-start.10 = (f32[208,256]{1,0:T(8,128)S(1)}, f32[208,256]{1,0:T(8,128)S(1)}, u32[]{:S(2)}, u32[]{:S(2)}) collective-permute-start(f32[208,256]{1,0:T(8,128)S(1)} %get-tuple-element.105), channel_id=1, source_target_pairs={{8,16},{16,8},{24,32},{32,24},{40,48},{48,40},{56,64},{64,56},{72,... | collective-permute-start | bytes 638984 | tf_op jit(solution)/shard_map/ppermute | solution.py:596
  47.4 1.9 %collective-permute-done.9.theirs = f32[3,8,128]{2,1,0:T(8,128)S(1)} collective-permute-done((f32[3,8,128]{2,1,0:T(8,128)S(1)}, f32[3,8,128]{2,1,0:T(8,128)S(1)}, u32[]{:S(2)}, u32[]{:S(2)}) %collective-permute-start.9) | collective-permute-done | bytes 12320 | tf_op jit(solution)/shard_map/ppermute | solution.py:596
  49.3 3.0 %collective-permute-done.10.xb = f32[208,256]{1,0:T(8,128)S(1)} collective-permute-done((f32[208,256]{1,0:T(8,128)S(1)}, f32[208,256]{1,0:T(8,128)S(1)}, u32[]{:S(2)}, u32[]{:S(2)}) %collective-permute-start.10) | collective-permute-done | bytes 213024 | tf_op jit(solution)/shard_map/ppermute | solution.py:596
  53.4 2.0 %collective-permute-start.13 = (f32[3,2,16,256]{3,2,1,0:T(8,128)S(1)}, f32[3,2,16,256]{3,2,1,0:T(8,128)S(1)}, u32[]{:S(2)}, u32[]{:S(2)}) collective-permute-start(f32[3,2,16,256]{3,2,1,0:T(8,128)S(1)} %get-tuple-element.112), channel_id=1, source_target_pairs={{1,2},{2,1},{3,4},{4,3},{5,6},{6,5},{7,0},{0,7},{9,10},{10,9},{11,... | collective-permute-start | bytes 294920 | tf_op jit(solution)/shard_map/ppermute | solution.py:596
  56.8 2.6 %shard_map.127 = (f32[3,4,32,256]{3,2,1,0:T(8,128)S(1)}, f32[8,128]{1,0:T(8,128)S(1)}) custom-call(f32[3,2,12,48,128]{4,3,2,1,0:T(8,128)S(1)} %get-tuple-element.96.u.u_ref.u_own, f32[3,2,10,48,128]{4,3,2,1,0:T(8,128)S(1)} %get-tuple-element.97.left.left_own, f32[3,2,10,48,128]{4,3,2,1,0:T(8,128)S(1)} %get-tuple-element.98.right.right_own, ...), custom_call_target="tpu_custom_call" | custom-call | bytes 7800000 | tf_op jit(solution)/shard_map/pallas_call | solution.py:580
  59.4 1.5 %collective-permute-done.11.theirs = f32[6,4,128]{2,1,0:T(4,128)S(1)} collective-permute-done((f32[6,4,128]{2,1,0:T(4,128)S(1)}, f32[6,4,128]{2,1,0:T(4,128)S(1)}, u32[]{:S(2)}, u32[]{:S(2)}) %collective-permute-start.11) | collective-permute-done | bytes 12320 | tf_op jit(solution)/shard_map/ppermute | solution.py:605
  61.0 3.0 %shard_map.129 = (f32[3,4,32,256]{3,2,1,0:T(8,128)S(1)}, f32[8,128]{1,0:T(8,128)S(1)}) custom-call(f32[200,256]{1,0:T(8,128)S(1)} %collective-permute-done.8.xa, f32[208,256]{1,0:T(8,128)S(1)} %collective-permute-done.10.xb, f32[3,2,12,48,128]{4,3,2,1,0:T(8,128)S(1)} %get-tuple-element.96.u.u_ref.u_own, ...), custom_call_target="tpu_custom_call" | custom-call | bytes 10800000 | tf_op jit(solution)/shard_map/pallas_call | solution.py:580
  64.0 2.3 %collective-permute-done.14.theirs = f32[6,8,128]{2,1,0:T(8,128)S(1)} collective-permute-done((f32[6,8,128]{2,1,0:T(8,128)S(1)}, f32[6,8,128]{2,1,0:T(8,128)S(1)}, u32[]{:S(2)}, u32[]{:S(2)}) %collective-permute-start.14) | collective-permute-done | bytes 24608 | tf_op jit(solution)/shard_map/ppermute | solution.py:605
  67.2 1.5 %shard_map.132 = (f32[3,8,32,256]{3,2,1,0:T(8,128)}, f32[3,8,32,256]{3,2,1,0:T(8,128)}, f32[8,128]{1,0:T(8,128)S(1)}) custom-call(f32[3,2,12,48,128]{4,3,2,1,0:T(8,128)S(1)} %get-tuple-element.96.u.u_ref.u_own, f32[3,4,32,256]{3,2,1,0:T(8,128)S(1)} %get-tuple-element.104.inner, f32[3,4,32,256]{3,2,1,0:T(8,128)S(1)} %get-tuple-element.107.edge, ...), custom_call_target="tpu_custom_call" | custom-call | bytes 4200000 | tf_op jit(solution)/shard_map/pallas_call | solution.py:580
  68.7 3.2 %collective-permute-done.15.theirs = f32[6,16,128]{2,1,0:T(8,128)S(1)} collective-permute-done((f32[6,16,128]{2,1,0:T(8,128)S(1)}, f32[6,16,128]{2,1,0:T(8,128)S(1)}, u32[]{:S(2)}, u32[]{:S(2)}) %collective-permute-start.15) | collective-permute-done | bytes 49184 | tf_op jit(solution)/shard_map/ppermute | solution.py:605
  73.1 3.5 %collective-permute-done.16.theirs = f32[6,32,128]{2,1,0:T(8,128)S(1)} collective-permute-done((f32[6,32,128]{2,1,0:T(8,128)S(1)}, f32[6,32,128]{2,1,0:T(8,128)S(1)}, u32[]{:S(2)}, u32[]{:S(2)}) %collective-permute-start.16) | collective-permute-done | bytes 98336 | tf_op jit(solution)/shard_map/ppermute | solution.py:605
  76.7 5.7 %collective-permute-done.17.theirs = f32[6,64,128]{2,1,0:T(8,128)S(1)} collective-permute-done((f32[6,64,128]{2,1,0:T(8,128)S(1)}, f32[6,64,128]{2,1,0:T(8,128)S(1)}, u32[]{:S(2)}, u32[]{:S(2)}) %collective-permute-start.17) | collective-permute-done | bytes 196640 | tf_op jit(solution)/shard_map/ppermute | solution.py:605
  (42 shorter events, 10.3 us)
Async XLA Ops:
  0.6 9.0 %copy-start.1 = (s32[3,2,16]{2,1,0:T(2,128)S(1)}, s32[3,2,16]{2,1,0:T(2,128)}, u32[]{:S(2)}) copy-start(s32[3,2,16]{2,1,0:T(2,128)} %pairs.5) | copy-start | bytes 1156
  3.3 9.0 %copy-start = (s32[4,8,32,256]{3,2,1,0:T(8,128)S(1)}, s32[4,8,32,256]{3,2,1,0:T(8,128)}, u32[]{:S(2)}) copy-start(s32[4,8,32,256]{3,2,1,0:T(8,128)} %masks.1) | copy-start | bytes 3145732
  3.3 12.7 %collective-permute-start.1 = (f32[208,256]{1,0:T(8,128)S(1)}, f32[208,256]{1,0:T(8,128)S(1)}, u32[]{:S(2)}, u32[]{:S(2)}) collective-permute-start(f32[208,256]{1,0:T(8,128)S(1)} %get-tuple-element.68), channel_id=1, source_target_pairs={{8,16},{16,8},{24,32},{32,24},{40,48},{48,40},{56,64},{64,56},{72,... | collective-permute-start | bytes 638984 | tf_op jit(solution)/shard_map/ppermute | solution.py:596
  12.2 3.8 %collective-permute-start = (f32[200,256]{1,0:T(8,128)S(1)}, f32[200,256]{1,0:T(8,128)S(1)}, u32[]{:S(2)}, u32[]{:S(2)}) collective-permute-start(f32[200,256]{1,0:T(8,128)S(1)} %get-tuple-element.67), channel_id=1, source_target_pairs={{0,8},{8,0},{16,24},{24,16},{32,40},{40,32},{48,56},{56,48},{64,72... | collective-permute-start | bytes 614408 | tf_op jit(solution)/shard_map/ppermute | solution.py:596
  16.1 7.4 %collective-permute-start.2 = (f32[3,2,16,256]{3,2,1,0:T(8,128)S(1)}, f32[3,2,16,256]{3,2,1,0:T(8,128)S(1)}, u32[]{:S(2)}, u32[]{:S(2)}) collective-permute-start(f32[3,2,16,256]{3,2,1,0:T(8,128)S(1)} %get-tuple-element.77), channel_id=1, source_target_pairs={{0,1},{1,0},{2,3},{3,2},{4,5},{5,4},{6,7},{7,6},{8,9},{9,8},{10,11... | collective-permute-start | bytes 294920 | tf_op jit(solution)/shard_map/ppermute | solution.py:596
  16.2 7.4 %collective-permute-start.3 = (f32[3,2,16,256]{3,2,1,0:T(8,128)S(1)}, f32[3,2,16,256]{3,2,1,0:T(8,128)S(1)}, u32[]{:S(2)}, u32[]{:S(2)}) collective-permute-start(f32[3,2,16,256]{3,2,1,0:T(8,128)S(1)} %get-tuple-element.78), channel_id=1, source_target_pairs={{1,2},{2,1},{3,4},{4,3},{5,6},{6,5},{7,0},{0,7},{9,10},{10,9},{11,... | collective-permute-start | bytes 294920 | tf_op jit(solution)/shard_map/ppermute | solution.py:596
  24.0 9.0 %collective-permute-start.5 = (f32[208,256]{1,0:T(8,128)S(1)}, f32[208,256]{1,0:T(8,128)S(1)}, u32[]{:S(2)}, u32[]{:S(2)}) collective-permute-start(f32[208,256]{1,0:T(8,128)S(1)} %get-tuple-element.85), channel_id=1, source_target_pairs={{8,16},{16,8},{24,32},{32,24},{40,48},{48,40},{56,64},{64,56},{72,... | collective-permute-start | bytes 638984 | tf_op jit(solution)/shard_map/ppermute | solution.py:596
  27.1 3.7 %collective-permute-start.4 = (f32[200,256]{1,0:T(8,128)S(1)}, f32[200,256]{1,0:T(8,128)S(1)}, u32[]{:S(2)}, u32[]{:S(2)}) collective-permute-start(f32[200,256]{1,0:T(8,128)S(1)} %get-tuple-element.84), channel_id=1, source_target_pairs={{0,8},{8,0},{16,24},{24,16},{32,40},{40,32},{48,56},{56,48},{64,72... | collective-permute-start | bytes 614408 | tf_op jit(solution)/shard_map/ppermute | solution.py:596
  33.0 7.1 %collective-permute-start.6 = (f32[3,2,16,256]{3,2,1,0:T(8,128)S(1)}, f32[3,2,16,256]{3,2,1,0:T(8,128)S(1)}, u32[]{:S(2)}, u32[]{:S(2)}) collective-permute-start(f32[3,2,16,256]{3,2,1,0:T(8,128)S(1)} %get-tuple-element.94), channel_id=1, source_target_pairs={{0,1},{1,0},{2,3},{3,2},{4,5},{5,4},{6,7},{7,6},{8,9},{9,8},{10,11... | collective-permute-start | bytes 294920 | tf_op jit(solution)/shard_map/ppermute | solution.py:596
  33.1 7.0 %collective-permute-start.7 = (f32[3,2,16,256]{3,2,1,0:T(8,128)S(1)}, f32[3,2,16,256]{3,2,1,0:T(8,128)S(1)}, u32[]{:S(2)}, u32[]{:S(2)}) collective-permute-start(f32[3,2,16,256]{3,2,1,0:T(8,128)S(1)} %get-tuple-element.95), channel_id=1, source_target_pairs={{1,2},{2,1},{3,4},{4,3},{5,6},{6,5},{7,0},{0,7},{9,10},{10,9},{11,... | collective-permute-start | bytes 294920 | tf_op jit(solution)/shard_map/ppermute | solution.py:596
  43.2 2.2 %collective-permute-start.8 = (f32[200,256]{1,0:T(8,128)S(1)}, f32[200,256]{1,0:T(8,128)S(1)}, u32[]{:S(2)}, u32[]{:S(2)}) collective-permute-start(f32[200,256]{1,0:T(8,128)S(1)} %get-tuple-element.101), channel_id=1, source_target_pairs={{0,8},{8,0},{16,24},{24,16},{32,40},{40,32},{48,56},{56,48},{64,72... | collective-permute-start | bytes 614408 | tf_op jit(solution)/shard_map/ppermute | solution.py:596
  43.3 9.0 %collective-permute-start.10 = (f32[208,256]{1,0:T(8,128)S(1)}, f32[208,256]{1,0:T(8,128)S(1)}, u32[]{:S(2)}, u32[]{:S(2)}) collective-permute-start(f32[208,256]{1,0:T(8,128)S(1)} %get-tuple-element.105), channel_id=1, source_target_pairs={{8,16},{16,8},{24,32},{32,24},{40,48},{48,40},{56,64},{64,56},{72,... | collective-permute-start | bytes 638984 | tf_op jit(solution)/shard_map/ppermute | solution.py:596
  45.5 3.8 %collective-permute-start.9 = (f32[3,8,128]{2,1,0:T(8,128)S(1)}, f32[3,8,128]{2,1,0:T(8,128)S(1)}, u32[]{:S(2)}, u32[]{:S(2)}) collective-permute-start(f32[3,8,128]{2,1,0:T(8,128)S(1)} %shard_map.125.ours), channel_id=1, source_target_pairs={{0,1},{1,0},{2,3},{3,2},{4,5},{5,4},{6,7},{7,6},{8,9},{9,8},{10,11... | collective-permute-start | bytes 36872 | tf_op jit(solution)/shard_map/ppermute | solution.py:596
  52.3 14.9 %collective-permute-start.12 = (f32[3,2,16,256]{3,2,1,0:T(8,128)S(1)}, f32[3,2,16,256]{3,2,1,0:T(8,128)S(1)}, u32[]{:S(2)}, u32[]{:S(2)}) collective-permute-start(f32[3,2,16,256]{3,2,1,0:T(8,128)S(1)} %get-tuple-element.111), channel_id=1, source_target_pairs={{0,1},{1,0},{2,3},{3,2},{4,5},{5,4},{6,7},{7,6},{8,9},{9,8},{10,11... | collective-permute-start | bytes 294920 | tf_op jit(solution)/shard_map/ppermute | solution.py:596
  53.4 13.9 %collective-permute-start.13 = (f32[3,2,16,256]{3,2,1,0:T(8,128)S(1)}, f32[3,2,16,256]{3,2,1,0:T(8,128)S(1)}, u32[]{:S(2)}, u32[]{:S(2)}) collective-permute-start(f32[3,2,16,256]{3,2,1,0:T(8,128)S(1)} %get-tuple-element.112), channel_id=1, source_target_pairs={{1,2},{2,1},{3,4},{4,3},{5,6},{6,5},{7,0},{0,7},{9,10},{10,9},{11,... | collective-permute-start | bytes 294920 | tf_op jit(solution)/shard_map/ppermute | solution.py:596
  55.4 5.6 %collective-permute-start.11 = (f32[6,4,128]{2,1,0:T(4,128)S(1)}, f32[6,4,128]{2,1,0:T(4,128)S(1)}, u32[]{:S(2)}, u32[]{:S(2)}) collective-permute-start(f32[6,4,128]{2,1,0:T(4,128)S(1)} %shard_map.126.after.ours.token), channel_id=1, source_target_pairs={{0,64},{8,72},{16,80},{24,88},{32,96},{40,104},{48,112},{56,120},{... | collective-permute-start | bytes 36872 | tf_op jit(solution)/shard_map/ppermute | solution.py:605
  61.0 5.3 %collective-permute-start.14 = (f32[6,8,128]{2,1,0:T(8,128)S(1)}, f32[6,8,128]{2,1,0:T(8,128)S(1)}, u32[]{:S(2)}, u32[]{:S(2)}) collective-permute-start(f32[6,8,128]{2,1,0:T(8,128)S(1)} %shard_map.128.after.ours), channel_id=1, source_target_pairs={{0,32},{8,40},{16,48},{24,56},{32,0},{40,8},{48,16},{56,24},{64,96... | collective-permute-start | bytes 73736 | tf_op jit(solution)/shard_map/ppermute | solution.py:605
  66.3 5.6 %collective-permute-start.15 = (f32[6,16,128]{2,1,0:T(8,128)S(1)}, f32[6,16,128]{2,1,0:T(8,128)S(1)}, u32[]{:S(2)}, u32[]{:S(2)}) collective-permute-start(f32[6,16,128]{2,1,0:T(8,128)S(1)} %shard_map.131.after.ours), channel_id=1, source_target_pairs={{0,2},{1,3},{2,0},{3,1},{4,6},{5,7},{6,4},{7,5},{8,10},{9,11},{10,... | collective-permute-start | bytes 147464 | tf_op jit(solution)/shard_map/ppermute | solution.py:605
  71.9 4.7 %collective-permute-start.16 = (f32[6,32,128]{2,1,0:T(8,128)S(1)}, f32[6,32,128]{2,1,0:T(8,128)S(1)}, u32[]{:S(2)}, u32[]{:S(2)}) collective-permute-start(f32[6,32,128]{2,1,0:T(8,128)S(1)} %shard_map.133.ours), channel_id=1, source_target_pairs={{0,4},{1,5},{2,6},{3,7},{4,0},{5,1},{6,2},{7,3},{8,12},{9,13},{10,... | collective-permute-start | bytes 294920 | tf_op jit(solution)/shard_map/ppermute | solution.py:605
  76.6 5.8 %collective-permute-start.17 = (f32[6,64,128]{2,1,0:T(8,128)S(1)}, f32[6,64,128]{2,1,0:T(8,128)S(1)}, u32[]{:S(2)}, u32[]{:S(2)}) collective-permute-start(f32[6,64,128]{2,1,0:T(8,128)S(1)} %shard_map.134.ours), channel_id=1, source_target_pairs={{0,16},{8,24},{16,0},{24,8},{32,48},{40,56},{48,32},{56,40},{64,80... | collective-permute-start | bytes 589832 | tf_op jit(solution)/shard_map/ppermute | solution.py:605

commit v5 on v4

--- a/solution.py
+++ b/solution.py
@@ -14,7 +14,10 @@
 CHUNK = 4
 STEP = 2
 GROUP = 4
-ROUNDS = (("slab", 8), ("slab", 4), ("split", 2), ("split", 4), ("slab", 2))
+ROUNDS = (
+    (("slab", 8), ("slab", 4), ("split", 2), ("split", 4), ("slab", 2)),
+    (("slab", 8), ("split", 2), ("slab", 4), ("slab", 2), ("split", 4)),
+)
 
 DT = 0.25
 STIFF = 0.5
@@ -212,9 +215,9 @@
     mine = (slab // 2) * (splits // 2) + split // 2
     other = group ^ mine
     slot = rank
-    for order, (axis, bit) in enumerate(ROUNDS):
-        place = bit // 2 * (splits // 2 if axis == "slab" else 1)
-        slot = slot + jnp.where((other & place) != 0, GROUP << order, 0)
+    for order, ways in enumerate(zip(*ROUNDS)):
+        even, odd = [bit // 2 * (splits // 2 if axis == "slab" else 1) for axis, bit in ways]
+        slot = slot + jnp.where((other & jnp.where(even_x, even, odd)) != 0, GROUP << order, 0)
     perm[...] = jnp.where(slot == lane, 1.0, 0.0)
 
     pst[...] = jnp.zeros_like(pst)
@@ -390,11 +393,18 @@
         for c in range(3):
             for h in range(2):
                 u[c, h, x + 2, rows, :] = u_own[c, h, x + 2, rows, :]
+        return carry
+
+    def sides(k, carry):
+        x = jnp.where(k < 3, k, k + CX - 6)
+        for c in range(3):
+            for h in range(2):
                 left[c, h, x + 1, rows, :] = left_own[c, h, x + 1, rows, :]
                 right[c, h, x + 1, rows, :] = right_own[c, h, x + 1, rows, :]
         return carry
 
     lax.fori_loop(0, CX, own, 0)
+    lax.fori_loop(0, 6, sides, 0)
     for x in (1, CX + 2):
         for y in range(LO, LO + CY, 8):
             turn(u, left, right, x, y)
@@ -601,8 +611,13 @@
 
 
 def share_round(gathered, number, token):
-    axis, bit = ROUNDS[number]
-    theirs = lax.ppermute(gathered, axis, [(i, i ^ bit) for i in range(lax.axis_size(axis))])
+    slabs, splits = lax.axis_size("slab"), lax.axis_size("split")
+    pairs = []
+    for i in range(slabs):
+        axis, bit = ROUNDS[i % 2][number]
+        other, across = (i ^ bit, 0) if axis == "slab" else (i, bit)
+        pairs += [(i * splits + j, other * splits + (j ^ across)) for j in range(splits)]
+    theirs = lax.ppermute(gathered, ("slab", "split"), pairs)
     (merged,) = call(merge_kernel, (gathered, theirs, token), [rows_of(2 * gathered.shape[1])], us=0.1)
     return merged
 
@@ -683,7 +698,7 @@
         scratch=(CROSSING,),
         us=1.4,
     )
-    for number in range(2, len(ROUNDS)):
+    for number in range(2, len(ROUNDS[0])):
         gathered = share_round(gathered, number, token)
     final_pos, final_vel = call(final_kernel, (perm, gathered), [jax.ShapeDtypeStruct(pp.shape, F32)] * 2)
     return (

time: 83.3 us -> 83.9 us (level)
  waiting for transfers between devices: 23.3 us -> 24.3 us
    ppermute x13, waiting for transfers between devices: 7.12 us -> 9 us  [swap(): return lax.ppermute(value, axis, pairs)]
    ppermute x13, starting transfers between devices: 22.4 us -> 21.2 us  [swap(): return lax.ppermute(value, axis, pairs)]
    ppermute x5, waiting for transfers between devices: 16.2 us -> 15.3 us  [share_round(): theirs = lax.ppermute(gathered, ('slab', 'split'), pairs)]
    ppermute x5, starting transfers between devices: 3.61 us -> 4.46 us  [share_round(): theirs = lax.ppermute(gathered, ('slab', 'split'), pairs)]
  transfers between devices with their start and end apart: 18 -> 18, of which waited for: 9 -> 10; matrix products, arithmetic and copies ran while one was open for 0% -> 0% of each run, Pallas kernels for 31% -> 31%
where the time goes in v5:
time: 83.9 us; the launch traced here: 84.2 us
  Pallas kernels  33.3 us (40%)
  starting transfers between devices  25.7 us (31%)
  waiting for transfers between devices  24.3 us (29%)
  between operations  0.87 us (1%)
    pallas_call x26, Pallas kernels, call(): pl.pallas_call(kernel, out_shape=outputs, in_specs=ins or [SMEM] * scalar...  33.3 us
    ppermute x13, starting transfers between devices, swap(): return lax.ppermute(value, axis, pairs)  21.2 us
    ppermute x5, waiting for transfers between devices, share_round(): theirs = lax.ppermute(gathered, ('slab', 'split'), pairs)  15.3 us
    ppermute x13, waiting for transfers between devices, swap(): return lax.ppermute(value, axis, pairs)  9 us
    ppermute x5, starting transfers between devices, share_round(): theirs = lax.ppermute(gathered, ('slab', 'split'), pairs)  4.46 us
  transfers between devices with their start and end apart: 18, of which 10 were waited for; matrix products, arithmetic and copies ran while one was open for 0% of the time, Pallas kernels for 31%

profile of v5, /device:TPU:0, one launch (start us, length us, event | category | flops | bytes accessed | tf_op | source)
XLA Modules:
  0.0 84.2 jit_solution(8173801523952988474)
XLA Ops:
  0.6 2.7 %shard_map.111 = (f32[3,2,12,48,128]{4,3,2,1,0:T(8,128)S(1)}, f32[3,8,32,256]{3,2,1,0:T(8,128)S(1)}, f32[7,8,128]{2,1,0:T(8,128)S(1)}, f32[128,128]{1,0:T(8,128)...) custom-call(f32[3,8,32,256]{3,2,1,0:T(8,128)} %u.1, ...), custom_call_target="tpu_custom_call" | custom-call | bytes 3000000 | tf_op jit(solution)/shard_map/pallas_call | solution.py:590
  3.3 6.3 %collective-permute-start.1 = (f32[208,256]{1,0:T(8,128)S(1)}, f32[208,256]{1,0:T(8,128)S(1)}, u32[]{:S(2)}, u32[]{:S(2)}) collective-permute-start(f32[208,256]{1,0:T(8,128)S(1)} %get-tuple-element.68), channel_id=1, source_target_pairs={{8,16},{16,8},{24,32},{32,24},{40,48},{48,40},{56,64},{64,56},{72,... | collective-permute-start | bytes 638984 | tf_op jit(solution)/shard_map/ppermute | solution.py:606
  9.6 2.6 %shard_map.114 = (f32[3,8,32,128]{3,2,1,0:T(8,128)S(1)}, f32[3,8,128]{2,1,0:T(8,128)S(1)}, f32[200,256]{1,0:T(8,128)S(1)}) custom-call(s32[3,2,16]{2,1,0:T(2,128)S(1)} %copy-done.1, f32[3,2,12,48,128]{4,3,2,1,0:T(8,128)S(1)} %get-tuple-element.62.u.u_ref.u_own, f32[7,8,128]{2,1,0:T(8,128)S(1)} %get-tuple-element.66.pst), custom_call_target="tpu_custom_call" | custom-call | bytes 4500000 | tf_op jit(solution)/shard_map/pallas_call | solution.py:590
  12.4 3.6 %shard_map.113 = (f32[3,4,32,256]{3,2,1,0:T(8,128)S(1)}, f32[3,2,10,48,128]{4,3,2,1,0:T(8,128)S(1)}, f32[3,2,10,48,128]{4,3,2,1,0:T(8,128)S(1)}, f32[8,128]{1,0:T(8,128)S(1)}) custom-call(f32[3,2,12,48,128]{4,3,2,1,0:T(8,128)S(1)} %get-tuple-element.62.u.u_ref.u_own, f32[3,8,32,256]{3,2,1,0:T(8,128)S(1)} %get-tuple-element.63.half, ...), custom_call_target="tpu_custom_call" | custom-call | bytes 10800000 | tf_op jit(solution)/shard_map/pallas_call | solution.py:590
  17.2 3.1 %collective-permute-start.3 = (f32[3,2,16,256]{3,2,1,0:T(8,128)S(1)}, f32[3,2,16,256]{3,2,1,0:T(8,128)S(1)}, u32[]{:S(2)}, u32[]{:S(2)}) collective-permute-start(f32[3,2,16,256]{3,2,1,0:T(8,128)S(1)} %get-tuple-element.78), channel_id=1, source_target_pairs={{1,2},{2,1},{3,4},{4,3},{5,6},{6,5},{7,0},{0,7},{9,10},{10,9},{11,... | collective-permute-start | bytes 294920 | tf_op jit(solution)/shard_map/ppermute | solution.py:606
  20.3 3.6 %shard_map.115 = (f32[3,4,32,256]{3,2,1,0:T(8,128)S(1)}, f32[8,128]{1,0:T(8,128)}) custom-call(f32[200,256]{1,0:T(8,128)S(1)} %collective-permute-done.xa, f32[208,256]{1,0:T(8,128)S(1)} %collective-permute-done.1.xb, f32[3,2,12,48,128]{4,3,2,1,0:T(8,128)S(1)} %get-tuple-element.62.u.u_ref.u_own, f32[3,2,10,48,128]{4,3,2,1,0:T(8,128)S(1)} %get-tuple-element.69.left_own, ...), custom_call_target="tpu_custom_call" | custom-call | bytes 10800000 | tf_op jit(solution)/shard_map/pallas_call | solution.py:590
  24.7 1.8 %collective-permute-start.5 = (f32[208,256]{1,0:T(8,128)S(1)}, f32[208,256]{1,0:T(8,128)S(1)}, u32[]{:S(2)}, u32[]{:S(2)}) collective-permute-start(f32[208,256]{1,0:T(8,128)S(1)} %get-tuple-element.85), channel_id=1, source_target_pairs={{8,16},{16,8},{24,32},{32,24},{40,48},{48,40},{56,64},{64,56},{72,... | collective-permute-start | bytes 638984 | tf_op jit(solution)/shard_map/ppermute | solution.py:606
  27.2 3.6 %shard_map.118 = (f32[3,4,32,256]{3,2,1,0:T(8,128)S(1)}, f32[3,2,10,48,128]{4,3,2,1,0:T(8,128)S(1)}, f32[3,2,10,48,128]{4,3,2,1,0:T(8,128)S(1)}, f32[8,128]{1,0:T(8,128)S(1)}) custom-call(f32[3,2,12,48,128]{4,3,2,1,0:T(8,128)S(1)} %get-tuple-element.80.u.u_ref.u_own, f32[3,8,32,256]{3,2,1,0:T(8,128)S(1)} %get-tuple-element.81.half, ...), custom_call_target="tpu_custom_call" | custom-call | bytes 10800000 | tf_op jit(solution)/shard_map/pallas_call | solution.py:590
  30.9 2.8 %collective-permute-done.5.xb = f32[208,256]{1,0:T(8,128)S(1)} collective-permute-done((f32[208,256]{1,0:T(8,128)S(1)}, f32[208,256]{1,0:T(8,128)S(1)}, u32[]{:S(2)}, u32[]{:S(2)}) %collective-permute-start.5) | collective-permute-done | bytes 213024 | tf_op jit(solution)/shard_map/ppermute | solution.py:606
  33.9 3.0 %collective-permute-start.7 = (f32[3,2,16,256]{3,2,1,0:T(8,128)S(1)}, f32[3,2,16,256]{3,2,1,0:T(8,128)S(1)}, u32[]{:S(2)}, u32[]{:S(2)}) collective-permute-start(f32[3,2,16,256]{3,2,1,0:T(8,128)S(1)} %get-tuple-element.95), channel_id=1, source_target_pairs={{1,2},{2,1},{3,4},{4,3},{5,6},{6,5},{7,0},{0,7},{9,10},{10,9},{11,... | collective-permute-start | bytes 294920 | tf_op jit(solution)/shard_map/ppermute | solution.py:606
  37.0 3.6 %shard_map.120 = (f32[3,4,32,256]{3,2,1,0:T(8,128)S(1)}, f32[8,128]{1,0:T(8,128)}) custom-call(f32[200,256]{1,0:T(8,128)S(1)} %collective-permute-done.4.xa, f32[208,256]{1,0:T(8,128)S(1)} %collective-permute-done.5.xb, f32[3,2,12,48,128]{4,3,2,1,0:T(8,128)S(1)} %get-tuple-element.80.u.u_ref.u_own, f32[3,2,10,48,128]{4,3,2,1,0:T(8,128)S(1)} %get-tuple-element.86.left_own, ...), custom_call_target="tpu_custom_call" | custom-call | bytes 10800000 | tf_op jit(solution)/shard_map/pallas_call | solution.py:590
  41.2 2.6 %shard_map.124 = (f32[3,8,32,128]{3,2,1,0:T(8,128)S(1)}, f32[3,8,128]{2,1,0:T(8,128)S(1)}, f32[200,256]{1,0:T(8,128)S(1)}) custom-call(s32[3,2,16]{2,1,0:T(2,128)S(1)} %copy-done.1, f32[3,2,12,48,128]{4,3,2,1,0:T(8,128)S(1)} %get-tuple-element.96.u.u_ref.u_own, f32[7,8,128]{2,1,0:T(8,128)S(1)} %get-tuple-element.100.pst), custom_call_target="tpu_custom_call" | custom-call | bytes 4500000 | tf_op jit(solution)/shard_map/pallas_call | solution.py:590
  43.9 1.6 %collective-permute-start.10 = (f32[208,256]{1,0:T(8,128)S(1)}, f32[208,256]{1,0:T(8,128)S(1)}, u32[]{:S(2)}, u32[]{:S(2)}) collective-permute-start(f32[208,256]{1,0:T(8,128)S(1)} %get-tuple-element.105), channel_id=1, source_target_pairs={{8,16},{16,8},{24,32},{32,24},{40,48},{48,40},{56,64},{64,56},{72,... | collective-permute-start | bytes 638984 | tf_op jit(solution)/shard_map/ppermute | solution.py:606
  47.1 2.2 %collective-permute-done.9.theirs = f32[3,8,128]{2,1,0:T(8,128)S(1)} collective-permute-done((f32[3,8,128]{2,1,0:T(8,128)S(1)}, f32[3,8,128]{2,1,0:T(8,128)S(1)}, u32[]{:S(2)}, u32[]{:S(2)}) %collective-permute-start.9) | collective-permute-done | bytes 12320 | tf_op jit(solution)/shard_map/ppermute | solution.py:606
  49.3 3.6 %collective-permute-done.10.xb = f32[208,256]{1,0:T(8,128)S(1)} collective-permute-done((f32[208,256]{1,0:T(8,128)S(1)}, f32[208,256]{1,0:T(8,128)S(1)}, u32[]{:S(2)}, u32[]{:S(2)}) %collective-permute-start.10) | collective-permute-done | bytes 213024 | tf_op jit(solution)/shard_map/ppermute | solution.py:606
  53.4 2.6 %collective-permute-start.13 = (f32[3,2,16,256]{3,2,1,0:T(8,128)S(1)}, f32[3,2,16,256]{3,2,1,0:T(8,128)S(1)}, u32[]{:S(2)}, u32[]{:S(2)}) collective-permute-start(f32[3,2,16,256]{3,2,1,0:T(8,128)S(1)} %get-tuple-element.112), channel_id=1, source_target_pairs={{1,2},{2,1},{3,4},{4,3},{5,6},{6,5},{7,0},{0,7},{9,10},{10,9},{11,... | collective-permute-start | bytes 294920 | tf_op jit(solution)/shard_map/ppermute | solution.py:606
  56.0 1.8 %collective-permute-start.11 = (f32[6,4,128]{2,1,0:T(4,128)S(1)}, f32[6,4,128]{2,1,0:T(4,128)S(1)}, u32[]{:S(2)}, u32[]{:S(2)}) collective-permute-start(f32[6,4,128]{2,1,0:T(4,128)S(1)} %shard_map.126.after.ours.token), channel_id=1, source_target_pairs={{0,64},{1,65},{2,66},{3,67},{4,68},{5,69},{6,70},{7,71},{8,72},{9,... | collective-permute-start | bytes 36872 | tf_op jit(solution)/shard_map/ppermute | solution.py:620
  57.8 2.6 %shard_map.127 = (f32[3,4,32,256]{3,2,1,0:T(8,128)S(1)}, f32[8,128]{1,0:T(8,128)S(1)}) custom-call(f32[3,2,12,48,128]{4,3,2,1,0:T(8,128)S(1)} %get-tuple-element.96.u.u_ref.u_own, f32[3,2,10,48,128]{4,3,2,1,0:T(8,128)S(1)} %get-tuple-element.97.left.left_own, f32[3,2,10,48,128]{4,3,2,1,0:T(8,128)S(1)} %get-tuple-element.98.right.right_own, ...), custom_call_target="tpu_custom_call" | custom-call | bytes 7800000 | tf_op jit(solution)/shard_map/pallas_call | solution.py:590
  61.2 3.0 %shard_map.129 = (f32[3,4,32,256]{3,2,1,0:T(8,128)S(1)}, f32[8,128]{1,0:T(8,128)S(1)}) custom-call(f32[200,256]{1,0:T(8,128)S(1)} %collective-permute-done.8.xa, f32[208,256]{1,0:T(8,128)S(1)} %collective-permute-done.10.xb, f32[3,2,12,48,128]{4,3,2,1,0:T(8,128)S(1)} %get-tuple-element.96.u.u_ref.u_own, ...), custom_call_target="tpu_custom_call" | custom-call | bytes 10800000 | tf_op jit(solution)/shard_map/pallas_call | solution.py:590
  64.2 2.3 %collective-permute-done.14.theirs = f32[6,8,128]{2,1,0:T(8,128)S(1)} collective-permute-done((f32[6,8,128]{2,1,0:T(8,128)S(1)}, f32[6,8,128]{2,1,0:T(8,128)S(1)}, u32[]{:S(2)}, u32[]{:S(2)}) %collective-permute-start.14) | collective-permute-done | bytes 24608 | tf_op jit(solution)/shard_map/ppermute | solution.py:620
  67.8 1.5 %shard_map.132 = (f32[3,8,32,256]{3,2,1,0:T(8,128)}, f32[3,8,32,256]{3,2,1,0:T(8,128)}, f32[8,128]{1,0:T(8,128)S(1)}) custom-call(f32[3,2,12,48,128]{4,3,2,1,0:T(8,128)S(1)} %get-tuple-element.96.u.u_ref.u_own, f32[3,4,32,256]{3,2,1,0:T(8,128)S(1)} %get-tuple-element.104.inner, f32[3,4,32,256]{3,2,1,0:T(8,128)S(1)} %get-tuple-element.107.edge, ...), custom_call_target="tpu_custom_call" | custom-call | bytes 4200000 | tf_op jit(solution)/shard_map/pallas_call | solution.py:590
  69.3 2.9 %collective-permute-done.15.theirs = f32[6,16,128]{2,1,0:T(8,128)S(1)} collective-permute-done((f32[6,16,128]{2,1,0:T(8,128)S(1)}, f32[6,16,128]{2,1,0:T(8,128)S(1)}, u32[]{:S(2)}, u32[]{:S(2)}) %collective-permute-start.15) | collective-permute-done | bytes 49184 | tf_op jit(solution)/shard_map/ppermute | solution.py:620
  73.4 3.7 %collective-permute-done.16.theirs = f32[6,32,128]{2,1,0:T(8,128)S(1)} collective-permute-done((f32[6,32,128]{2,1,0:T(8,128)S(1)}, f32[6,32,128]{2,1,0:T(8,128)S(1)}, u32[]{:S(2)}, u32[]{:S(2)}) %collective-permute-start.16) | collective-permute-done | bytes 98336 | tf_op jit(solution)/shard_map/ppermute | solution.py:620
  77.3 5.7 %collective-permute-done.17.theirs = f32[6,64,128]{2,1,0:T(8,128)S(1)} collective-permute-done((f32[6,64,128]{2,1,0:T(8,128)S(1)}, f32[6,64,128]{2,1,0:T(8,128)S(1)}, u32[]{:S(2)}, u32[]{:S(2)}) %collective-permute-start.17) | collective-permute-done | bytes 196640 | tf_op jit(solution)/shard_map/ppermute | solution.py:620
  (42 shorter events, 10.7 us)
Async XLA Ops:
  0.6 9.0 %copy-start.1 = (s32[3,2,16]{2,1,0:T(2,128)S(1)}, s32[3,2,16]{2,1,0:T(2,128)}, u32[]{:S(2)}) copy-start(s32[3,2,16]{2,1,0:T(2,128)} %pairs.5) | copy-start | bytes 1156
  3.3 9.0 %copy-start = (s32[4,8,32,256]{3,2,1,0:T(8,128)S(1)}, s32[4,8,32,256]{3,2,1,0:T(8,128)}, u32[]{:S(2)}) copy-start(s32[4,8,32,256]{3,2,1,0:T(8,128)} %masks.1) | copy-start | bytes 3145732
  3.3 12.7 %collective-permute-start.1 = (f32[208,256]{1,0:T(8,128)S(1)}, f32[208,256]{1,0:T(8,128)S(1)}, u32[]{:S(2)}, u32[]{:S(2)}) collective-permute-start(f32[208,256]{1,0:T(8,128)S(1)} %get-tuple-element.68), channel_id=1, source_target_pairs={{8,16},{16,8},{24,32},{32,24},{40,48},{48,40},{56,64},{64,56},{72,... | collective-permute-start | bytes 638984 | tf_op jit(solution)/shard_map/ppermute | solution.py:606
  12.2 3.8 %collective-permute-start = (f32[200,256]{1,0:T(8,128)S(1)}, f32[200,256]{1,0:T(8,128)S(1)}, u32[]{:S(2)}, u32[]{:S(2)}) collective-permute-start(f32[200,256]{1,0:T(8,128)S(1)} %get-tuple-element.67), channel_id=1, source_target_pairs={{0,8},{8,0},{16,24},{24,16},{32,40},{40,32},{48,56},{56,48},{64,72... | collective-permute-start | bytes 614408 | tf_op jit(solution)/shard_map/ppermute | solution.py:606
  16.1 7.8 %collective-permute-start.2 = (f32[3,2,16,256]{3,2,1,0:T(8,128)S(1)}, f32[3,2,16,256]{3,2,1,0:T(8,128)S(1)}, u32[]{:S(2)}, u32[]{:S(2)}) collective-permute-start(f32[3,2,16,256]{3,2,1,0:T(8,128)S(1)} %get-tuple-element.77), channel_id=1, source_target_pairs={{0,1},{1,0},{2,3},{3,2},{4,5},{5,4},{6,7},{7,6},{8,9},{9,8},{10,11... | collective-permute-start | bytes 294920 | tf_op jit(solution)/shard_map/ppermute | solution.py:606
  17.2 7.0 %collective-permute-start.3 = (f32[3,2,16,256]{3,2,1,0:T(8,128)S(1)}, f32[3,2,16,256]{3,2,1,0:T(8,128)S(1)}, u32[]{:S(2)}, u32[]{:S(2)}) collective-permute-start(f32[3,2,16,256]{3,2,1,0:T(8,128)S(1)} %get-tuple-element.78), channel_id=1, source_target_pairs={{1,2},{2,1},{3,4},{4,3},{5,6},{6,5},{7,0},{0,7},{9,10},{10,9},{11,... | collective-permute-start | bytes 294920 | tf_op jit(solution)/shard_map/ppermute | solution.py:606
  24.7 9.0 %collective-permute-start.5 = (f32[208,256]{1,0:T(8,128)S(1)}, f32[208,256]{1,0:T(8,128)S(1)}, u32[]{:S(2)}, u32[]{:S(2)}) collective-permute-start(f32[208,256]{1,0:T(8,128)S(1)} %get-tuple-element.85), channel_id=1, source_target_pairs={{8,16},{16,8},{24,32},{32,24},{40,48},{48,40},{56,64},{64,56},{72,... | collective-permute-start | bytes 638984 | tf_op jit(solution)/shard_map/ppermute | solution.py:606
  27.1 3.7 %collective-permute-start.4 = (f32[200,256]{1,0:T(8,128)S(1)}, f32[200,256]{1,0:T(8,128)S(1)}, u32[]{:S(2)}, u32[]{:S(2)}) collective-permute-start(f32[200,256]{1,0:T(8,128)S(1)} %get-tuple-element.84), channel_id=1, source_target_pairs={{0,8},{8,0},{16,24},{24,16},{32,40},{40,32},{48,56},{56,48},{64,72... | collective-permute-start | bytes 614408 | tf_op jit(solution)/shard_map/ppermute | solution.py:606
  33.7 6.8 %collective-permute-start.6 = (f32[3,2,16,256]{3,2,1,0:T(8,128)S(1)}, f32[3,2,16,256]{3,2,1,0:T(8,128)S(1)}, u32[]{:S(2)}, u32[]{:S(2)}) collective-permute-start(f32[3,2,16,256]{3,2,1,0:T(8,128)S(1)} %get-tuple-element.94), channel_id=1, source_target_pairs={{0,1},{1,0},{2,3},{3,2},{4,5},{5,4},{6,7},{7,6},{8,9},{9,8},{10,11... | collective-permute-start | bytes 294920 | tf_op jit(solution)/shard_map/ppermute | solution.py:606
  33.9 6.7 %collective-permute-start.7 = (f32[3,2,16,256]{3,2,1,0:T(8,128)S(1)}, f32[3,2,16,256]{3,2,1,0:T(8,128)S(1)}, u32[]{:S(2)}, u32[]{:S(2)}) collective-permute-start(f32[3,2,16,256]{3,2,1,0:T(8,128)S(1)} %get-tuple-element.95), channel_id=1, source_target_pairs={{1,2},{2,1},{3,4},{4,3},{5,6},{6,5},{7,0},{0,7},{9,10},{10,9},{11,... | collective-permute-start | bytes 294920 | tf_op jit(solution)/shard_map/ppermute | solution.py:606
  43.8 1.7 %collective-permute-start.8 = (f32[200,256]{1,0:T(8,128)S(1)}, f32[200,256]{1,0:T(8,128)S(1)}, u32[]{:S(2)}, u32[]{:S(2)}) collective-permute-start(f32[200,256]{1,0:T(8,128)S(1)} %get-tuple-element.101), channel_id=1, source_target_pairs={{0,8},{8,0},{16,24},{24,16},{32,40},{40,32},{48,56},{56,48},{64,72... | collective-permute-start | bytes 614408 | tf_op jit(solution)/shard_map/ppermute | solution.py:606
  43.9 9.0 %collective-permute-start.10 = (f32[208,256]{1,0:T(8,128)S(1)}, f32[208,256]{1,0:T(8,128)S(1)}, u32[]{:S(2)}, u32[]{:S(2)}) collective-permute-start(f32[208,256]{1,0:T(8,128)S(1)} %get-tuple-element.105), channel_id=1, source_target_pairs={{8,16},{16,8},{24,32},{32,24},{40,48},{48,40},{56,64},{64,56},{72,... | collective-permute-start | bytes 638984 | tf_op jit(solution)/shard_map/ppermute | solution.py:606
  45.5 3.8 %collective-permute-start.9 = (f32[3,8,128]{2,1,0:T(8,128)S(1)}, f32[3,8,128]{2,1,0:T(8,128)S(1)}, u32[]{:S(2)}, u32[]{:S(2)}) collective-permute-start(f32[3,8,128]{2,1,0:T(8,128)S(1)} %shard_map.125.ours), channel_id=1, source_target_pairs={{0,1},{1,0},{2,3},{3,2},{4,5},{5,4},{6,7},{7,6},{8,9},{9,8},{10,11... | collective-permute-start | bytes 36872 | tf_op jit(solution)/shard_map/ppermute | solution.py:606
  52.9 14.9 %collective-permute-start.12 = (f32[3,2,16,256]{3,2,1,0:T(8,128)S(1)}, f32[3,2,16,256]{3,2,1,0:T(8,128)S(1)}, u32[]{:S(2)}, u32[]{:S(2)}) collective-permute-start(f32[3,2,16,256]{3,2,1,0:T(8,128)S(1)} %get-tuple-element.111), channel_id=1, source_target_pairs={{0,1},{1,0},{2,3},{3,2},{4,5},{5,4},{6,7},{7,6},{8,9},{9,8},{10,11... | collective-permute-start | bytes 294920 | tf_op jit(solution)/shard_map/ppermute | solution.py:606
  53.4 14.4 %collective-permute-start.13 = (f32[3,2,16,256]{3,2,1,0:T(8,128)S(1)}, f32[3,2,16,256]{3,2,1,0:T(8,128)S(1)}, u32[]{:S(2)}, u32[]{:S(2)}) collective-permute-start(f32[3,2,16,256]{3,2,1,0:T(8,128)S(1)} %get-tuple-element.112), channel_id=1, source_target_pairs={{1,2},{2,1},{3,4},{4,3},{5,6},{6,5},{7,0},{0,7},{9,10},{10,9},{11,... | collective-permute-start | bytes 294920 | tf_op jit(solution)/shard_map/ppermute | solution.py:606
  56.0 5.2 %collective-permute-start.11 = (f32[6,4,128]{2,1,0:T(4,128)S(1)}, f32[6,4,128]{2,1,0:T(4,128)S(1)}, u32[]{:S(2)}, u32[]{:S(2)}) collective-permute-start(f32[6,4,128]{2,1,0:T(4,128)S(1)} %shard_map.126.after.ours.token), channel_id=1, source_target_pairs={{0,64},{1,65},{2,66},{3,67},{4,68},{5,69},{6,70},{7,71},{8,72},{9,... | collective-permute-start | bytes 36872 | tf_op jit(solution)/shard_map/ppermute | solution.py:620
  61.2 5.3 %collective-permute-start.14 = (f32[6,8,128]{2,1,0:T(8,128)S(1)}, f32[6,8,128]{2,1,0:T(8,128)S(1)}, u32[]{:S(2)}, u32[]{:S(2)}) collective-permute-start(f32[6,8,128]{2,1,0:T(8,128)S(1)} %shard_map.128.after.ours), channel_id=1, source_target_pairs={{0,32},{1,33},{2,34},{3,35},{4,36},{5,37},{6,38},{7,39},{8,10},{9,... | collective-permute-start | bytes 73736 | tf_op jit(solution)/shard_map/ppermute | solution.py:620
  66.5 5.6 %collective-permute-start.15 = (f32[6,16,128]{2,1,0:T(8,128)S(1)}, f32[6,16,128]{2,1,0:T(8,128)S(1)}, u32[]{:S(2)}, u32[]{:S(2)}) collective-permute-start(f32[6,16,128]{2,1,0:T(8,128)S(1)} %shard_map.131.after.ours), channel_id=1, source_target_pairs={{0,2},{1,3},{2,0},{3,1},{4,6},{5,7},{6,4},{7,5},{8,40},{9,41},{10,... | collective-permute-start | bytes 147464 | tf_op jit(solution)/shard_map/ppermute | solution.py:620
  72.1 5.0 %collective-permute-start.16 = (f32[6,32,128]{2,1,0:T(8,128)S(1)}, f32[6,32,128]{2,1,0:T(8,128)S(1)}, u32[]{:S(2)}, u32[]{:S(2)}) collective-permute-start(f32[6,32,128]{2,1,0:T(8,128)S(1)} %shard_map.133.ours), channel_id=1, source_target_pairs={{0,4},{1,5},{2,6},{3,7},{4,0},{5,1},{6,2},{7,3},{8,24},{9,25},{10,... | collective-permute-start | bytes 294920 | tf_op jit(solution)/shard_map/ppermute | solution.py:620
  77.2 5.8 %collective-permute-start.17 = (f32[6,64,128]{2,1,0:T(8,128)S(1)}, f32[6,64,128]{2,1,0:T(8,128)S(1)}, u32[]{:S(2)}, u32[]{:S(2)}) collective-permute-start(f32[6,64,128]{2,1,0:T(8,128)S(1)} %shard_map.134.ours), channel_id=1, source_target_pairs={{0,16},{1,17},{2,18},{3,19},{4,20},{5,21},{6,22},{7,23},{8,12},{9,... | collective-permute-start | bytes 589832 | tf_op jit(solution)/shard_map/ppermute | solution.py:620

commit v6 on v5

--- a/solution.py
+++ b/solution.py
@@ -535,10 +535,11 @@
         out[3 + c] = (pst[3 + c] + 0.5 * DT * acc)[0:GROUP]
 
 
-def merge_kernel(ours, theirs, token, out):
-    count = ours.shape[1]
-    out[:, 0:count] = ours[...]
-    out[:, count : 2 * count] = theirs[...]
+def merge_kernel(*refs):
+    *parts, token, out = refs
+    count = parts[0].shape[1]
+    for k, part in enumerate(parts):
+        out[:, k * count : (k + 1) * count] = part[...]
 
 
 def last_kernel(u, inner, edge, surface, ya_own, yb_own, ya, yb, rim, after, u_out, v_out, token, crossing):
@@ -554,12 +555,13 @@
     token[...] = crossing[0, 0, 0]
 
 
-def final_kernel(perm, gathered, pos_out, vel_out):
+def final_kernel(perm, *refs):
+    *parts, token, pos_out, vel_out = refs
     for c in range(3):
         for at, out in ((c, pos_out), (3 + c, vel_out)):
             out[c] = jnp.dot(
                 perm[...],
-                gathered[at],
+                jnp.concatenate([part[at] for part in parts], axis=0),
                 precision=lax.Precision.HIGHEST,
                 preferred_element_type=F32,
             )
@@ -610,15 +612,27 @@
     return jax.ShapeDtypeStruct((6, count, 128), F32)
 
 
-def share_round(gathered, number, token):
+def swapped(gathered, rounds):
     slabs, splits = lax.axis_size("slab"), lax.axis_size("split")
     pairs = []
     for i in range(slabs):
-        axis, bit = ROUNDS[i % 2][number]
-        other, across = (i ^ bit, 0) if axis == "slab" else (i, bit)
-        pairs += [(i * splits + j, other * splits + (j ^ across)) for j in range(splits)]
-    theirs = lax.ppermute(gathered, ("slab", "split"), pairs)
-    (merged,) = call(merge_kernel, (gathered, theirs, token), [rows_of(2 * gathered.shape[1])], us=0.1)
+        for j in range(splits):
+            place = {"slab": i, "split": j}
+            for number in rounds:
+                axis, bit = ROUNDS[i % 2][number]
+                place[axis] ^= bit
+            pairs.append((i * splits + j, place["slab"] * splits + place["split"]))
+    return lax.ppermute(gathered, ("slab", "split"), pairs)
+
+
+def shared(gathered, first, count):
+    subsets = [[first + k for k in range(count) if number >> k & 1] for number in range(1, 1 << count)]
+    return [gathered] + [swapped(gathered, rounds) for rounds in subsets]
+
+
+def merge(parts, token):
+    rows = sum(part.shape[1] for part in parts)
+    (merged,) = call(merge_kernel, (*parts, token), [rows_of(rows)], us=0.1)
     return merged
 
 
@@ -672,7 +686,7 @@
         ya, yb = call(corner_kernel, (ya_own, yb_own, xa, xb, own_force, after), [YA, YA], us=0.1)
         ya, yb = swap(ya, "split", 0), swap(yb, "split", 1)
         if last:
-            gathered = after = share_round(gathered, 0, token)
+            gathered = after = merge(shared(gathered, 0, 1), token)
         edge, token = call(
             functools.partial(edge_kernel, scale),
             (xa, xb, u, left, right, half, words, after),
@@ -690,7 +704,7 @@
             us=1.3,
         )
 
-    gathered = share_round(gathered, 1, token)
+    gathered = merge(shared(gathered, 1, 2), token)
     final_u, final_v, token = call(
         last_kernel,
         (u, inner, edge, surface, ya_own, yb_own, ya, yb, rim, gathered),
@@ -698,9 +712,11 @@
         scratch=(CROSSING,),
         us=1.4,
     )
-    for number in range(2, len(ROUNDS[0])):
-        gathered = share_round(gathered, number, token)
-    final_pos, final_vel = call(final_kernel, (perm, gathered), [jax.ShapeDtypeStruct(pp.shape, F32)] * 2)
+    final_pos, final_vel = call(
+        final_kernel,
+        (perm, *shared(gathered, 3, 2), token),
+        [jax.ShapeDtypeStruct(pp.shape, F32)] * 2,
+    )
     return (
         final_u,
         final_v,

time: 83.9 us -> 76.1 us (0.907)
  waiting for transfers between devices: 24.3 us -> 11.9 us
  starting transfers between devices: 25.7 us -> 28.4 us
  Pallas kernels: 33.3 us -> 34.8 us
    ppermute x5 -> x7, waiting for transfers between devices: 15.3 us -> 4.98 us  [swapped(): return lax.ppermute(gathered, ('slab', 'split'), pairs)]
    ppermute x5 -> x7, starting transfers between devices: 4.46 us -> 10.3 us  [swapped(): return lax.ppermute(gathered, ('slab', 'split'), pairs)]
    ppermute x13, starting transfers between devices: 21.2 us -> 18.1 us  [swap(): return lax.ppermute(value, axis, pairs)]
    ppermute x13, waiting for transfers between devices: 9 us -> 6.94 us  [swap(): return lax.ppermute(value, axis, pairs)]
    pallas_call x26 -> x23, Pallas kernels: 33.3 us -> 34.8 us  [call(): pl.pallas_call(kernel, out_shape=outputs, in_specs=ins or [SMEM] * scalar...]
  transfers between devices with their start and end apart: 18 -> 20, of which waited for: 10 -> 6; matrix products, arithmetic and copies ran while one was open for 0% -> 0% of each run, Pallas kernels for 31% -> 36%
where the time goes in v6:
time: 76.1 us
  Pallas kernels  34.8 us (46%)
  starting transfers between devices  28.4 us (37%)
  waiting for transfers between devices  11.9 us (16%)
  between operations  0.92 us (1%)
    pallas_call x23, Pallas kernels, call(): pl.pallas_call(kernel, out_shape=outputs, in_specs=ins or [SMEM] * scalar...  34.8 us
    ppermute x13, starting transfers between devices, swap(): return lax.ppermute(value, axis, pairs)  18.1 us
    ppermute x7, starting transfers between devices, swapped(): return lax.ppermute(gathered, ('slab', 'split'), pairs)  10.3 us
    ppermute x13, waiting for transfers between devices, swap(): return lax.ppermute(value, axis, pairs)  6.94 us
    ppermute x7, waiting for transfers between devices, swapped(): return lax.ppermute(gathered, ('slab', 'split'), pairs)  4.98 us
  transfers between devices with their start and end apart: 20, of which 6 were waited for; matrix products, arithmetic and copies ran while one was open for 0% of the time, Pallas kernels for 36%

profile of v6, /device:TPU:0, one launch (start us, length us, event | category | flops | bytes accessed | tf_op | source)
XLA Modules:
  0.0 76.1 jit_solution(13229800381833904491)
XLA Ops:
  0.6 2.7 %shard_map.111 = (f32[3,2,12,48,128]{4,3,2,1,0:T(8,128)S(1)}, f32[3,8,32,256]{3,2,1,0:T(8,128)S(1)}, f32[7,8,128]{2,1,0:T(8,128)S(1)}, f32[128,128]{1,0:T(8,128)...) custom-call(f32[3,8,32,256]{3,2,1,0:T(8,128)} %u.1, ...), custom_call_target="tpu_custom_call" | custom-call | bytes 3000000 | tf_op jit(solution)/shard_map/pallas_call | solution.py:592
  3.3 6.3 %collective-permute-start.1 = (f32[208,256]{1,0:T(8,128)S(1)}, f32[208,256]{1,0:T(8,128)S(1)}, u32[]{:S(2)}, u32[]{:S(2)}) collective-permute-start(f32[208,256]{1,0:T(8,128)S(1)} %get-tuple-element.68), channel_id=1, source_target_pairs={{8,16},{16,8},{24,32},{32,24},{40,48},{48,40},{56,64},{64,56},{72,... | collective-permute-start | bytes 638984 | tf_op jit(solution)/shard_map/ppermute | solution.py:608
  9.6 2.2 %shard_map.114 = (f32[3,8,32,128]{3,2,1,0:T(8,128)S(1)}, f32[3,8,128]{2,1,0:T(8,128)S(1)}, f32[200,256]{1,0:T(8,128)S(1)}) custom-call(s32[3,2,16]{2,1,0:T(2,128)S(1)} %copy-done.1, f32[3,2,12,48,128]{4,3,2,1,0:T(8,128)S(1)} %get-tuple-element.62.u.u_ref.u_own, f32[7,8,128]{2,1,0:T(8,128)S(1)} %get-tuple-element.66.pst), custom_call_target="tpu_custom_call" | custom-call | bytes 4500000 | tf_op jit(solution)/shard_map/pallas_call | solution.py:592
  12.0 3.6 %shard_map.113 = (f32[3,4,32,256]{3,2,1,0:T(8,128)S(1)}, f32[3,2,10,48,128]{4,3,2,1,0:T(8,128)S(1)}, f32[3,2,10,48,128]{4,3,2,1,0:T(8,128)S(1)}, f32[8,128]{1,0:T(8,128)S(1)}) custom-call(f32[3,2,12,48,128]{4,3,2,1,0:T(8,128)S(1)} %get-tuple-element.62.u.u_ref.u_own, f32[3,8,32,256]{3,2,1,0:T(8,128)S(1)} %get-tuple-element.63.half, ...), custom_call_target="tpu_custom_call" | custom-call | bytes 10800000 | tf_op jit(solution)/shard_map/pallas_call | solution.py:592
  15.6 1.6 %collective-permute-start.2 = (f32[3,2,16,256]{3,2,1,0:T(8,128)S(1)}, f32[3,2,16,256]{3,2,1,0:T(8,128)S(1)}, u32[]{:S(2)}, u32[]{:S(2)}) collective-permute-start(f32[3,2,16,256]{3,2,1,0:T(8,128)S(1)} %get-tuple-element.77), channel_id=1, source_target_pairs={{0,1},{1,0},{2,3},{3,2},{4,5},{5,4},{6,7},{7,6},{8,9},{9,8},{10,11... | collective-permute-start | bytes 294920 | tf_op jit(solution)/shard_map/ppermute | solution.py:608
  17.2 1.5 %collective-permute-start.3 = (f32[3,2,16,256]{3,2,1,0:T(8,128)S(1)}, f32[3,2,16,256]{3,2,1,0:T(8,128)S(1)}, u32[]{:S(2)}, u32[]{:S(2)}) collective-permute-start(f32[3,2,16,256]{3,2,1,0:T(8,128)S(1)} %get-tuple-element.78), channel_id=1, source_target_pairs={{1,2},{2,1},{3,4},{4,3},{5,6},{6,5},{7,0},{0,7},{9,10},{10,9},{11,... | collective-permute-start | bytes 294920 | tf_op jit(solution)/shard_map/ppermute | solution.py:608
  18.7 3.6 %shard_map.115 = (f32[3,4,32,256]{3,2,1,0:T(8,128)S(1)}, f32[8,128]{1,0:T(8,128)}) custom-call(f32[200,256]{1,0:T(8,128)S(1)} %collective-permute-done.xa, f32[208,256]{1,0:T(8,128)S(1)} %collective-permute-done.1.xb, f32[3,2,12,48,128]{4,3,2,1,0:T(8,128)S(1)} %get-tuple-element.62.u.u_ref.u_own, f32[3,2,10,48,128]{4,3,2,1,0:T(8,128)S(1)} %get-tuple-element.69.left_own, ...), custom_call_target="tpu_custom_call" | custom-call | bytes 10800000 | tf_op jit(solution)/shard_map/pallas_call | solution.py:592
  22.3 2.0 %collective-permute-done.3.yb = f32[3,2,16,256]{3,2,1,0:T(8,128)S(1)} collective-permute-done((f32[3,2,16,256]{3,2,1,0:T(8,128)S(1)}, f32[3,2,16,256]{3,2,1,0:T(8,128)S(1)}, u32[]{:S(2)}, u32[]{:S(2)}) %collective-permute-start.3) | collective-permute-done | bytes 98336 | tf_op jit(solution)/shard_map/ppermute | solution.py:608
  24.7 1.8 %collective-permute-start.5 = (f32[208,256]{1,0:T(8,128)S(1)}, f32[208,256]{1,0:T(8,128)S(1)}, u32[]{:S(2)}, u32[]{:S(2)}) collective-permute-start(f32[208,256]{1,0:T(8,128)S(1)} %get-tuple-element.85), channel_id=1, source_target_pairs={{8,16},{16,8},{24,32},{32,24},{40,48},{48,40},{56,64},{64,56},{72,... | collective-permute-start | bytes 638984 | tf_op jit(solution)/shard_map/ppermute | solution.py:608
  26.5 2.6 %shard_map.119 = (f32[3,8,32,128]{3,2,1,0:T(8,128)S(1)}, f32[3,8,128]{2,1,0:T(8,128)S(1)}, f32[200,256]{1,0:T(8,128)S(1)}) custom-call(s32[3,2,16]{2,1,0:T(2,128)S(1)} %copy-done.1, f32[3,2,12,48,128]{4,3,2,1,0:T(8,128)S(1)} %get-tuple-element.80.u.u_ref.u_own, f32[7,8,128]{2,1,0:T(8,128)S(1)} %get-tuple-element.83.pst), custom_call_target="tpu_custom_call" | custom-call | bytes 4500000 | tf_op jit(solution)/shard_map/pallas_call | solution.py:592
  29.2 3.6 %shard_map.118 = (f32[3,4,32,256]{3,2,1,0:T(8,128)S(1)}, f32[3,2,10,48,128]{4,3,2,1,0:T(8,128)S(1)}, f32[3,2,10,48,128]{4,3,2,1,0:T(8,128)S(1)}, f32[8,128]{1,0:T(8,128)S(1)}) custom-call(f32[3,2,12,48,128]{4,3,2,1,0:T(8,128)S(1)} %get-tuple-element.80.u.u_ref.u_own, f32[3,8,32,256]{3,2,1,0:T(8,128)S(1)} %get-tuple-element.81.half, ...), custom_call_target="tpu_custom_call" | custom-call | bytes 10800000 | tf_op jit(solution)/shard_map/pallas_call | solution.py:592
  33.8 1.8 %collective-permute-start.7 = (f32[3,2,16,256]{3,2,1,0:T(8,128)S(1)}, f32[3,2,16,256]{3,2,1,0:T(8,128)S(1)}, u32[]{:S(2)}, u32[]{:S(2)}) collective-permute-start(f32[3,2,16,256]{3,2,1,0:T(8,128)S(1)} %get-tuple-element.95), channel_id=1, source_target_pairs={{1,2},{2,1},{3,4},{4,3},{5,6},{6,5},{7,0},{0,7},{9,10},{10,9},{11,... | collective-permute-start | bytes 294920 | tf_op jit(solution)/shard_map/ppermute | solution.py:608
  35.6 3.6 %shard_map.120 = (f32[3,4,32,256]{3,2,1,0:T(8,128)S(1)}, f32[8,128]{1,0:T(8,128)}) custom-call(f32[200,256]{1,0:T(8,128)S(1)} %collective-permute-done.4.xa, f32[208,256]{1,0:T(8,128)S(1)} %collective-permute-done.5.xb, f32[3,2,12,48,128]{4,3,2,1,0:T(8,128)S(1)} %get-tuple-element.80.u.u_ref.u_own, f32[3,2,10,48,128]{4,3,2,1,0:T(8,128)S(1)} %get-tuple-element.86.left_own, ...), custom_call_target="tpu_custom_call" | custom-call | bytes 10800000 | tf_op jit(solution)/shard_map/pallas_call | solution.py:592
  41.1 2.6 %shard_map.124 = (f32[3,8,32,128]{3,2,1,0:T(8,128)S(1)}, f32[3,8,128]{2,1,0:T(8,128)S(1)}, f32[200,256]{1,0:T(8,128)S(1)}) custom-call(s32[3,2,16]{2,1,0:T(2,128)S(1)} %copy-done.1, f32[3,2,12,48,128]{4,3,2,1,0:T(8,128)S(1)} %get-tuple-element.96.u.u_ref.u_own, f32[7,8,128]{2,1,0:T(8,128)S(1)} %get-tuple-element.100.pst), custom_call_target="tpu_custom_call" | custom-call | bytes 4500000 | tf_op jit(solution)/shard_map/pallas_call | solution.py:592
  43.8 4.3 %collective-permute-start.10 = (f32[208,256]{1,0:T(8,128)S(1)}, f32[208,256]{1,0:T(8,128)S(1)}, u32[]{:S(2)}, u32[]{:S(2)}) collective-permute-start(f32[208,256]{1,0:T(8,128)S(1)} %get-tuple-element.105), channel_id=1, source_target_pairs={{8,16},{16,8},{24,32},{32,24},{40,48},{48,40},{56,64},{64,56},{72,... | collective-permute-start | bytes 638984 | tf_op jit(solution)/shard_map/ppermute | solution.py:608
  49.2 2.7 %collective-permute-done.9.theirs = f32[3,8,128]{2,1,0:T(8,128)S(1)} collective-permute-done((f32[3,8,128]{2,1,0:T(8,128)S(1)}, f32[3,8,128]{2,1,0:T(8,128)S(1)}, u32[]{:S(2)}, u32[]{:S(2)}) %collective-permute-start.9) | collective-permute-done | bytes 12320 | tf_op jit(solution)/shard_map/ppermute | solution.py:608
  52.2 2.6 %shard_map.127 = (f32[3,4,32,256]{3,2,1,0:T(8,128)S(1)}, f32[8,128]{1,0:T(8,128)S(1)}) custom-call(f32[3,2,12,48,128]{4,3,2,1,0:T(8,128)S(1)} %get-tuple-element.96.u.u_ref.u_own, f32[3,2,10,48,128]{4,3,2,1,0:T(8,128)S(1)} %get-tuple-element.97.left.left_own, f32[3,2,10,48,128]{4,3,2,1,0:T(8,128)S(1)} %get-tuple-element.98.right.right_own, ...), custom_call_target="tpu_custom_call" | custom-call | bytes 7800000 | tf_op jit(solution)/shard_map/pallas_call | solution.py:592
  54.9 2.5 %collective-permute-done.11.refs_1_ = f32[6,4,128]{2,1,0:T(4,128)S(1)} collective-permute-done((f32[6,4,128]{2,1,0:T(4,128)S(1)}, f32[6,4,128]{2,1,0:T(4,128)S(1)}, u32[]{:S(2)}, u32[]{:S(2)}) %collective-permute-start.11) | collective-permute-done | bytes 12320 | tf_op jit(solution)/shard_map/ppermute | solution.py:625
  57.5 6.4 %collective-permute-start.16 = (f32[6,8,128]{2,1,0:T(8,128)S(1)}, f32[6,8,128]{2,1,0:T(8,128)S(1)}, u32[]{:S(2)}, u32[]{:S(2)}) collective-permute-start(f32[6,8,128]{2,1,0:T(8,128)S(1)} %shard_map.128.after.refs_0_), channel_id=1, source_target_pairs={{0,34},{1,35},{2,32},{3,33},{4,38},{5,39},{6,36},{7,37},{8,42},{9,... | collective-permute-start | bytes 73736 | tf_op jit(solution)/shard_map/ppermute | solution.py:625
  64.3 3.0 %shard_map.129 = (f32[3,4,32,256]{3,2,1,0:T(8,128)S(1)}, f32[8,128]{1,0:T(8,128)S(1)}) custom-call(f32[200,256]{1,0:T(8,128)S(1)} %collective-permute-done.8.xa, f32[208,256]{1,0:T(8,128)S(1)} %collective-permute-done.10.xb, f32[3,2,12,48,128]{4,3,2,1,0:T(8,128)S(1)} %get-tuple-element.96.u.u_ref.u_own, ...), custom_call_target="tpu_custom_call" | custom-call | bytes 10800000 | tf_op jit(solution)/shard_map/pallas_call | solution.py:592
  67.4 1.8 %collective-permute-start.17 = (f32[6,32,128]{2,1,0:T(8,128)S(1)}, f32[6,32,128]{2,1,0:T(8,128)S(1)}, u32[]{:S(2)}, u32[]{:S(2)}) collective-permute-start(f32[6,32,128]{2,1,0:T(8,128)S(1)} %shard_map.131.after.refs_0_), channel_id=1, source_target_pairs={{0,4},{1,5},{2,6},{3,7},{4,0},{5,1},{6,2},{7,3},{8,24},{9,25},{10,... | collective-permute-start | bytes 294920 | tf_op jit(solution)/shard_map/ppermute | solution.py:625
  69.2 1.8 %collective-permute-start.19 = (f32[6,32,128]{2,1,0:T(8,128)S(1)}, f32[6,32,128]{2,1,0:T(8,128)S(1)}, u32[]{:S(2)}, u32[]{:S(2)}) collective-permute-start(f32[6,32,128]{2,1,0:T(8,128)S(1)} %shard_map.131.after.refs_0_), channel_id=1, source_target_pairs={{0,20},{1,21},{2,22},{3,23},{4,16},{5,17},{6,18},{7,19},{8,28},{9,... | collective-permute-start | bytes 294920 | tf_op jit(solution)/shard_map/ppermute | solution.py:625
  70.9 1.5 %shard_map.132 = (f32[3,8,32,256]{3,2,1,0:T(8,128)}, f32[3,8,32,256]{3,2,1,0:T(8,128)}, f32[8,128]{1,0:T(8,128)S(1)}) custom-call(f32[3,2,12,48,128]{4,3,2,1,0:T(8,128)S(1)} %get-tuple-element.96.u.u_ref.u_own, f32[3,4,32,256]{3,2,1,0:T(8,128)S(1)} %get-tuple-element.104.inner, f32[3,4,32,256]{3,2,1,0:T(8,128)S(1)} %get-tuple-element.107.edge, ...), custom_call_target="tpu_custom_call" | custom-call | bytes 4200000 | tf_op jit(solution)/shard_map/pallas_call | solution.py:592
  72.4 2.4 %collective-permute-done.18.refs_2_ = f32[6,32,128]{2,1,0:T(8,128)S(1)} collective-permute-done((f32[6,32,128]{2,1,0:T(8,128)S(1)}, f32[6,32,128]{2,1,0:T(8,128)S(1)}, u32[]{:S(2)}, u32[]{:S(2)}) %collective-permute-start.18) | collective-permute-done | bytes 98336 | tf_op jit(solution)/shard_map/ppermute | solution.py:625
  (43 shorter events, 6.8 us)
Async XLA Ops:
  0.6 9.0 %copy-start.1 = (s32[3,2,16]{2,1,0:T(2,128)S(1)}, s32[3,2,16]{2,1,0:T(2,128)}, u32[]{:S(2)}) copy-start(s32[3,2,16]{2,1,0:T(2,128)} %pairs.5) | copy-start | bytes 1156
  3.3 8.5 %copy-start = (s32[4,8,32,256]{3,2,1,0:T(8,128)S(1)}, s32[4,8,32,256]{3,2,1,0:T(8,128)}, u32[]{:S(2)}) copy-start(s32[4,8,32,256]{3,2,1,0:T(8,128)} %masks.1) | copy-start | bytes 3145732
  3.3 12.2 %collective-permute-start.1 = (f32[208,256]{1,0:T(8,128)S(1)}, f32[208,256]{1,0:T(8,128)S(1)}, u32[]{:S(2)}, u32[]{:S(2)}) collective-permute-start(f32[208,256]{1,0:T(8,128)S(1)} %get-tuple-element.68), channel_id=1, source_target_pairs={{8,16},{16,8},{24,32},{32,24},{40,48},{48,40},{56,64},{64,56},{72,... | collective-permute-start | bytes 638984 | tf_op jit(solution)/shard_map/ppermute | solution.py:608
  11.8 3.8 %collective-permute-start = (f32[200,256]{1,0:T(8,128)S(1)}, f32[200,256]{1,0:T(8,128)S(1)}, u32[]{:S(2)}, u32[]{:S(2)}) collective-permute-start(f32[200,256]{1,0:T(8,128)S(1)} %get-tuple-element.67), channel_id=1, source_target_pairs={{0,8},{8,0},{16,24},{24,16},{32,40},{40,32},{48,56},{56,48},{64,72... | collective-permute-start | bytes 614408 | tf_op jit(solution)/shard_map/ppermute | solution.py:608
  15.6 6.6 %collective-permute-start.2 = (f32[3,2,16,256]{3,2,1,0:T(8,128)S(1)}, f32[3,2,16,256]{3,2,1,0:T(8,128)S(1)}, u32[]{:S(2)}, u32[]{:S(2)}) collective-permute-start(f32[3,2,16,256]{3,2,1,0:T(8,128)S(1)} %get-tuple-element.77), channel_id=1, source_target_pairs={{0,1},{1,0},{2,3},{3,2},{4,5},{5,4},{6,7},{7,6},{8,9},{9,8},{10,11... | collective-permute-start | bytes 294920 | tf_op jit(solution)/shard_map/ppermute | solution.py:608
  17.2 7.0 %collective-permute-start.3 = (f32[3,2,16,256]{3,2,1,0:T(8,128)S(1)}, f32[3,2,16,256]{3,2,1,0:T(8,128)S(1)}, u32[]{:S(2)}, u32[]{:S(2)}) collective-permute-start(f32[3,2,16,256]{3,2,1,0:T(8,128)S(1)} %get-tuple-element.78), channel_id=1, source_target_pairs={{1,2},{2,1},{3,4},{4,3},{5,6},{6,5},{7,0},{0,7},{9,10},{10,9},{11,... | collective-permute-start | bytes 294920 | tf_op jit(solution)/shard_map/ppermute | solution.py:608
  24.7 9.0 %collective-permute-start.5 = (f32[208,256]{1,0:T(8,128)S(1)}, f32[208,256]{1,0:T(8,128)S(1)}, u32[]{:S(2)}, u32[]{:S(2)}) collective-permute-start(f32[208,256]{1,0:T(8,128)S(1)} %get-tuple-element.85), channel_id=1, source_target_pairs={{8,16},{16,8},{24,32},{32,24},{40,48},{48,40},{56,64},{64,56},{72,... | collective-permute-start | bytes 638984 | tf_op jit(solution)/shard_map/ppermute | solution.py:608
  29.1 3.7 %collective-permute-start.4 = (f32[200,256]{1,0:T(8,128)S(1)}, f32[200,256]{1,0:T(8,128)S(1)}, u32[]{:S(2)}, u32[]{:S(2)}) collective-permute-start(f32[200,256]{1,0:T(8,128)S(1)} %get-tuple-element.84), channel_id=1, source_target_pairs={{0,8},{8,0},{16,24},{24,16},{32,40},{40,32},{48,56},{56,48},{64,72... | collective-permute-start | bytes 614408 | tf_op jit(solution)/shard_map/ppermute | solution.py:608
  33.7 5.5 %collective-permute-start.6 = (f32[3,2,16,256]{3,2,1,0:T(8,128)S(1)}, f32[3,2,16,256]{3,2,1,0:T(8,128)S(1)}, u32[]{:S(2)}, u32[]{:S(2)}) collective-permute-start(f32[3,2,16,256]{3,2,1,0:T(8,128)S(1)} %get-tuple-element.94), channel_id=1, source_target_pairs={{0,1},{1,0},{2,3},{3,2},{4,5},{5,4},{6,7},{7,6},{8,9},{9,8},{10,11... | collective-permute-start | bytes 294920 | tf_op jit(solution)/shard_map/ppermute | solution.py:608
  33.8 6.8 %collective-permute-start.7 = (f32[3,2,16,256]{3,2,1,0:T(8,128)S(1)}, f32[3,2,16,256]{3,2,1,0:T(8,128)S(1)}, u32[]{:S(2)}, u32[]{:S(2)}) collective-permute-start(f32[3,2,16,256]{3,2,1,0:T(8,128)S(1)} %get-tuple-element.95), channel_id=1, source_target_pairs={{1,2},{2,1},{3,4},{4,3},{5,6},{6,5},{7,0},{0,7},{9,10},{10,9},{11,... | collective-permute-start | bytes 294920 | tf_op jit(solution)/shard_map/ppermute | solution.py:608
  43.7 4.4 %collective-permute-start.8 = (f32[200,256]{1,0:T(8,128)S(1)}, f32[200,256]{1,0:T(8,128)S(1)}, u32[]{:S(2)}, u32[]{:S(2)}) collective-permute-start(f32[200,256]{1,0:T(8,128)S(1)} %get-tuple-element.101), channel_id=1, source_target_pairs={{0,8},{8,0},{16,24},{24,16},{32,40},{40,32},{48,56},{56,48},{64,72... | collective-permute-start | bytes 614408 | tf_op jit(solution)/shard_map/ppermute | solution.py:608
  43.8 20.1 %collective-permute-start.10 = (f32[208,256]{1,0:T(8,128)S(1)}, f32[208,256]{1,0:T(8,128)S(1)}, u32[]{:S(2)}, u32[]{:S(2)}) collective-permute-start(f32[208,256]{1,0:T(8,128)S(1)} %get-tuple-element.105), channel_id=1, source_target_pairs={{8,16},{16,8},{24,32},{32,24},{40,48},{48,40},{56,64},{64,56},{72,... | collective-permute-start | bytes 638984 | tf_op jit(solution)/shard_map/ppermute | solution.py:608
  48.1 3.8 %collective-permute-start.9 = (f32[3,8,128]{2,1,0:T(8,128)S(1)}, f32[3,8,128]{2,1,0:T(8,128)S(1)}, u32[]{:S(2)}, u32[]{:S(2)}) collective-permute-start(f32[3,8,128]{2,1,0:T(8,128)S(1)} %shard_map.125.ours), channel_id=1, source_target_pairs={{0,1},{1,0},{2,3},{3,2},{4,5},{5,4},{6,7},{7,6},{8,9},{9,8},{10,11... | collective-permute-start | bytes 36872 | tf_op jit(solution)/shard_map/ppermute | solution.py:608
  51.9 5.5 %collective-permute-start.11 = (f32[6,4,128]{2,1,0:T(4,128)S(1)}, f32[6,4,128]{2,1,0:T(4,128)S(1)}, u32[]{:S(2)}, u32[]{:S(2)}) collective-permute-start(f32[6,4,128]{2,1,0:T(4,128)S(1)} %shard_map.126.after.refs_0_.token), channel_id=1, source_target_pairs={{0,64},{1,65},{2,66},{3,67},{4,68},{5,69},{6,70},{7,71},{8,72},{9,... | collective-permute-start | bytes 36872 | tf_op jit(solution)/shard_map/ppermute | solution.py:625
  57.4 9.9 %collective-permute-start.14 = (f32[6,8,128]{2,1,0:T(8,128)S(1)}, f32[6,8,128]{2,1,0:T(8,128)S(1)}, u32[]{:S(2)}, u32[]{:S(2)}) collective-permute-start(f32[6,8,128]{2,1,0:T(8,128)S(1)} %shard_map.128.after.refs_0_), channel_id=1, source_target_pairs={{0,32},{1,33},{2,34},{3,35},{4,36},{5,37},{6,38},{7,39},{8,10},{9,... | collective-permute-start | bytes 73736 | tf_op jit(solution)/shard_map/ppermute | solution.py:625
  57.4 9.9 %collective-permute-start.15 = (f32[6,8,128]{2,1,0:T(8,128)S(1)}, f32[6,8,128]{2,1,0:T(8,128)S(1)}, u32[]{:S(2)}, u32[]{:S(2)}) collective-permute-start(f32[6,8,128]{2,1,0:T(8,128)S(1)} %shard_map.128.after.refs_0_), channel_id=1, source_target_pairs={{0,2},{1,3},{2,0},{3,1},{4,6},{5,7},{6,4},{7,5},{8,40},{9,41},{10,... | collective-permute-start | bytes 73736 | tf_op jit(solution)/shard_map/ppermute | solution.py:625
  57.5 9.8 %collective-permute-start.16 = (f32[6,8,128]{2,1,0:T(8,128)S(1)}, f32[6,8,128]{2,1,0:T(8,128)S(1)}, u32[]{:S(2)}, u32[]{:S(2)}) collective-permute-start(f32[6,8,128]{2,1,0:T(8,128)S(1)} %shard_map.128.after.refs_0_), channel_id=1, source_target_pairs={{0,34},{1,35},{2,32},{3,33},{4,38},{5,39},{6,36},{7,37},{8,42},{9,... | collective-permute-start | bytes 73736 | tf_op jit(solution)/shard_map/ppermute | solution.py:625
  63.9 7.0 %collective-permute-start.12 = (f32[3,2,16,256]{3,2,1,0:T(8,128)S(1)}, f32[3,2,16,256]{3,2,1,0:T(8,128)S(1)}, u32[]{:S(2)}, u32[]{:S(2)}) collective-permute-start(f32[3,2,16,256]{3,2,1,0:T(8,128)S(1)} %get-tuple-element.111), channel_id=1, source_target_pairs={{0,1},{1,0},{2,3},{3,2},{4,5},{5,4},{6,7},{7,6},{8,9},{9,8},{10,11... | collective-permute-start | bytes 294920 | tf_op jit(solution)/shard_map/ppermute | solution.py:608
  64.0 6.9 %collective-permute-start.13 = (f32[3,2,16,256]{3,2,1,0:T(8,128)S(1)}, f32[3,2,16,256]{3,2,1,0:T(8,128)S(1)}, u32[]{:S(2)}, u32[]{:S(2)}) collective-permute-start(f32[3,2,16,256]{3,2,1,0:T(8,128)S(1)} %get-tuple-element.112), channel_id=1, source_target_pairs={{1,2},{2,1},{3,4},{4,3},{5,6},{6,5},{7,0},{0,7},{9,10},{10,9},{11,... | collective-permute-start | bytes 294920 | tf_op jit(solution)/shard_map/ppermute | solution.py:608
  67.4 5.0 %collective-permute-start.17 = (f32[6,32,128]{2,1,0:T(8,128)S(1)}, f32[6,32,128]{2,1,0:T(8,128)S(1)}, u32[]{:S(2)}, u32[]{:S(2)}) collective-permute-start(f32[6,32,128]{2,1,0:T(8,128)S(1)} %shard_map.131.after.refs_0_), channel_id=1, source_target_pairs={{0,4},{1,5},{2,6},{3,7},{4,0},{5,1},{6,2},{7,3},{8,24},{9,25},{10,... | collective-permute-start | bytes 294920 | tf_op jit(solution)/shard_map/ppermute | solution.py:625
  69.2 5.7 %collective-permute-start.18 = (f32[6,32,128]{2,1,0:T(8,128)S(1)}, f32[6,32,128]{2,1,0:T(8,128)S(1)}, u32[]{:S(2)}, u32[]{:S(2)}) collective-permute-start(f32[6,32,128]{2,1,0:T(8,128)S(1)} %shard_map.131.after.refs_0_), channel_id=1, source_target_pairs={{0,16},{1,17},{2,18},{3,19},{4,20},{5,21},{6,22},{7,23},{8,12},{9,... | collective-permute-start | bytes 294920 | tf_op jit(solution)/shard_map/ppermute | solution.py:625
  69.2 5.7 %collective-permute-start.19 = (f32[6,32,128]{2,1,0:T(8,128)S(1)}, f32[6,32,128]{2,1,0:T(8,128)S(1)}, u32[]{:S(2)}, u32[]{:S(2)}) collective-permute-start(f32[6,32,128]{2,1,0:T(8,128)S(1)} %shard_map.131.after.refs_0_), channel_id=1, source_target_pairs={{0,20},{1,21},{2,22},{3,23},{4,16},{5,17},{6,18},{7,19},{8,28},{9,... | collective-permute-start | bytes 294920 | tf_op jit(solution)/shard_map/ppermute | solution.py:625

commit v7 on v6

--- a/solution.py
+++ b/solution.py
@@ -11,7 +11,7 @@
 SUB = 3
 SL = 4
 SLOTS = 16
-CHUNK = 4
+CHUNK = 8
 STEP = 2
 GROUP = 4
 ROUNDS = (
@@ -557,14 +557,16 @@
 
 def final_kernel(perm, *refs):
     *parts, token, pos_out, vel_out = refs
+    once = perm[...].astype(jnp.bfloat16)
+    order = jnp.concatenate([once] * 3, axis=1)
     for c in range(3):
         for at, out in ((c, pos_out), (3 + c, vel_out)):
-            out[c] = jnp.dot(
-                perm[...],
-                jnp.concatenate([part[at] for part in parts], axis=0),
-                precision=lax.Precision.HIGHEST,
-                preferred_element_type=F32,
-            )
+            left = jnp.concatenate([part[at] for part in parts], axis=0)
+            pieces = []
+            for _ in range(3):
+                pieces.append(left.astype(jnp.bfloat16))
+                left = left - pieces[-1].astype(F32)
+            out[c] = jnp.dot(order, jnp.concatenate(pieces, axis=0), preferred_element_type=F32)
 
 
 VMEM = pl.BlockSpec(memory_space=pltpu.VMEM)

time: 76.1 us -> 76.7 us (level)
  starting transfers between devices: 28.4 us -> 35.6 us
  Pallas kernels: 34.8 us -> 29.2 us
  waiting for transfers between devices: 11.9 us -> 11 us
    pallas_call x23, Pallas kernels: 34.8 us -> 29.2 us  [call(): pl.pallas_call(kernel, out_shape=outputs, in_specs=ins or [SMEM] * scalar...]
    ppermute x13, starting transfers between devices: 18.1 us -> 23.6 us  [swap(): return lax.ppermute(value, axis, pairs)]
    ppermute x7, waiting for transfers between devices: 4.98 us -> 3.14 us  [swapped(): return lax.ppermute(gathered, ('slab', 'split'), pairs)]
    ppermute x7, starting transfers between devices: 10.3 us -> 12 us  [swapped(): return lax.ppermute(gathered, ('slab', 'split'), pairs)]
    ppermute x13, waiting for transfers between devices: 6.94 us -> 7.86 us  [swap(): return lax.ppermute(value, axis, pairs)]
  transfers between devices with their start and end apart: 20 -> 20, of which waited for: 6 -> 6; matrix products, arithmetic and copies ran while one was open for 0% -> 0% of each run, Pallas kernels for 36% -> 31%
where the time goes in v7:
time: 76.7 us
  starting transfers between devices  35.6 us (46%)
  Pallas kernels  29.2 us (38%)
  waiting for transfers between devices  11 us (14%)
  between operations  0.89 us (1%)
    pallas_call x23, Pallas kernels, call(): pl.pallas_call(kernel, out_shape=outputs, in_specs=ins or [SMEM] * scalar...  29.2 us
    ppermute x13, starting transfers between devices, swap(): return lax.ppermute(value, axis, pairs)  23.6 us
    ppermute x7, starting transfers between devices, swapped(): return lax.ppermute(gathered, ('slab', 'split'), pairs)  12 us
    ppermute x13, waiting for transfers between devices, swap(): return lax.ppermute(value, axis, pairs)  7.86 us
    ppermute x7, waiting for transfers between devices, swapped(): return lax.ppermute(gathered, ('slab', 'split'), pairs)  3.14 us
  transfers between devices with their start and end apart: 20, of which 6 were waited for; matrix products, arithmetic and copies ran while one was open for 0% of the time, Pallas kernels for 31%

profile of v7, /device:TPU:0, one launch (start us, length us, event | category | flops | bytes accessed | tf_op | source)
XLA Modules:
  0.0 76.7 jit_solution(634608864885793231)
XLA Ops:
  0.6 2.7 %shard_map.111 = (f32[3,2,12,48,128]{4,3,2,1,0:T(8,128)S(1)}, f32[3,8,32,256]{3,2,1,0:T(8,128)S(1)}, f32[7,8,128]{2,1,0:T(8,128)S(1)}, f32[128,128]{1,0:T(8,128)...) custom-call(f32[3,8,32,256]{3,2,1,0:T(8,128)} %u.1, ...), custom_call_target="tpu_custom_call" | custom-call | bytes 3000000 | tf_op jit(solution)/shard_map/pallas_call | solution.py:594
  3.3 6.3 %collective-permute-start.1 = (f32[208,256]{1,0:T(8,128)S(1)}, f32[208,256]{1,0:T(8,128)S(1)}, u32[]{:S(2)}, u32[]{:S(2)}) collective-permute-start(f32[208,256]{1,0:T(8,128)S(1)} %get-tuple-element.68), channel_id=1, source_target_pairs={{8,16},{16,8},{24,32},{32,24},{40,48},{48,40},{56,64},{64,56},{72,... | collective-permute-start | bytes 638984 | tf_op jit(solution)/shard_map/ppermute | solution.py:610
  10.5 3.6 %shard_map.113 = (f32[3,4,32,256]{3,2,1,0:T(8,128)S(1)}, f32[3,2,10,48,128]{4,3,2,1,0:T(8,128)S(1)}, f32[3,2,10,48,128]{4,3,2,1,0:T(8,128)S(1)}, f32[8,128]{1,0:T(8,128)S(1)}) custom-call(f32[3,2,12,48,128]{4,3,2,1,0:T(8,128)S(1)} %get-tuple-element.62.u.u_ref.u_own, f32[3,8,32,256]{3,2,1,0:T(8,128)S(1)} %get-tuple-element.63.half, ...), custom_call_target="tpu_custom_call" | custom-call | bytes 10800000 | tf_op jit(solution)/shard_map/pallas_call | solution.py:594
  14.1 3.4 %collective-permute-start.2 = (f32[3,2,16,256]{3,2,1,0:T(8,128)S(1)}, f32[3,2,16,256]{3,2,1,0:T(8,128)S(1)}, u32[]{:S(2)}, u32[]{:S(2)}) collective-permute-start(f32[3,2,16,256]{3,2,1,0:T(8,128)S(1)} %get-tuple-element.77), channel_id=1, source_target_pairs={{0,1},{1,0},{2,3},{3,2},{4,5},{5,4},{6,7},{7,6},{8,9},{9,8},{10,11... | collective-permute-start | bytes 294920 | tf_op jit(solution)/shard_map/ppermute | solution.py:610
  17.5 2.2 %collective-permute-start.3 = (f32[3,2,16,256]{3,2,1,0:T(8,128)S(1)}, f32[3,2,16,256]{3,2,1,0:T(8,128)S(1)}, u32[]{:S(2)}, u32[]{:S(2)}) collective-permute-start(f32[3,2,16,256]{3,2,1,0:T(8,128)S(1)} %get-tuple-element.78), channel_id=1, source_target_pairs={{1,2},{2,1},{3,4},{4,3},{5,6},{6,5},{7,0},{0,7},{9,10},{10,9},{11,... | collective-permute-start | bytes 294920 | tf_op jit(solution)/shard_map/ppermute | solution.py:610
  19.7 3.6 %shard_map.115 = (f32[3,4,32,256]{3,2,1,0:T(8,128)S(1)}, f32[8,128]{1,0:T(8,128)}) custom-call(f32[200,256]{1,0:T(8,128)S(1)} %collective-permute-done.xa, f32[208,256]{1,0:T(8,128)S(1)} %collective-permute-done.1.xb, f32[3,2,12,48,128]{4,3,2,1,0:T(8,128)S(1)} %get-tuple-element.62.u.u_ref.u_own, f32[3,2,10,48,128]{4,3,2,1,0:T(8,128)S(1)} %get-tuple-element.69.left_own, ...), custom_call_target="tpu_custom_call" | custom-call | bytes 10800000 | tf_op jit(solution)/shard_map/pallas_call | solution.py:594
  23.3 1.2 %collective-permute-done.3.yb = f32[3,2,16,256]{3,2,1,0:T(8,128)S(1)} collective-permute-done((f32[3,2,16,256]{3,2,1,0:T(8,128)S(1)}, f32[3,2,16,256]{3,2,1,0:T(8,128)S(1)}, u32[]{:S(2)}, u32[]{:S(2)}) %collective-permute-start.3) | collective-permute-done | bytes 98336 | tf_op jit(solution)/shard_map/ppermute | solution.py:610
  25.0 1.5 %collective-permute-start.5 = (f32[208,256]{1,0:T(8,128)S(1)}, f32[208,256]{1,0:T(8,128)S(1)}, u32[]{:S(2)}, u32[]{:S(2)}) collective-permute-start(f32[208,256]{1,0:T(8,128)S(1)} %get-tuple-element.85), channel_id=1, source_target_pairs={{8,16},{16,8},{24,32},{32,24},{40,48},{48,40},{56,64},{64,56},{72,... | collective-permute-start | bytes 638984 | tf_op jit(solution)/shard_map/ppermute | solution.py:610
  27.2 3.6 %shard_map.118 = (f32[3,4,32,256]{3,2,1,0:T(8,128)S(1)}, f32[3,2,10,48,128]{4,3,2,1,0:T(8,128)S(1)}, f32[3,2,10,48,128]{4,3,2,1,0:T(8,128)S(1)}, f32[8,128]{1,0:T(8,128)S(1)}) custom-call(f32[3,2,12,48,128]{4,3,2,1,0:T(8,128)S(1)} %get-tuple-element.80.u.u_ref.u_own, f32[3,8,32,256]{3,2,1,0:T(8,128)S(1)} %get-tuple-element.81.half, ...), custom_call_target="tpu_custom_call" | custom-call | bytes 10800000 | tf_op jit(solution)/shard_map/pallas_call | solution.py:594
  30.9 3.1 %collective-permute-done.5.xb = f32[208,256]{1,0:T(8,128)S(1)} collective-permute-done((f32[208,256]{1,0:T(8,128)S(1)}, f32[208,256]{1,0:T(8,128)S(1)}, u32[]{:S(2)}, u32[]{:S(2)}) %collective-permute-start.5) | collective-permute-done | bytes 213024 | tf_op jit(solution)/shard_map/ppermute | solution.py:610
  34.1 2.3 %collective-permute-start.7 = (f32[3,2,16,256]{3,2,1,0:T(8,128)S(1)}, f32[3,2,16,256]{3,2,1,0:T(8,128)S(1)}, u32[]{:S(2)}, u32[]{:S(2)}) collective-permute-start(f32[3,2,16,256]{3,2,1,0:T(8,128)S(1)} %get-tuple-element.95), channel_id=1, source_target_pairs={{1,2},{2,1},{3,4},{4,3},{5,6},{6,5},{7,0},{0,7},{9,10},{10,9},{11,... | collective-permute-start | bytes 294920 | tf_op jit(solution)/shard_map/ppermute | solution.py:610
  36.4 3.6 %shard_map.120 = (f32[3,4,32,256]{3,2,1,0:T(8,128)S(1)}, f32[8,128]{1,0:T(8,128)}) custom-call(f32[200,256]{1,0:T(8,128)S(1)} %collective-permute-done.4.xa, f32[208,256]{1,0:T(8,128)S(1)} %collective-permute-done.5.xb, f32[3,2,12,48,128]{4,3,2,1,0:T(8,128)S(1)} %get-tuple-element.80.u.u_ref.u_own, f32[3,2,10,48,128]{4,3,2,1,0:T(8,128)S(1)} %get-tuple-element.86.left_own, ...), custom_call_target="tpu_custom_call" | custom-call | bytes 10800000 | tf_op jit(solution)/shard_map/pallas_call | solution.py:594
  42.4 5.1 %collective-permute-start.10 = (f32[208,256]{1,0:T(8,128)S(1)}, f32[208,256]{1,0:T(8,128)S(1)}, u32[]{:S(2)}, u32[]{:S(2)}) collective-permute-start(f32[208,256]{1,0:T(8,128)S(1)} %get-tuple-element.105), channel_id=1, source_target_pairs={{8,16},{16,8},{24,32},{32,24},{40,48},{48,40},{56,64},{64,56},{72,... | collective-permute-start | bytes 638984 | tf_op jit(solution)/shard_map/ppermute | solution.py:610
  48.7 2.5 %collective-permute-done.9.theirs = f32[3,8,128]{2,1,0:T(8,128)S(1)} collective-permute-done((f32[3,8,128]{2,1,0:T(8,128)S(1)}, f32[3,8,128]{2,1,0:T(8,128)S(1)}, u32[]{:S(2)}, u32[]{:S(2)}) %collective-permute-start.9) | collective-permute-done | bytes 12320 | tf_op jit(solution)/shard_map/ppermute | solution.py:610
  51.3 1.9 %collective-permute-start.11 = (f32[6,4,128]{2,1,0:T(4,128)S(1)}, f32[6,4,128]{2,1,0:T(4,128)S(1)}, u32[]{:S(2)}, u32[]{:S(2)}) collective-permute-start(f32[6,4,128]{2,1,0:T(4,128)S(1)} %shard_map.126.after.refs_0_.token), channel_id=1, source_target_pairs={{0,64},{1,65},{2,66},{3,67},{4,68},{5,69},{6,70},{7,71},{8,72},{9,... | collective-permute-start | bytes 36872 | tf_op jit(solution)/shard_map/ppermute | solution.py:627
  53.2 2.6 %shard_map.127 = (f32[3,4,32,256]{3,2,1,0:T(8,128)S(1)}, f32[8,128]{1,0:T(8,128)S(1)}) custom-call(f32[3,2,12,48,128]{4,3,2,1,0:T(8,128)S(1)} %get-tuple-element.96.u.u_ref.u_own, f32[3,2,10,48,128]{4,3,2,1,0:T(8,128)S(1)} %get-tuple-element.97.left.left_own, f32[3,2,10,48,128]{4,3,2,1,0:T(8,128)S(1)} %get-tuple-element.98.right.right_own, ...), custom_call_target="tpu_custom_call" | custom-call | bytes 7800000 | tf_op jit(solution)/shard_map/pallas_call | solution.py:594
  56.6 1.6 %collective-permute-start.15 = (f32[6,8,128]{2,1,0:T(8,128)S(1)}, f32[6,8,128]{2,1,0:T(8,128)S(1)}, u32[]{:S(2)}, u32[]{:S(2)}) collective-permute-start(f32[6,8,128]{2,1,0:T(8,128)S(1)} %shard_map.128.after.refs_0_), channel_id=1, source_target_pairs={{0,2},{1,3},{2,0},{3,1},{4,6},{5,7},{6,4},{7,5},{8,40},{9,41},{10,... | collective-permute-start | bytes 73736 | tf_op jit(solution)/shard_map/ppermute | solution.py:627
  58.2 4.9 %collective-permute-start.16 = (f32[6,8,128]{2,1,0:T(8,128)S(1)}, f32[6,8,128]{2,1,0:T(8,128)S(1)}, u32[]{:S(2)}, u32[]{:S(2)}) collective-permute-start(f32[6,8,128]{2,1,0:T(8,128)S(1)} %shard_map.128.after.refs_0_), channel_id=1, source_target_pairs={{0,34},{1,35},{2,32},{3,33},{4,38},{5,39},{6,36},{7,37},{8,42},{9,... | collective-permute-start | bytes 73736 | tf_op jit(solution)/shard_map/ppermute | solution.py:627
  63.4 1.7 %collective-permute-start.13 = (f32[3,2,16,256]{3,2,1,0:T(8,128)S(1)}, f32[3,2,16,256]{3,2,1,0:T(8,128)S(1)}, u32[]{:S(2)}, u32[]{:S(2)}) collective-permute-start(f32[3,2,16,256]{3,2,1,0:T(8,128)S(1)} %get-tuple-element.112), channel_id=1, source_target_pairs={{1,2},{2,1},{3,4},{4,3},{5,6},{6,5},{7,0},{0,7},{9,10},{10,9},{11,... | collective-permute-start | bytes 294920 | tf_op jit(solution)/shard_map/ppermute | solution.py:610
  65.1 3.0 %shard_map.129 = (f32[3,4,32,256]{3,2,1,0:T(8,128)S(1)}, f32[8,128]{1,0:T(8,128)S(1)}) custom-call(f32[200,256]{1,0:T(8,128)S(1)} %collective-permute-done.8.xa, f32[208,256]{1,0:T(8,128)S(1)} %collective-permute-done.10.xb, f32[3,2,12,48,128]{4,3,2,1,0:T(8,128)S(1)} %get-tuple-element.96.u.u_ref.u_own, ...), custom_call_target="tpu_custom_call" | custom-call | bytes 10800000 | tf_op jit(solution)/shard_map/pallas_call | solution.py:594
  68.2 1.8 %collective-permute-start.17 = (f32[6,32,128]{2,1,0:T(8,128)S(1)}, f32[6,32,128]{2,1,0:T(8,128)S(1)}, u32[]{:S(2)}, u32[]{:S(2)}) collective-permute-start(f32[6,32,128]{2,1,0:T(8,128)S(1)} %shard_map.131.after.refs_0_), channel_id=1, source_target_pairs={{0,4},{1,5},{2,6},{3,7},{4,0},{5,1},{6,2},{7,3},{8,24},{9,25},{10,... | collective-permute-start | bytes 294920 | tf_op jit(solution)/shard_map/ppermute | solution.py:627
  70.0 1.8 %collective-permute-start.19 = (f32[6,32,128]{2,1,0:T(8,128)S(1)}, f32[6,32,128]{2,1,0:T(8,128)S(1)}, u32[]{:S(2)}, u32[]{:S(2)}) collective-permute-start(f32[6,32,128]{2,1,0:T(8,128)S(1)} %shard_map.131.after.refs_0_), channel_id=1, source_target_pairs={{0,20},{1,21},{2,22},{3,23},{4,16},{5,17},{6,18},{7,19},{8,28},{9,... | collective-permute-start | bytes 294920 | tf_op jit(solution)/shard_map/ppermute | solution.py:627
  71.8 1.5 %shard_map.132 = (f32[3,8,32,256]{3,2,1,0:T(8,128)}, f32[3,8,32,256]{3,2,1,0:T(8,128)}, f32[8,128]{1,0:T(8,128)S(1)}) custom-call(f32[3,2,12,48,128]{4,3,2,1,0:T(8,128)S(1)} %get-tuple-element.96.u.u_ref.u_own, f32[3,4,32,256]{3,2,1,0:T(8,128)S(1)} %get-tuple-element.104.inner, f32[3,4,32,256]{3,2,1,0:T(8,128)S(1)} %get-tuple-element.107.edge, ...), custom_call_target="tpu_custom_call" | custom-call | bytes 4200000 | tf_op jit(solution)/shard_map/pallas_call | solution.py:594
  73.2 2.4 %collective-permute-done.18.refs_2_ = f32[6,32,128]{2,1,0:T(8,128)S(1)} collective-permute-done((f32[6,32,128]{2,1,0:T(8,128)S(1)}, f32[6,32,128]{2,1,0:T(8,128)S(1)}, u32[]{:S(2)}, u32[]{:S(2)}) %collective-permute-start.18) | collective-permute-done | bytes 98336 | tf_op jit(solution)/shard_map/ppermute | solution.py:627
  (43 shorter events, 7.9 us)
Async XLA Ops:
  0.6 9.0 %copy-start.1 = (s32[3,2,16]{2,1,0:T(2,128)S(1)}, s32[3,2,16]{2,1,0:T(2,128)}, u32[]{:S(2)}) copy-start(s32[3,2,16]{2,1,0:T(2,128)} %pairs.5) | copy-start | bytes 1156
  3.3 7.0 %copy-start = (s32[4,8,32,256]{3,2,1,0:T(8,128)S(1)}, s32[4,8,32,256]{3,2,1,0:T(8,128)}, u32[]{:S(2)}) copy-start(s32[4,8,32,256]{3,2,1,0:T(8,128)} %masks.1) | copy-start | bytes 3145732
  3.3 10.7 %collective-permute-start.1 = (f32[208,256]{1,0:T(8,128)S(1)}, f32[208,256]{1,0:T(8,128)S(1)}, u32[]{:S(2)}, u32[]{:S(2)}) collective-permute-start(f32[208,256]{1,0:T(8,128)S(1)} %get-tuple-element.68), channel_id=1, source_target_pairs={{8,16},{16,8},{24,32},{32,24},{40,48},{48,40},{56,64},{64,56},{72,... | collective-permute-start | bytes 638984 | tf_op jit(solution)/shard_map/ppermute | solution.py:610
  10.2 3.8 %collective-permute-start = (f32[200,256]{1,0:T(8,128)S(1)}, f32[200,256]{1,0:T(8,128)S(1)}, u32[]{:S(2)}, u32[]{:S(2)}) collective-permute-start(f32[200,256]{1,0:T(8,128)S(1)} %get-tuple-element.67), channel_id=1, source_target_pairs={{0,8},{8,0},{16,24},{24,16},{32,40},{40,32},{48,56},{56,48},{64,72... | collective-permute-start | bytes 614408 | tf_op jit(solution)/shard_map/ppermute | solution.py:610
  14.1 9.2 %collective-permute-start.2 = (f32[3,2,16,256]{3,2,1,0:T(8,128)S(1)}, f32[3,2,16,256]{3,2,1,0:T(8,128)S(1)}, u32[]{:S(2)}, u32[]{:S(2)}) collective-permute-start(f32[3,2,16,256]{3,2,1,0:T(8,128)S(1)} %get-tuple-element.77), channel_id=1, source_target_pairs={{0,1},{1,0},{2,3},{3,2},{4,5},{5,4},{6,7},{7,6},{8,9},{9,8},{10,11... | collective-permute-start | bytes 294920 | tf_op jit(solution)/shard_map/ppermute | solution.py:610
  17.5 7.0 %collective-permute-start.3 = (f32[3,2,16,256]{3,2,1,0:T(8,128)S(1)}, f32[3,2,16,256]{3,2,1,0:T(8,128)S(1)}, u32[]{:S(2)}, u32[]{:S(2)}) collective-permute-start(f32[3,2,16,256]{3,2,1,0:T(8,128)S(1)} %get-tuple-element.78), channel_id=1, source_target_pairs={{1,2},{2,1},{3,4},{4,3},{5,6},{6,5},{7,0},{0,7},{9,10},{10,9},{11,... | collective-permute-start | bytes 294920 | tf_op jit(solution)/shard_map/ppermute | solution.py:610
  25.0 9.0 %collective-permute-start.5 = (f32[208,256]{1,0:T(8,128)S(1)}, f32[208,256]{1,0:T(8,128)S(1)}, u32[]{:S(2)}, u32[]{:S(2)}) collective-permute-start(f32[208,256]{1,0:T(8,128)S(1)} %get-tuple-element.85), channel_id=1, source_target_pairs={{8,16},{16,8},{24,32},{32,24},{40,48},{48,40},{56,64},{64,56},{72,... | collective-permute-start | bytes 638984 | tf_op jit(solution)/shard_map/ppermute | solution.py:610
  27.1 3.7 %collective-permute-start.4 = (f32[200,256]{1,0:T(8,128)S(1)}, f32[200,256]{1,0:T(8,128)S(1)}, u32[]{:S(2)}, u32[]{:S(2)}) collective-permute-start(f32[200,256]{1,0:T(8,128)S(1)} %get-tuple-element.84), channel_id=1, source_target_pairs={{0,8},{8,0},{16,24},{24,16},{32,40},{40,32},{48,56},{56,48},{64,72... | collective-permute-start | bytes 614408 | tf_op jit(solution)/shard_map/ppermute | solution.py:610
  34.0 6.0 %collective-permute-start.6 = (f32[3,2,16,256]{3,2,1,0:T(8,128)S(1)}, f32[3,2,16,256]{3,2,1,0:T(8,128)S(1)}, u32[]{:S(2)}, u32[]{:S(2)}) collective-permute-start(f32[3,2,16,256]{3,2,1,0:T(8,128)S(1)} %get-tuple-element.94), channel_id=1, source_target_pairs={{0,1},{1,0},{2,3},{3,2},{4,5},{5,4},{6,7},{7,6},{8,9},{9,8},{10,11... | collective-permute-start | bytes 294920 | tf_op jit(solution)/shard_map/ppermute | solution.py:610
  34.1 6.8 %collective-permute-start.7 = (f32[3,2,16,256]{3,2,1,0:T(8,128)S(1)}, f32[3,2,16,256]{3,2,1,0:T(8,128)S(1)}, u32[]{:S(2)}, u32[]{:S(2)}) collective-permute-start(f32[3,2,16,256]{3,2,1,0:T(8,128)S(1)} %get-tuple-element.95), channel_id=1, source_target_pairs={{1,2},{2,1},{3,4},{4,3},{5,6},{6,5},{7,0},{0,7},{9,10},{10,9},{11,... | collective-permute-start | bytes 294920 | tf_op jit(solution)/shard_map/ppermute | solution.py:610
  42.1 5.4 %collective-permute-start.8 = (f32[200,256]{1,0:T(8,128)S(1)}, f32[200,256]{1,0:T(8,128)S(1)}, u32[]{:S(2)}, u32[]{:S(2)}) collective-permute-start(f32[200,256]{1,0:T(8,128)S(1)} %get-tuple-element.101), channel_id=1, source_target_pairs={{0,8},{8,0},{16,24},{24,16},{32,40},{40,32},{48,56},{56,48},{64,72... | collective-permute-start | bytes 614408 | tf_op jit(solution)/shard_map/ppermute | solution.py:610
  42.4 20.7 %collective-permute-start.10 = (f32[208,256]{1,0:T(8,128)S(1)}, f32[208,256]{1,0:T(8,128)S(1)}, u32[]{:S(2)}, u32[]{:S(2)}) collective-permute-start(f32[208,256]{1,0:T(8,128)S(1)} %get-tuple-element.105), channel_id=1, source_target_pairs={{8,16},{16,8},{24,32},{32,24},{40,48},{48,40},{56,64},{64,56},{72,... | collective-permute-start | bytes 638984 | tf_op jit(solution)/shard_map/ppermute | solution.py:610
  47.5 3.8 %collective-permute-start.9 = (f32[3,8,128]{2,1,0:T(8,128)S(1)}, f32[3,8,128]{2,1,0:T(8,128)S(1)}, u32[]{:S(2)}, u32[]{:S(2)}) collective-permute-start(f32[3,8,128]{2,1,0:T(8,128)S(1)} %shard_map.125.ours), channel_id=1, source_target_pairs={{0,1},{1,0},{2,3},{3,2},{4,5},{5,4},{6,7},{7,6},{8,9},{9,8},{10,11... | collective-permute-start | bytes 36872 | tf_op jit(solution)/shard_map/ppermute | solution.py:610
  51.3 5.3 %collective-permute-start.11 = (f32[6,4,128]{2,1,0:T(4,128)S(1)}, f32[6,4,128]{2,1,0:T(4,128)S(1)}, u32[]{:S(2)}, u32[]{:S(2)}) collective-permute-start(f32[6,4,128]{2,1,0:T(4,128)S(1)} %shard_map.126.after.refs_0_.token), channel_id=1, source_target_pairs={{0,64},{1,65},{2,66},{3,67},{4,68},{5,69},{6,70},{7,71},{8,72},{9,... | collective-permute-start | bytes 36872 | tf_op jit(solution)/shard_map/ppermute | solution.py:627
  56.6 11.6 %collective-permute-start.14 = (f32[6,8,128]{2,1,0:T(8,128)S(1)}, f32[6,8,128]{2,1,0:T(8,128)S(1)}, u32[]{:S(2)}, u32[]{:S(2)}) collective-permute-start(f32[6,8,128]{2,1,0:T(8,128)S(1)} %shard_map.128.after.refs_0_), channel_id=1, source_target_pairs={{0,32},{1,33},{2,34},{3,35},{4,36},{5,37},{6,38},{7,39},{8,10},{9,... | collective-permute-start | bytes 73736 | tf_op jit(solution)/shard_map/ppermute | solution.py:627
  56.6 11.6 %collective-permute-start.15 = (f32[6,8,128]{2,1,0:T(8,128)S(1)}, f32[6,8,128]{2,1,0:T(8,128)S(1)}, u32[]{:S(2)}, u32[]{:S(2)}) collective-permute-start(f32[6,8,128]{2,1,0:T(8,128)S(1)} %shard_map.128.after.refs_0_), channel_id=1, source_target_pairs={{0,2},{1,3},{2,0},{3,1},{4,6},{5,7},{6,4},{7,5},{8,40},{9,41},{10,... | collective-permute-start | bytes 73736 | tf_op jit(solution)/shard_map/ppermute | solution.py:627
  58.2 9.9 %collective-permute-start.16 = (f32[6,8,128]{2,1,0:T(8,128)S(1)}, f32[6,8,128]{2,1,0:T(8,128)S(1)}, u32[]{:S(2)}, u32[]{:S(2)}) collective-permute-start(f32[6,8,128]{2,1,0:T(8,128)S(1)} %shard_map.128.after.refs_0_), channel_id=1, source_target_pairs={{0,34},{1,35},{2,32},{3,33},{4,38},{5,39},{6,36},{7,37},{8,42},{9,... | collective-permute-start | bytes 73736 | tf_op jit(solution)/shard_map/ppermute | solution.py:627
  63.1 8.6 %collective-permute-start.12 = (f32[3,2,16,256]{3,2,1,0:T(8,128)S(1)}, f32[3,2,16,256]{3,2,1,0:T(8,128)S(1)}, u32[]{:S(2)}, u32[]{:S(2)}) collective-permute-start(f32[3,2,16,256]{3,2,1,0:T(8,128)S(1)} %get-tuple-element.111), channel_id=1, source_target_pairs={{0,1},{1,0},{2,3},{3,2},{4,5},{5,4},{6,7},{7,6},{8,9},{9,8},{10,11... | collective-permute-start | bytes 294920 | tf_op jit(solution)/shard_map/ppermute | solution.py:610
  63.4 8.4 %collective-permute-start.13 = (f32[3,2,16,256]{3,2,1,0:T(8,128)S(1)}, f32[3,2,16,256]{3,2,1,0:T(8,128)S(1)}, u32[]{:S(2)}, u32[]{:S(2)}) collective-permute-start(f32[3,2,16,256]{3,2,1,0:T(8,128)S(1)} %get-tuple-element.112), channel_id=1, source_target_pairs={{1,2},{2,1},{3,4},{4,3},{5,6},{6,5},{7,0},{0,7},{9,10},{10,9},{11,... | collective-permute-start | bytes 294920 | tf_op jit(solution)/shard_map/ppermute | solution.py:610
  68.2 5.0 %collective-permute-start.17 = (f32[6,32,128]{2,1,0:T(8,128)S(1)}, f32[6,32,128]{2,1,0:T(8,128)S(1)}, u32[]{:S(2)}, u32[]{:S(2)}) collective-permute-start(f32[6,32,128]{2,1,0:T(8,128)S(1)} %shard_map.131.after.refs_0_), channel_id=1, source_target_pairs={{0,4},{1,5},{2,6},{3,7},{4,0},{5,1},{6,2},{7,3},{8,24},{9,25},{10,... | collective-permute-start | bytes 294920 | tf_op jit(solution)/shard_map/ppermute | solution.py:627
  70.0 5.7 %collective-permute-start.18 = (f32[6,32,128]{2,1,0:T(8,128)S(1)}, f32[6,32,128]{2,1,0:T(8,128)S(1)}, u32[]{:S(2)}, u32[]{:S(2)}) collective-permute-start(f32[6,32,128]{2,1,0:T(8,128)S(1)} %shard_map.131.after.refs_0_), channel_id=1, source_target_pairs={{0,16},{1,17},{2,18},{3,19},{4,20},{5,21},{6,22},{7,23},{8,12},{9,... | collective-permute-start | bytes 294920 | tf_op jit(solution)/shard_map/ppermute | solution.py:627
  70.0 5.7 %collective-permute-start.19 = (f32[6,32,128]{2,1,0:T(8,128)S(1)}, f32[6,32,128]{2,1,0:T(8,128)S(1)}, u32[]{:S(2)}, u32[]{:S(2)}) collective-permute-start(f32[6,32,128]{2,1,0:T(8,128)S(1)} %shard_map.131.after.refs_0_), channel_id=1, source_target_pairs={{0,20},{1,21},{2,22},{3,23},{4,16},{5,17},{6,18},{7,19},{8,28},{9,... | collective-permute-start | bytes 294920 | tf_op jit(solution)/shard_map/ppermute | solution.py:627
